TPU v7x, 32 devices: a whole 2x2x4 slice. The times are simulated.
32 devices in a mesh: groups: 2 (over x), attn: 8 (over z, y), expert: 2 (over core).
Axes of the slice: x: 2, y: 2, z: 4, core: 2. Of those that a mesh axis runs over, the one named last changes fastest.
Arguments:
- queries: bfloat16 [512, 6144], P(('groups', 'attn'), 'expert'), parts along dimension 0, may hold values from -128 to 128
- new_kv: bfloat16 [512, 2048], P(('groups', 'attn'), 'expert'), parts along dimension 0, may hold values from -16 to 16
- kv_pool: bfloat16 [1152, 16, 2048], P(('groups', 'attn'), None, 'expert'), parts along dimension 0, may hold values from -16 to 16
- page_counts: int32 [16, 32], P(('groups', 'attn')), parts along dimension 0, may hold values from 1 to 8, 72 in all within a row
- tail_tokens: int32 [512], P(('groups', 'attn')), parts along dimension 0, may hold values from 1 to 16
- page_order: int32 [16, 72], P(('groups', 'attn')), parts along dimension 0, may hold values from 0 to 71, each once within a row
- residual: bfloat16 [512, 6144], P(('groups', 'attn'), 'expert'), parts along dimension 0, may hold values from -100 to 100
- norm_gain: float32 [6144], P('expert'), may hold values from 0.5 to 1.5
- routes: int32 [512, 2], P(('groups', 'attn')), parts along dimension 0, may hold values from 0 to 7, as said below
- route_gates: float32 [512, 2], P(('groups', 'attn')), parts along dimension 0, may hold values from 0.2 to 0.8
- w_gate: bfloat16 [2, 6144, 2048], P('expert', None, 'attn'), may hold values from -0.078125 to 0.078125
- w_up: bfloat16 [2, 6144, 2048], P('expert', None, 'attn'), may hold values from -0.078125 to 0.078125
- w_down: bfloat16 [2, 2048, 6144], P('expert', 'attn'), may hold values from -0.125 to 0.125
- mig_pages: int32 [16, 2], P(('groups', 'attn')), parts along dimension 0, may hold values from 0 to 71, as said below
- mig_dest: int32 [16, 2], P(('groups', 'attn')), parts along dimension 0, may hold values from -1 to 7, as said below
Outputs:
- layer_out: bfloat16 [512, 6144], P(('groups', 'attn'), 'expert'), parts along dimension 0
- arrived: bfloat16 [32, 16, 2048], P(('groups', 'attn'), None, 'expert'), parts along dimension 0
There are 2 independent parts, one for each index of `groups`. A program takes and returns all parts, laid end to end along the dimension named above; an argument that names none is the same for every part. Nothing has to cross between parts.
Inputs may be any that keep to these rules, and one draw needn't show every extreme that they name: `page_counts`: row a gives the pages of the 32 requests of attn index a and sums to 72. `page_order`: each row orders its 72 pages. `routes`: each row names two different experts; of the 32 rows of one attn index, each expert below 2 is named by at most 12 rows, and by exactly 12 rows at some attn index. `mig_pages`: the pages of one row differ. `mig_dest`: a row names each attn index at most once; an attn index is named by at most 2 entries in all, and one by exactly 2.
All inputs are finite; a program needn't handle non-finite values.
Results may differ from a plain program's by a relative error of at most 0.0045.
Values may be sent and summed in bfloat16 or wider, within the bound.
No kernel may reach another device: no remote copies, remote signals or barrier semaphores. Data moves between devices by JAX's collectives and lax.ppermute only.
A program may use at most 128 MiB of HBM per device.

v0:
```python
import jax
import jax.numpy as jnp
from jax import lax
from jax.sharding import PartitionSpec as P

D = 6144
HD = 128
PAGE = 16
MAXP = 8
CAP = 12


EPSILON = 1e-05


def attend(queries, new_kv, kv_pool, counts, tail_counts, order_row):
    row_count = queries.shape[0]
    heads_here = kv_pool.shape[2] // (2 * HD)
    group_size = queries.shape[1] // (heads_here * HD)
    offsets = jnp.cumsum(counts) - counts
    slot_ids = jnp.minimum(
        offsets[:, None] + jnp.arange(MAXP, dtype=jnp.int32)[None, :], kv_pool.shape[0] - 1
    )
    page_ids = jnp.take(order_row, slot_ids, axis=0)
    cached = jnp.take(kv_pool, page_ids.reshape(-1), axis=0).reshape(
        row_count, MAXP * PAGE, heads_here, 2, HD
    )
    lengths = (counts - 1) * PAGE + tail_counts
    query_heads = queries.reshape(row_count, heads_here, group_size, HD)
    newest = new_kv.reshape(row_count, heads_here, 2, HD)
    score_scale = HD ** (-0.5)
    scores = (
        jnp.einsum(
            "rkgd,rtkd->rkgt", query_heads, cached[:, :, :, 0], preferred_element_type=jnp.float32
        )
        * score_scale
    )
    own_score = (
        jnp.einsum(
            "rkgd,rkd->rkg", query_heads, newest[:, :, 0], preferred_element_type=jnp.float32
        )
        * score_scale
    )
    in_range = (jnp.arange(MAXP * PAGE, dtype=jnp.int32)[None, :] < lengths[:, None])[
        :, None, None, :
    ]
    row_top = jnp.maximum(jnp.max(jnp.where(in_range, scores, -jnp.inf), axis=-1), own_score)
    weights = jnp.where(in_range, jnp.exp(scores - row_top[..., None]), 0.0)
    own_weight = jnp.exp(own_score - row_top)
    denominator = jnp.sum(weights, axis=-1) + own_weight
    probabilities = (weights / denominator[..., None]).astype(jnp.bfloat16)
    own_prob = lax.optimization_barrier((own_weight / denominator).astype(jnp.bfloat16)).astype(
        jnp.float32
    )
    mixed_heads = jnp.einsum(
        "rkgt,rtkd->rkgd", probabilities, cached[:, :, :, 1], preferred_element_type=jnp.float32
    )
    mixed_heads = mixed_heads + own_prob[..., None] * newest[:, :, 1][:, :, None, :].astype(
        jnp.float32
    )
    return mixed_heads.reshape(row_count, heads_here * group_size * HD)


def per_device(
    queries,
    new_kv,
    kv_pool,
    page_counts,
    tail_tokens,
    page_order,
    residual,
    norm_gain,
    routes,
    route_gates,
    w_gate,
    w_up,
    w_down,
    mig_pages,
    mig_dest,
):
    attended = attend(queries, new_kv, kv_pool, page_counts[0], tail_tokens, page_order[0])
    hidden = residual.astype(jnp.float32) + attended
    squares = lax.psum(jnp.sum(hidden * hidden, axis=1), "expert")
    normed = (hidden * lax.rsqrt(squares[:, None] / D + EPSILON) * norm_gain).astype(jnp.bfloat16)
    hosted = lax.axis_size("expert")
    own_expert = lax.axis_index("expert")
    half_width = normed.shape[1]
    slot_iota = jnp.arange(CAP, dtype=jnp.int32)
    dispatch_maps = []
    combine_maps = []
    for expert in range(hosted):
        chosen = routes == expert
        member = jnp.any(chosen, axis=1)
        gate_share = jnp.sum(jnp.where(chosen, route_gates, 0.0), axis=1)
        slot_rank = jnp.cumsum(member.astype(jnp.int32)) - 1
        onehot = (slot_rank[None, :] == slot_iota[:, None]) & member[None, :]
        dispatch_maps.append(onehot.astype(jnp.bfloat16))
        combine_maps.append(jnp.where(onehot, gate_share[None, :], 0.0))
    dispatch_all = jnp.stack(dispatch_maps)
    combine_all = jnp.stack(combine_maps)
    outgoing = jnp.einsum(
        "ecr,rd->ecd", dispatch_all, normed, preferred_element_type=jnp.float32
    ).astype(jnp.bfloat16)
    gate_split = w_gate[0].reshape(hosted, half_width, -1)
    up_split = w_up[0].reshape(hosted, half_width, -1)
    everyone = lax.all_gather(outgoing[None], ("attn", "expert"), axis=0, tiled=True)
    by_source = everyone.reshape(-1, hosted, hosted, CAP, half_width)
    own_rows = lax.dynamic_index_in_dim(by_source, own_expert, 2, keepdims=False)
    gate_value = jnp.einsum(
        "kcsd,cdf->ksf", own_rows, gate_split, preferred_element_type=jnp.float32
    )
    up_value = jnp.einsum("kcsd,cdf->ksf", own_rows, up_split, preferred_element_type=jnp.float32)
    active_part = (jax.nn.silu(gate_value) * up_value).astype(jnp.bfloat16)
    active = active_part.reshape(-1, active_part.shape[2])
    down_matrix = w_down[0]
    summed = lax.psum_scatter(
        jnp.dot(active, down_matrix, preferred_element_type=jnp.float32).astype(jnp.bfloat16),
        "attn",
        scatter_dimension=0,
        tiled=True,
    )
    expert_out = summed.reshape(CAP, hosted, half_width)
    returned = lax.all_to_all(expert_out, "expert", split_axis=1, concat_axis=1, tiled=True)
    moe_term = jnp.einsum(
        "ecr,ced->rd", combine_all, returned.astype(jnp.float32), precision=lax.Precision.HIGHEST
    )
    layer_out = (hidden + moe_term).astype(jnp.bfloat16)
    own_index = lax.axis_index("attn")
    entries = mig_pages.shape[1]
    targets = mig_dest[0]
    payload = jnp.take(kv_pool, mig_pages[0], axis=0)
    blocks = lax.all_gather(payload[None], "attn", axis=0, tiled=True)
    aimed_at = lax.all_gather(targets[None], "attn", axis=0, tiled=True)
    chosen_here = aimed_at == own_index
    picked = jnp.einsum(
        "ki,kipc->kpc", chosen_here.astype(jnp.bfloat16), blocks, preferred_element_type=jnp.float32
    ).astype(jnp.bfloat16)
    flags_now = jnp.any(chosen_here, axis=1).astype(jnp.int32)
    arrival_rank = jnp.cumsum(flags_now) - 1
    compact_map = (
        (arrival_rank[None, :] == jnp.arange(entries, dtype=jnp.int32)[:, None])
        & (flags_now[None, :] > 0)
    ).astype(jnp.bfloat16)
    arrived = jnp.einsum(
        "jn,npc->jpc", compact_map, picked, preferred_element_type=jnp.float32
    ).astype(jnp.bfloat16)
    return (layer_out, arrived)


def solution(mesh):
    return jax.shard_map(
        per_device,
        mesh=mesh,
        in_specs=(
            P(("groups", "attn"), "expert"),
            P(("groups", "attn"), "expert"),
            P(("groups", "attn"), None, "expert"),
            P(("groups", "attn"), None),
            P(("groups", "attn")),
            P(("groups", "attn"), None),
            P(("groups", "attn"), "expert"),
            P("expert"),
            P(("groups", "attn"), None),
            P(("groups", "attn"), None),
            P("expert", None, "attn"),
            P("expert", None, "attn"),
            P("expert", "attn", None),
            P(("groups", "attn"), None),
            P(("groups", "attn"), None),
        ),
        out_specs=(P(("groups", "attn"), "expert"), P(("groups", "attn"), None, "expert")),
        check_vma=False,
    )
```

profile of v0, /device:TPU:0, one launch (start us, length us, event | category | flops | bytes accessed | tf_op | source)
XLA Modules:
  0.0 206.3 jit_solution(298156829678333514)
XLA Ops:
  7.2 0.9 copy.65
  8.3 0.7 fusion.59
  9.4 1.9 gather_fusion
  11.4 10.3 %gather_fusion.1 = bf16[256,16,1024]{2,1,0:T(8,128)(2,1)} fusion(bf16[72,16,1024]{2,1,0:T(8,128)(2,1)} %param.17, s32[1024]{0:T(1024)S(1)} %pad_clamp_fusion.1), kind=kCustom, calls=%fused_computation.1 | custom fusion | bytes 16778240 | tf_op jit(solution)/shard_map/jit(_take)/gather | solution.py:25
  21.7 14.4 %gather.21 = bf16[32,128,4,2,128]{4,3,2,1,0:T(2,128)(2,1)} reshape(bf16[256,16,1024]{2,1,0:T(8,128)(2,1)} %gather_fusion.1) | data formatting | bytes 16777216 | tf_op jit(solution)/shard_map/jit(_take)/gather | solution.py:25
  36.3 1.2 reshape.606
  37.7 5.2 %copy_select_fusion = bf16[32,128,4,2,128]{4,1,2,0,3:T(8,128)(2,1)S(1)} fusion(bf16[32,128,4,2,128]{4,3,2,1,0:T(2,128)(2,1)} %gather.21, pred[32,128]{1,0:T(8,128)(4,1)S(1)} %copy.67), kind=kLoop, calls=%fused_computation.3 | loop fusion | flops 4194304 | bytes 16781312 | tf_op jit(solution)/shard_map/jit(_take)/select_n | solution.py:25
  43.2 2.4 %select_reduce_fusion = (f32[32,4,6]{2,1,0:T(4,128)S(1)}, f32[32,4,128,6]{2,3,1,0:T(8,128)S(1)}) fusion(pred[32,128]{1,0:T(8,128)(4,1)S(1)} %iota_compare_fusion, bf16[32,4,6,128]{3,2,1,0:T(8,128)(2,1)S(1)} %reshape.606, bf16[32,128,4,2,128]{4,1,2,0,3:T(8,128)(2,1)S(1)} %copy_select_fusion), kind=kOutput, calls=%fused_computation.32 | convolution fusion | flops 25459968 | bytes 4856832 | tf_op jit(solution)/shard_map/rkgd,rtkd->rkgt/dot_general | solution.py:33
  46.2 2.1 fusion.12
  48.3 1.1 reshape.608
  49.4 1.1 multiply_reduce_fusion
  50.5 2.6 %psum.7 = f32[32]{0:T(128)S(1)} all-reduce(f32[32]{0:T(128)S(1)} %multiply_reduce_fusion), channel_id=1, replica_groups=mesh['groups'=2,'attn'=8,'expert'=2] {'expert'}, use_global_device_ids=true, to_apply=%region_10.11 | all-reduce | flops 32 | bytes 256 | tf_op jit(solution)/shard_map/psum | solution.py:83
  53.1 0.6 add_rsqrt_fusion
  55.2 0.7 copy.72
  55.9 0.6 reduce-window.34
  56.6 1.4 add_reduce_fusion
  58.0 1.1 convert_bitcast_fusion.2
  59.1 0.7 copy.71
  59.8 0.6 reduce-window.33
  60.5 0.9 add_reduce_fusion.1
  61.9 0.7 fusion.47
  62.6 1.9 convolution_convert_fusion.1
  64.5 22.2 %all-gather.1 = s32[8,1,2]{2,1,0:T(1,128)S(1)} all-gather(s32[1,1,2]{2,1,0:T(1,128)} %bitcast.137), channel_id=1, replica_groups=mesh['groups'=2,'attn'=8,'expert'=2] {'attn'}, dimensions={0}, use_global_device_ids=true | all-gather | bytes 72 | tf_op jit(solution)/shard_map/all_gather | solution.py:133
  87.4 0.7 reduce-window.35
  88.4 0.7 fusion.57
  89.1 2.8 %gather_fusion.2 = bf16[2,16,1024]{2,1,0:T(8,128)(2,1)} fusion(bf16[72,16,1024]{2,1,0:T(8,128)(2,1)} %param.17, s32[1024]{0:T(1024)S(1)} %pad_clamp_fusion), kind=kCustom, calls=%fused_computation.2 | custom fusion | bytes 131080 | tf_op jit(solution)/shard_map/jit(_take)/gather | solution.py:131
  91.9 0.7 compare_and_fusion.1
  92.6 0.7 add_bitcast_fusion
  93.3 0.9 bitcast_select_fusion
  94.2 32.7 %all_gather.11 = bf16[8,2,16,1024]{3,2,1,0:T(8,128)(2,1)S(1)} all-gather(bf16[1,2,16,1024]{3,2,1,0:T(8,128)(2,1)S(1)} %bitcast_select_fusion), channel_id=1, replica_groups=mesh['groups'=2,'attn'=8,'expert'=2] {'attn'}, dimensions={0}, use_global_device_ids=true | all-gather | bytes 589824 | tf_op jit(solution)/shard_map/all_gather | solution.py:132
  126.8 0.7 fusion.27
  127.9 0.6 copy.76
  130.3 2.1 %fusion.14 = f32[8,12,256]{2,1,0:T(8,128)S(1)} fusion(bf16[2,3072,256,1]{2,1,0,3:T(8,128)(2,1)S(1)} %bitcast.123, bf16[8,2,2,12,3072]{4,3,2,1,0:T(8,128)(2,1)} %bitcast.125, s32[]{:T(128)S(6)} %select_n.153), kind=kOutput, calls=%fused_computation.22 | convolution fusion | flops 301989888 | bytes 4816900 | tf_op jit(solution)/shard_map/kcsd,cdf->ksf/dot_general | solution.py:109
  132.7 3.1 %fusion.23 = bf16[8,12,256]{2,1,0:T(8,128)(2,1)} fusion(bf16[2,3072,256,1]{2,1,0,3:T(8,128)(2,1)} %bitcast.127, bf16[8,2,2,12,3072]{4,3,2,1,0:T(8,128)(2,1)S(1)} %bitcast.126, s32[]{:T(128)S(6)} %select_n.153, f32[8,12,256]{2,1,0:T(8,128)S(1)} %fusion.14), kind=kOutput, calls=%fused_computation.25 | convolution fusion | flops 302137344 | bytes 4898820 | tf_op jit(solution)/shard_map/kcsd,cdf->ksf/dot_general | solution.py:112
  135.8 1.5 reshape.610
  137.3 3.6 %convolution_convert_fusion = bf16[96,6144]{1,0:T(8,128)(2,1)} fusion(bf16[96,256]{1,0:T(8,128)(2,1)} %reshape.610, bf16[1,256,6144]{2,1,0:T(8,128)(2,1)} %param.27), kind=kOutput, calls=%fused_computation.4 | convolution fusion | flops 302579712 | bytes 4374528 | tf_op jit(solution)/shard_map/dot_general | solution.py:117
  140.8 30.2 %fusion = bf16[16,6144]{1,0:T(8,128)(2,1)} fusion(bf16[96,6144]{1,0:T(8,128)(2,1)} %convolution_convert_fusion), kind=kCustom, calls=%all-reduce-scatter | all-reduce-scatter fusion | flops 786433 | bytes 1376768
  171.1 1.0 slice.26
  172.0 3.2 %collective-permute-start = (bf16[16,6144]{1,0:T(8,128)(2,1)}, bf16[16,6144]{1,0:T(8,128)(2,1)}, u32[]{:S(2)}, u32[]{:S(2)}) collective-permute-start(bf16[16,6144]{1,0:T(8,128)(2,1)} %fusion), channel_id=1, source_target_pairs={{0,2},{2,4},{4,6},{6,8},{8,10},{10,12},{12,14},{1,3},{3,5},{5,7},{... | collective-permute-start | bytes 589832
  175.2 2.0 collective-permute-start.1
  177.2 0.7 broadcast_select_fusion
  177.9 1.8 collective-permute-done.1
  179.7 9.6 %concatenate = bf16[44,6144]{1,0:T(8,128)(2,1)} concatenate(bf16[12,6144]{1,0:T(8,128)(2,1)} %collective-permute-done.1, bf16[16,6144]{1,0:T(8,128)(2,1)} %collective-permute-done, bf16[16,6144]{1,0:T(8,128)(2,1)} %fusion), dimensions={0} | concatenate | bytes 1081344
  189.3 1.7 constant_dynamic-slice_fusion
  191.0 1.7 reshape.611
  192.6 0.9 copy.74
  193.6 3.9 %all_to_all.5 = bf16[12,2,3072]{2,0,1:T(8,128)(2,1)S(1)} all-to-all(bf16[12,2,3072]{2,0,1:T(8,128)(2,1)S(1)} %copy.74), channel_id=1, replica_groups=mesh['groups'=2,'attn'=8,'expert'=2] {'expert'}, dimensions={1} | all-to-all | bytes 294912 | tf_op jit(solution)/shard_map/all_to_all | solution.py:123
  197.5 2.0 fusion.4
  (61 shorter events, 6.7 us)
Async XLA Ops:
  7.2 123.2 %copy-start = (bf16[1,6144,256]{2,1,0:T(8,128)(2,1)S(1)}, bf16[1,6144,256]{2,1,0:T(8,128)(2,1)}, u32[]{:S(2)}) copy-start(bf16[1,6144,256]{2,1,0:T(8,128)(2,1)} %param.25) | copy-start | bytes 9437188
  7.2 2.2 %copy-start.1 = (s32[1,72]{1,0:T(1,128)S(1)}, s32[1,72]{1,0:T(1,128)}, u32[]{:S(2)}) copy-start(s32[1,72]{1,0:T(1,128)} %param.20) | copy-start | bytes 868
  7.2 123.1 %all-gather.4.cloned.1.call-start = ((), (), s32[]{:S(2)}) async-start(), calls=%async_computation.1 | async-start | bytes 3342336 | tf_op jit(solution)/shard_map/all_gather | solution.py:106
  21.7 15.8 %copy-start.3 = (bf16[32,1024]{1,0:T(8,128)(2,1)S(1)}, bf16[32,1024]{1,0:T(8,128)(2,1)}, u32[]{:S(2)}) copy-start(bf16[32,1024]{1,0:T(8,128)(2,1)} %param.16) | copy-start | bytes 196612
  46.2 7.5 %copy-start.6 = (s32[32,2]{0,1:T(2,128)S(1)}, s32[32,2]{0,1:T(2,128)}, u32[]{:S(2)}) copy-start(s32[32,2]{0,1:T(2,128)} %param.23) | copy-start | bytes 772
  54.2 0.5 copy-start.5
  60.5 69.2 %copy-start.7 = (s32[32,2]{0,1:T(2,128)S(1)}, s32[32,2]{0,1:T(2,128)}, u32[]{:S(2)}) copy-start(s32[32,2]{0,1:T(2,128)} %param.23) | copy-start | bytes 772
  60.5 69.2 %copy-start.8 = (f32[32,2]{0,1:T(2,128)S(1)}, f32[32,2]{0,1:T(2,128)}, u32[]{:S(2)}) copy-start(f32[32,2]{0,1:T(2,128)} %param.24) | copy-start | bytes 772
  61.3 0.5 copy-start.4
  91.9 35.6 %copy-start.9 = (pred[8]{0:T(512)(128)(4,1)S(1)}, pred[8]{0:T(512)(128)(4,1)}, u32[]{:S(2)}) copy-start(pred[8]{0:T(512)(128)(4,1)} %get-tuple-element.25) | copy-start | bytes 28
  91.9 36.7 %copy-start.10 = (u32[32]{0:T(128)S(1)}, u32[32]{0:T(128)}, u32[]{:S(2)}) copy-start(u32[32]{0:T(128)} %constant.103) | copy-start | bytes 388
  130.3 2.4 %copy-start.2 = (bf16[32,12,3072]{2,1,0:T(8,128)(2,1)S(1)}, bf16[32,12,3072]{2,1,0:T(8,128)(2,1)}, u32[]{:S(2)}) copy-start(bf16[32,12,3072]{2,1,0:T(8,128)(2,1)} %all-gather.4.cloned.1.call-done) | copy-start | bytes 7077892
  172.0 7.7 %collective-permute-start = (bf16[16,6144]{1,0:T(8,128)(2,1)}, bf16[16,6144]{1,0:T(8,128)(2,1)}, u32[]{:S(2)}, u32[]{:S(2)}) collective-permute-start(bf16[16,6144]{1,0:T(8,128)(2,1)} %fusion), channel_id=1, source_target_pairs={{0,2},{2,4},{4,6},{6,8},{8,10},{10,12},{12,14},{1,3},{3,5},{5,7},{... | collective-permute-start | bytes 589832
  175.2 4.5 %collective-permute-start.1 = (bf16[12,6144]{1,0:T(8,128)(2,1)S(1)}, bf16[12,6144]{1,0:T(8,128)(2,1)}, u32[]{:S(2)}, u32[]{:S(2)}) collective-permute-start(bf16[12,6144]{1,0:T(8,128)(2,1)S(1)} %slice.26), channel_id=1, source_target_pairs={{0,4},{2,6},{4,8},{6,10},{8,12},{10,14},{1,5},{3,7},{5,9},{7,11},{... | collective-permute-start | bytes 442376
Sparse Core Ops, SparseCore 0:
  64.6 52.9 all-gather.3
where the time goes:
time: 208 us; the launch traced here: 206 us
  blocking collectives  91.6 us (44%)
  local copies, waits for them, and re-layouts  53.7 us (26%)
  other arithmetic  20.7 us (10%)
  matrix products  18.5 us (9%)
  between operations  14.8 us (7%)
  starting transfers between devices  5.2 us (2%)
    all_gather x1, blocking collectives, per_device(): blocks = lax.all_gather(payload[None], 'attn', axis=0, tiled=True)  32.7 us
    unnamed x1, blocking collectives  30.2 us
    gather x2, local copies, waits for them, and re-layouts, attend(): jnp.take(kv_pool, page_ids.reshape(-1), axis=0)  24.7 us
    all_gather x1, blocking collectives, per_device(): aimed_at = lax.all_gather(targets[None], 'attn', axis=0, tiled=True)  22.2 us
    unnamed x27, local copies, waits for them, and re-layouts  14.8 us
    select_n x2, other arithmetic, attend(): jnp.take(kv_pool, page_ids.reshape(-1), axis=0)  5.26 us
    unnamed x2, starting transfers between devices  5.16 us
  transfers between devices with their start and end apart: 3, of which 1 were waited for; matrix products, arithmetic and copies ran while one was open for 5% of the time, Pallas kernels for 0%

commit v1 on v0

v1 whole, which is shorter than its diff:
```python
import functools

import jax
import jax.numpy as jnp
from jax import lax
from jax.experimental import pallas as pl
from jax.experimental.pallas import tpu as pltpu
from jax.sharding import PartitionSpec as P

D = 6144
HD = 128
PAGE = 16
CAP = 12
EPSILON = 1e-05
HALF = D // 2
QUARTER = D // 4
LO = 8
SLOT_COLS = HALF + QUARTER
LANES = 128
SCORE_SCALE = HD ** (-0.5)
NEG = -1e30
F32 = jnp.float32
BF16 = jnp.bfloat16
VMEM = pl.BlockSpec(memory_space=pltpu.VMEM)
SMEM = pl.BlockSpec(memory_space=pltpu.SMEM)
ANY = pl.BlockSpec(memory_space=pl.ANY)


def iota(shape, dim):
    return lax.broadcasted_iota(jnp.int32, shape, dim)


def eye(size):
    return iota((size, size), 0) == iota((size, size), 1)


def to_column(row, size):
    return jnp.sum(jnp.where(eye(size), row, 0.0), axis=1, keepdims=True)


def to_row(column, size):
    return jnp.sum(jnp.where(eye(size), column, 0.0), axis=0, keepdims=True)


def dot(a, b):
    return lax.dot_general(a, b, (((1,), (0,)), ((), ())), preferred_element_type=F32)


def dot_t(a, b):
    return lax.dot_general(a, b, (((1,), (1,)), ((), ())), preferred_element_type=F32)


def members(routes, expert):
    chosen = (routes[:, 0:1] == expert) | (routes[:, 1:2] == expert)
    return jnp.where(chosen, 1.0, 0.0)


def mix_slots(shape, dim, part):
    index = iota(shape, dim)
    here = (index >= 4 * part) & (index < 4 * part + 4)
    return jnp.where(here, index - 4 * part + LO, -1).astype(F32)


def split_three(value):
    high = value.astype(BF16)
    rest = value - high.astype(F32)
    middle = rest.astype(BF16)
    low = (rest - middle.astype(F32)).astype(BF16)
    return high.astype(F32), middle.astype(F32), low.astype(F32)


def attend_kernel(
    hosted, queries, new_kv, pool, counts, tails, order, residual, gain, routes, mig_pages, mig_dest, hidden, slots, moved
):
    rows = queries.shape[0]
    tokens = pool.shape[0]
    pages = tokens // PAGE
    heads_here = pool.shape[1] // (2 * HD)
    group = queries.shape[1] // (heads_here * HD)
    width = queries.shape[1]

    counts_row = counts[...].astype(F32)
    row_a, row_b = iota((rows, rows), 0), iota((rows, rows), 1)
    first = jnp.sum(jnp.where(row_b < row_a, counts_row, 0.0), axis=1, keepdims=True)
    count = to_column(counts_row, rows)
    tail = to_column(tails[...].astype(F32), rows)
    place = iota((rows, pages), 1).astype(F32)
    inside = (place >= first) & (place < first + count)
    held = jnp.where(inside, jnp.where(place == first + count - 1.0, tail, float(PAGE)), 0.0)
    page_at = to_column(order[...].astype(F32), pages)
    page_of = (iota((pages, tokens), 1) // PAGE).astype(F32)
    placed = jnp.where(page_at == page_of, 1.0, 0.0).astype(BF16)
    limit = dot(held.astype(BF16), placed)
    visible = (iota((rows, tokens), 1) % PAGE).astype(F32) < limit
    penalty = jnp.where(visible, 0.0, NEG)[None]
    own_penalty = jnp.where(eye(rows), 0.0, NEG)[None]

    squares = jnp.zeros((rows, HD), F32)
    for head in range(heads_here):
        base = head * group * HD
        query = jnp.concatenate(
            [queries[:, base + g * HD : base + (g + 1) * HD] for g in range(group)], axis=0
        )
        key_at, value_at = 2 * head * HD, (2 * head + 1) * HD
        scores = dot_t(query, pool[:, key_at : key_at + HD]) * SCORE_SCALE
        own = dot_t(query, new_kv[:, key_at : key_at + HD]) * SCORE_SCALE
        scores = (scores.reshape(group, rows, tokens) + penalty).reshape(group * rows, tokens)
        own = (own.reshape(group, rows, rows) + own_penalty).reshape(group * rows, rows)
        top = jnp.maximum(
            jnp.max(scores, axis=1, keepdims=True), jnp.max(own, axis=1, keepdims=True)
        )
        weights = jnp.exp(scores - top)
        own_weights = jnp.exp(own - top)
        total = jnp.sum(weights, axis=1, keepdims=True) + jnp.sum(own_weights, axis=1, keepdims=True)
        inverse = 1.0 / total
        mixed = dot((weights * inverse).astype(BF16), pool[:, value_at : value_at + HD])
        mixed = mixed + dot((own_weights * inverse).astype(BF16), new_kv[:, value_at : value_at + HD])
        for g in range(group):
            columns = slice(base + g * HD, base + (g + 1) * HD)
            part = residual[:, columns].astype(F32) + mixed[g * rows : (g + 1) * rows]
            hidden[:, columns] = part
            squares = squares + part * part
    square_row = to_row(jnp.sum(squares, axis=1, keepdims=True), rows)

    scaled = (hidden[...] * gain[...]).astype(BF16)
    lows, mixes = [], []
    for expert in range(hosted):
        member = members(routes[...], expert)
        member_row = to_row(member, rows)
        rank = jnp.sum(jnp.where(row_a <= row_b, member, 0.0), axis=0, keepdims=True) - 1.0
        rank = jnp.where(member_row > 0.0, rank, -2.0)
        lows.append(rank == iota((LO, rows), 0).astype(F32))
        mixes.append([rank == mix_slots((LO, rows), 0, part) for part in range(2)])
    picked = []
    for part in range(2):
        maps = [jnp.where(m, 1.0, 0.0) for m in lows] + [jnp.where(m[part], 1.0, 0.0) for m in mixes]
        stacked = jnp.concatenate(maps, axis=0).astype(BF16)
        picked.append(dot(stacked, scaled[:, part * QUARTER : (part + 1) * QUARTER]))
    lane = iota((LO, LANES), 1)
    for expert in range(hosted):
        low_at, mix_at = expert * LO, (hosted + expert) * LO
        low_sum = jnp.sum(jnp.where(lows[expert], square_row, 0.0), axis=1, keepdims=True)
        mix_map = mixes[expert][0] | mixes[expert][1]
        mix_sum = jnp.sum(jnp.where(mix_map, square_row, 0.0), axis=1, keepdims=True)
        extra = jnp.zeros((LO, LANES), F32)
        for at, piece in enumerate(split_three(low_sum) + split_three(mix_sum)):
            extra = jnp.where(lane == at, piece, extra)
        for part in range(2):
            columns = slice(part * QUARTER, (part + 1) * QUARTER)
            slots[expert, :, columns] = picked[part][low_at : low_at + LO].astype(BF16)
        mixed_rows = picked[0][mix_at : mix_at + LO] + picked[1][mix_at : mix_at + LO]
        slots[expert, :, HALF:SLOT_COLS] = mixed_rows.astype(BF16)
        slots[expert, :, SLOT_COLS:] = extra.astype(BF16)

    entries = mig_pages.shape[1]
    page_width = pool.shape[1]
    lane = iota((PAGE, LANES), 1)
    notes = jnp.where(lane == entries, lax.axis_index("attn").astype(F32), 0.0)
    for entry in range(entries):
        start = pl.multiple_of(mig_pages[0, entry] * PAGE, PAGE)
        moved[:, entry * page_width : (entry + 1) * page_width] = pool[pl.ds(start, PAGE), :]
        notes = jnp.where(lane == entry, mig_dest[0, entry].astype(F32), notes)
    moved[:, entries * page_width :] = notes.astype(BF16)


def pack_kernel(mine, theirs, moved, message):
    lane = iota((LO, LANES), 1)
    extra = mine[:, SLOT_COLS:].astype(F32) + theirs[:, SLOT_COLS:].astype(F32)
    low_scale = lax.rsqrt(jnp.sum(jnp.where(lane < 3, extra, 0.0), axis=1, keepdims=True) / D + EPSILON)
    mix_sum = jnp.sum(jnp.where((lane >= 3) & (lane < 6), extra, 0.0), axis=1, keepdims=True)
    mix_scale = lax.rsqrt(mix_sum / D + EPSILON)
    first_half = lax.axis_index("expert") == 0
    for columns, scale in ((slice(0, HALF), low_scale), (slice(HALF, SLOT_COLS), mix_scale)):
        a = mine[:, columns].astype(F32) * scale
        b = theirs[:, columns].astype(F32) * scale
        both = jnp.concatenate([jnp.where(first_half, a, b), jnp.where(first_half, b, a)], axis=0)
        message[:, columns] = both.astype(BF16)
    message[:, SLOT_COLS:] = moved[...]


def ffn_kernel(n, cut, *refs):
    blocks, (gate_hbm, up_hbm, down_hbm) = refs[: n + 1], refs[n + 1 : n + 4]
    outs = refs[n + 4 : 2 * n + 4]
    low_rows, mix_rows, gate, up, down, gate_sum, up_sum, sems = refs[2 * n + 4 :]
    copies = []
    for q in range(4):
        part = pl.ds(q * QUARTER, QUARTER)
        copies.append(pltpu.make_async_copy(gate_hbm.at[part, :], gate.at[part, :], sems.at[0, q]))
        copies.append(pltpu.make_async_copy(up_hbm.at[part, :], up.at[part, :], sems.at[1, q]))
    for q in range(4):
        part = pl.ds(q * QUARTER, QUARTER)
        copies.append(pltpu.make_async_copy(down_hbm.at[:, part], down.at[:, part], sems.at[2, q]))
    for copy in copies:
        copy.start()
    for j in range(n - 1):
        low_rows[16 * j : 16 * j + 16, :] = blocks[j][:, :HALF]
        mix_rows[16 * j : 16 * j + 16, :] = blocks[j][:, HALF:SLOT_COLS]
    j = n - 1
    low_rows[16 * j : 16 * j + 16, :] = blocks[j][:, :HALF]
    mix_rows[16 * j : 16 * j + 16, : cut - HALF] = blocks[j][:, HALF:cut]
    mix_rows[16 * j : 16 * j + 16, cut - HALF :] = blocks[n][:, : SLOT_COLS - cut]

    size = min(n, 8)
    span = 16 * size
    row = iota((span, 1), 0) % 16
    for q in range(4):
        copies[2 * q].wait()
        copies[2 * q + 1].wait()
        low_here, mix_here = (row // 8) == q // 2, (row // 4) == q
        part = slice(q * QUARTER, (q + 1) * QUARTER)
        within = slice((q % 2) * QUARTER, (q % 2 + 1) * QUARTER)
        for at in range(0, 16 * n, span):
            left = jnp.concatenate([low_rows[at : at + span, within], mix_rows[at : at + span, :]], axis=0)
            for weight, total in ((gate, gate_sum), (up, up_sum)):
                product = dot(left, weight[part, :])
                low = jnp.where(low_here, product[:span], 0.0)
                mix = jnp.where(mix_here, product[span:], 0.0)
                if q == 0:
                    total[0, at : at + span, :] = low
                    total[1, at : at + span, :] = mix
                else:
                    total[0, at : at + span, :] += low
                    total[1, at : at + span, :] += mix

    for copy in copies[8:]:
        copy.wait()
    lower = iota((8 * size, 1), 0) % 8 < 4
    width = gate.shape[1]

    def fold(total, at):
        low, mix = [
            jnp.sum(total[k, at : at + span, :].reshape(size, 2, 8, width), axis=1).reshape(8 * size, width)
            for k in range(2)
        ]
        other = jnp.where(lower, pltpu.roll(mix, 8 * size - 4, 0), pltpu.roll(mix, 4, 0))
        return low, mix + other

    first_rows = iota((8, 1), 0) < 4
    for at in range(0, 16 * n, span):
        pieces = [jax.nn.silu(g) * u for g, u in zip(fold(gate_sum, at), fold(up_sum, at))]
        active = jnp.concatenate([p.reshape(size, 8, width) for p in pieces], axis=1)
        active = active.reshape(span, width).astype(BF16)
        quarters = [dot(active, down[:, q * QUARTER : (q + 1) * QUARTER]) for q in range(4)]
        for j in range(size):
            out = outs[at // 16 + j]
            low_at, mix_at = slice(16 * j, 16 * j + 8), slice(16 * j + 8, 16 * j + 16)
            for part in range(2):
                both = jnp.concatenate([quarters[part][low_at], quarters[2 + part][low_at]], axis=0)
                out[:, part * QUARTER : (part + 1) * QUARTER] = both.astype(BF16)
            both = jnp.concatenate(
                [jnp.where(first_rows, quarters[k][mix_at], quarters[k + 1][mix_at]) for k in (0, 2)], axis=0
            )
            out[:, HALF:] = both.astype(BF16)


def arrive_kernel(n, cut, page_width, *refs):
    blocks, arrived, board, board_smem, sem = refs[: n + 1], refs[n + 1], refs[n + 2], refs[n + 3], refs[n + 4]
    entries = arrived.shape[0]
    notes_at = SLOT_COLS + entries * page_width
    heads = [block[:, notes_at:].astype(F32)[0:1] for block in blocks[: n - 1]]
    heads.append(blocks[n][:, notes_at - cut :].astype(F32)[0:1])
    notes = jnp.concatenate(heads, axis=0)
    lane = iota((n, LANES), 1)
    match = (notes == lax.axis_index("attn").astype(F32)) & (lane < entries)
    named = jnp.max(jnp.where(match, 1.0, 0.0), axis=1, keepdims=True)
    source = jnp.sum(jnp.where(lane == entries, notes, 0.0), axis=1, keepdims=True)
    earlier = to_row(source, n) < source
    rank = jnp.sum(jnp.where(earlier, to_row(named, n), 0.0), axis=1, keepdims=True)
    board[...] = jnp.where(match, rank, -1.0).astype(jnp.int32)
    copy = pltpu.make_async_copy(board, board_smem, sem)
    copy.start()
    arrived[...] = jnp.zeros_like(arrived)
    copy.wait()
    for j in range(n):
        block, shift = (blocks[j], 0) if j < n - 1 else (blocks[n], cut)
        for entry in range(entries):
            slot = board_smem[j, entry]
            at = SLOT_COLS + entry * page_width - shift

            @pl.when(slot >= 0)
            def _():
                arrived[slot] = block[:, at : at + page_width]


def finish_kernel(own, from_left, from_right, mine, other):
    total = own[...].astype(F32) + from_left[...].astype(F32) + from_right[...].astype(F32)
    first_half = lax.axis_index("expert") == 0
    top, bottom = total[:LO], total[LO:]
    mine[...] = jnp.where(first_half, top, bottom).astype(BF16)
    other[...] = jnp.where(first_half, bottom, top).astype(BF16)


def combine_kernel(hosted, hidden, mine, theirs, routes, gates, layer_out):
    rows = hidden.shape[0]
    first_half = lax.axis_index("expert") == 0
    a, b = mine[...].astype(F32), theirs[...].astype(F32)
    by_expert = [jnp.where(first_half, a, b).astype(BF16), jnp.where(first_half, b, a).astype(BF16)]
    row_a, row_b = iota((rows, rows), 0), iota((rows, rows), 1)
    terms = [[], []]
    for expert in range(hosted):
        member = members(routes[...], expert)
        share = jnp.sum(jnp.where(routes[...] == expert, gates[...], 0.0), axis=1, keepdims=True)
        rank = jnp.sum(jnp.where(row_b <= row_a, to_row(member, rows), 0.0), axis=1, keepdims=True) - 1.0
        rank = jnp.where(member > 0.0, rank, -2.0)
        low = jnp.where(rank == iota((rows, LO), 1).astype(F32), 1.0, 0.0).astype(BF16)
        for part in range(2):
            columns = slice(part * QUARTER, (part + 1) * QUARTER)
            mix = jnp.where(rank == mix_slots((rows, LO), 1, part), 1.0, 0.0).astype(BF16)
            value = dot(low, by_expert[expert][:, columns]) + dot(mix, by_expert[expert][:, HALF:])
            terms[part].append(share * value)
    for part in range(2):
        columns = slice(part * QUARTER, (part + 1) * QUARTER)
        layer_out[:, columns] = (hidden[:, columns] + (terms[part][0] + terms[part][1])).astype(BF16)


def call(kernel, outs, in_specs, args, scratch=(), flops=0, bytes_accessed=0, vmem=32 << 20):
    many = isinstance(outs, (list, tuple))
    return pl.pallas_call(
        kernel,
        out_shape=outs,
        in_specs=in_specs,
        out_specs=[VMEM] * len(outs) if many else VMEM,
        scratch_shapes=list(scratch),
        compiler_params=pltpu.CompilerParams(vmem_limit_bytes=vmem),
        cost_estimate=pl.CostEstimate(flops=flops, bytes_accessed=bytes_accessed, transcendentals=0),
    )(*args)


def ring_order(n):
    return [0, 2, 4, 6, 7, 5, 3, 1] if n == 8 else list(range(n))


def add(a, b):
    return (a.astype(F32) + b.astype(F32)).astype(BF16)


def per_device(
    n,
    hosted,
    queries,
    new_kv,
    kv_pool,
    page_counts,
    tail_tokens,
    page_order,
    residual,
    norm_gain,
    routes,
    route_gates,
    w_gate,
    w_up,
    w_down,
    mig_pages,
    mig_dest,
):
    rows, width = queries.shape
    page_width = kv_pool.shape[2]
    entries = mig_pages.shape[1]
    pool = kv_pool.reshape(-1, page_width)
    around = ring_order(n)
    right = [(around[i], around[(i + 1) % n]) for i in range(n)]
    left = [(b, a) for a, b in right]
    swap = [(0, 1), (1, 0)]
    shape = jax.ShapeDtypeStruct

    moved_cols = entries * page_width + LANES
    hidden, slots, moved = call(
        functools.partial(attend_kernel, hosted),
        [
            shape((rows, width), F32),
            shape((hosted, LO, SLOT_COLS + LANES), BF16),
            shape((PAGE, moved_cols), BF16),
        ],
        [VMEM] * 9 + [SMEM] * 2,
        (
            queries,
            new_kv,
            pool,
            page_counts,
            tail_tokens.reshape(1, -1),
            page_order,
            residual,
            norm_gain.reshape(1, -1),
            routes,
            mig_pages,
            mig_dest,
        ),
        flops=500_000_000,
        bytes_accessed=3_500_000,
    )

    own_expert = lax.axis_index("expert")
    mine = lax.dynamic_index_in_dim(slots, own_expert, 0, keepdims=False)
    other = lax.dynamic_index_in_dim(slots, 1 - own_expert, 0, keepdims=False)
    theirs = lax.ppermute(other, "expert", swap)
    cols = SLOT_COLS + moved_cols
    message = call(
        pack_kernel,
        shape((2 * LO, cols), BF16),
        [VMEM] * 3,
        (mine, theirs, moved),
        flops=500_000,
        bytes_accessed=500_000,
    )

    far = n // 2
    cut = HALF + 3 * LANES
    from_left, from_right = [message], [message]
    for _ in range(far - 1):
        from_left.append(lax.ppermute(from_left[-1], "attn", right))
        from_right.append(lax.ppermute(from_right[-1], "attn", left))
    last_a = lax.ppermute(from_left[-1][:, :cut], "attn", right)
    last_b = lax.ppermute(from_right[-1][:, cut:], "attn", left)
    blocks = [message] + from_left[1:] + from_right[1:] + [last_a, last_b]

    ff = w_gate.shape[2]
    size = 16 * n
    outs = call(
        functools.partial(ffn_kernel, n, cut),
        [shape((2 * LO, SLOT_COLS), BF16)] * n,
        [VMEM] * (n + 1) + [ANY] * 3,
        (*blocks, w_gate[0], w_up[0], w_down[0]),
        scratch=(
            pltpu.VMEM((size, HALF), BF16),
            pltpu.VMEM((size, QUARTER), BF16),
            pltpu.VMEM((D, ff), BF16),
            pltpu.VMEM((D, ff), BF16),
            pltpu.VMEM((ff, D), BF16),
            pltpu.VMEM((2, size, ff), F32),
            pltpu.VMEM((2, size, ff), F32),
            pltpu.SemaphoreType.DMA((3, 4)),
        ),
        flops=2_000_000_000,
        bytes_accessed=12_000_000,
        vmem=48 << 20,
    )
    arrived = call(
        functools.partial(arrive_kernel, n, cut, page_width),
        shape((entries, PAGE, page_width), BF16),
        [VMEM] * (n + 1),
        tuple(blocks),
        scratch=(
            pltpu.VMEM((n, LANES), jnp.int32),
            pltpu.SMEM((n, LANES), jnp.int32),
            pltpu.SemaphoreType.DMA,
        ),
        flops=100_000,
        bytes_accessed=2_000_000,
    )

    to_left = {k: outs[k] for k in range(1, far)}
    to_right = {k: outs[far - 1 + k] for k in range(1, far)}
    split = SLOT_COLS // 2
    going_right = lax.ppermute(outs[n - 1][:, :split], "attn", right)
    going_left = lax.ppermute(outs[n - 1][:, split:], "attn", left)
    for k in range(far - 1, 0, -1):
        if k == far - 1:
            send_right = jnp.concatenate([add(to_right[k][:, :split], going_right), to_right[k][:, split:]], axis=1)
            send_left = jnp.concatenate([to_left[k][:, :split], add(to_left[k][:, split:], going_left)], axis=1)
        else:
            send_right, send_left = add(to_right[k], going_right), add(to_left[k], going_left)
        going_right = lax.ppermute(send_right, "attn", right)
        going_left = lax.ppermute(send_left, "attn", left)
    kept, other_half = call(
        finish_kernel,
        [shape((LO, SLOT_COLS), BF16)] * 2,
        [VMEM] * 3,
        (outs[0], going_right, going_left),
        flops=500_000,
        bytes_accessed=600_000,
    )
    returned = lax.ppermute(other_half, "expert", swap)
    layer_out = call(
        functools.partial(combine_kernel, hosted),
        shape((rows, width), BF16),
        [VMEM] * 5,
        (hidden, kept, returned, routes, route_gates),
        flops=20_000_000,
        bytes_accessed=800_000,
    )
    return layer_out, arrived


def solution(mesh):
    n, hosted = mesh.shape["attn"], mesh.shape["expert"]
    return jax.shard_map(
        functools.partial(per_device, n, hosted),
        mesh=mesh,
        in_specs=(
            P(("groups", "attn"), "expert"),
            P(("groups", "attn"), "expert"),
            P(("groups", "attn"), None, "expert"),
            P(("groups", "attn"), None),
            P(("groups", "attn")),
            P(("groups", "attn"), None),
            P(("groups", "attn"), "expert"),
            P("expert"),
            P(("groups", "attn"), None),
            P(("groups", "attn"), None),
            P("expert", None, "attn"),
            P("expert", None, "attn"),
            P("expert", "attn", None),
            P(("groups", "attn"), None),
            P(("groups", "attn"), None),
        ),
        out_specs=(P(("groups", "attn"), "expert"), P(("groups", "attn"), None, "expert")),
        check_vma=False,
    )
```

time: 208 us -> 72.4 us (0.35)
  blocking collectives: 91.6 us -> 0 us
  local copies, waits for them, and re-layouts: 53.7 us -> 9.52 us
  waiting for transfers between devices: 1.81 us -> 32 us
  other arithmetic: 20.7 us -> 0.22 us
  matrix products: 18.5 us -> 0 us
  between operations: 14.8 us -> 0.98 us
  starting transfers between devices: 5.2 us -> 18.2 us
  Pallas kernels: 0 us -> 11.1 us
    all_gather x2 -> x0, blocking collectives: 54.9 us -> none  [the longest x1 32.7 us: per_device(): blocks = lax.all_gather(payload[None], 'attn', axis=0, tiled=True)]
    ppermute x0 -> x18, waiting for transfers between devices: none -> 32 us  [the longest x3 14.4 us: per_device(): from_left.append(lax.ppermute(from_left[-1], 'attn', right))]
    unnamed x1 -> x0, blocking collectives: 30.2 us -> none
    gather x6 -> x0, local copies, waits for them, and re-layouts: 29.5 us -> none  [the longest x2 24.7 us: attend(): jnp.take(kv_pool, page_ids.reshape(-1), axis=0)]
    dot_general x10 -> x0, matrix products: 18.5 us -> none  [the longest x1 3.57 us: per_device(): jnp.dot(active, down_matrix, preferred_element_type=jnp.float32)]
    ppermute x0 -> x18, starting transfers between devices: none -> 18.2 us  [the longest x3 6.25 us: per_device(): from_left.append(lax.ppermute(from_left[-1], 'attn', right))]
    pallas_call x0 -> x6, Pallas kernels: none -> 11.1 us  [call(): pl.pallas_call(kernel, out_shape=outs, in_specs=in_specs, out_specs=[VMEM...]
    select_n x6 -> x0, other arithmetic: 7.62 us -> none  [the longest x2 5.26 us: attend(): jnp.take(kv_pool, page_ids.reshape(-1), axis=0)]
  transfers between devices with their start and end apart: 3 -> 18, of which waited for: 1 -> 10; matrix products, arithmetic and copies ran while one was open for 5% -> 0% of each run, Pallas kernels for 0% -> 2%
where the time goes in v1:
time: 72.4 us; the launch traced here: 72.1 us
  waiting for transfers between devices  32 us (44%)
  starting transfers between devices  18.2 us (25%)
  Pallas kernels  11.1 us (15%)
  local copies, waits for them, and re-layouts  9.52 us (13%)
  between operations  0.98 us (1%)
    ppermute x3, waiting for transfers between devices, per_device(): from_left.append(lax.ppermute(from_left[-1], 'attn', right))  14.4 us
    pallas_call x6, Pallas kernels, call(): pl.pallas_call(kernel, out_shape=outs, in_specs=in_specs, out_specs=[VMEM...  11.1 us
    unnamed x58, local copies, waits for them, and re-layouts  9.45 us
    ppermute x3, waiting for transfers between devices, per_device(): going_left = lax.ppermute(send_left, 'attn', left)  9.04 us
    ppermute x3, starting transfers between devices, per_device(): from_left.append(lax.ppermute(from_left[-1], 'attn', right))  6.25 us
    ppermute x1, waiting for transfers between devices, per_device(): last_b = lax.ppermute(from_right[-1][:, cut:], 'attn', left)  4.07 us
    ppermute x3, starting transfers between devices, per_device(): going_left = lax.ppermute(send_left, 'attn', left)  3.29 us
    ppermute x3, starting transfers between devices, per_device(): going_right = lax.ppermute(send_right, 'attn', right)  3.11 us
  transfers between devices with their start and end apart: 18, of which 10 were waited for; matrix products, arithmetic and copies ran while one was open for 0% of the time, Pallas kernels for 2%

profile of v1, /device:TPU:0, one launch (start us, length us, event | category | flops | bytes accessed | tf_op | source)
XLA Modules:
  0.0 72.1 jit_solution(15695873953530843790)
XLA Ops:
  0.6 0.9 %copy.17.routes = s32[32,2]{1,0:T(8,128)S(1)} copy(s32[32,2]{0,1:T(2,128)} %param.23) | data formatting | bytes 512 | tf_op args[8]
  1.6 1.7 %copy-done.1 = bf16[72,16,1024]{2,1,0:T(8,128)(2,1)S(1)} copy-done((bf16[72,16,1024]{2,1,0:T(8,128)(2,1)S(1)}, bf16[72,16,1024]{2,1,0:T(8,128)(2,1)}, u32[]{:S(2)}) %copy-start.1) | copy-done | bytes 2359320
  3.3 0.9 %copy-done.18 = bf16[32,3072]{1,0:T(8,128)(2,1)S(1)} copy-done((bf16[32,3072]{1,0:T(8,128)(2,1)S(1)}, bf16[32,3072]{1,0:T(8,128)(2,1)}, u32[]{:S(2)}) %copy-start.18) | copy-done | bytes 196632
  4.2 0.9 %copy-done.19 = bf16[32,3072]{1,0:T(8,128)(2,1)S(1)} copy-done((bf16[32,3072]{1,0:T(8,128)(2,1)S(1)}, bf16[32,3072]{1,0:T(8,128)(2,1)}, u32[]{:S(2)}) %copy-start.19) | copy-done | bytes 196632
  5.1 0.8 %copy-done.20 = bf16[32,1024]{1,0:T(8,128)(2,1)S(1)} copy-done((bf16[32,1024]{1,0:T(8,128)(2,1)S(1)}, bf16[32,1024]{1,0:T(8,128)(2,1)}, u32[]{:S(2)}) %copy-start.20) | copy-done | bytes 65560
  6.0 0.7 copy-done.21
  6.7 0.7 copy-done.22
  7.3 0.7 copy-done.23
  8.0 0.7 copy-done.24
  8.6 0.7 copy-done.25
  9.3 0.7 copy-done.26
  9.9 3.8 %shard_map.158 = (f32[32,3072]{1,0:T(8,128)S(1)}, bf16[2,8,4736]{2,1,0:T(8,128)(2,1)S(1)}, bf16[16,2176]{1,0:T(8,128)(2,1)S(1)}) custom-call(bf16[32,3072]{1,0:T(8,128)(2,1)S(1)} %copy-done.18, bf16[32,1024]{1,0:T(8,128)(2,1)S(1)} %copy-done.20, bf16[1152,1024]{1,0:T(8,128)(2,1)S(1)} %bitcast.11, s32[1,32]{1,0:T(1,128)S(1)} %copy-done.22, ...), custom_call_target="tpu_custom_call" | custom-call | flops 500000000 | bytes 3500000 | tf_op jit(solution)/shard_map/pallas_call | solution.py:318
  13.8 0.5 collective-permute-start
  14.3 0.9 %collective-permute-done.theirs = bf16[8,4736]{1,0:T(8,128)(2,1)S(1)} collective-permute-done((bf16[8,4736]{1,0:T(8,128)(2,1)S(1)}, bf16[8,4736]{1,0:T(8,128)(2,1)S(1)}, u32[]{:S(2)}, u32[]{:S(2)}) %collective-permute-start) | collective-permute-done | bytes 75808 | tf_op jit(solution)/shard_map/ppermute | solution.py:395
  15.2 0.1 shard_map.159.refs_0_
  15.3 3.0 %collective-permute-start.1 = (bf16[16,6784]{1,0:T(8,128)(2,1)S(1)}, bf16[16,6784]{1,0:T(8,128)(2,1)S(1)}, u32[]{:S(2)}, u32[]{:S(2)}) collective-permute-start(bf16[16,6784]{1,0:T(8,128)(2,1)S(1)} %shard_map.159.refs_0_), channel_id=1, source_target_pairs={{0,4},{4,8},{8,12},{12,14},{14,10},{10,6},{6,2},{2,0},{1,5},{5,9},... | collective-permute-start | bytes 651272 | tf_op jit(solution)/shard_map/ppermute | solution.py:410
  18.3 0.0 collective-permute-start.4
  18.3 5.6 %collective-permute-done.1.refs_1_ = bf16[16,6784]{1,0:T(8,128)(2,1)S(1)} collective-permute-done((bf16[16,6784]{1,0:T(8,128)(2,1)S(1)}, bf16[16,6784]{1,0:T(8,128)(2,1)S(1)}, u32[]{:S(2)}, u32[]{:S(2)}) %collective-permute-start.1) | collective-permute-done | bytes 217120 | tf_op jit(solution)/shard_map/ppermute | solution.py:410
  23.9 1.8 %collective-permute-start.2 = (bf16[16,6784]{1,0:T(8,128)(2,1)S(1)}, bf16[16,6784]{1,0:T(8,128)(2,1)S(1)}, u32[]{:S(2)}, u32[]{:S(2)}) collective-permute-start(bf16[16,6784]{1,0:T(8,128)(2,1)S(1)} %collective-permute-done.1.refs_1_), channel_id=1, source_target_pairs={{0,4},{4,8},{8,12},{12,14},{14,10},{10,6},{6,2},{2,0},{1,5},{5,9},... | collective-permute-start | bytes 651272 | tf_op jit(solution)/shard_map/ppermute | solution.py:410
  25.7 0.2 collective-permute-start.5
  25.9 4.9 %collective-permute-done.2.refs_2_ = bf16[16,6784]{1,0:T(8,128)(2,1)S(1)} collective-permute-done((bf16[16,6784]{1,0:T(8,128)(2,1)S(1)}, bf16[16,6784]{1,0:T(8,128)(2,1)S(1)}, u32[]{:S(2)}, u32[]{:S(2)}) %collective-permute-start.2) | collective-permute-done | bytes 217120 | tf_op jit(solution)/shard_map/ppermute | solution.py:410
  30.8 1.5 %collective-permute-start.3 = (bf16[16,6784]{1,0:T(8,128)(2,1)S(1)}, bf16[16,6784]{1,0:T(8,128)(2,1)S(1)}, u32[]{:S(2)}, u32[]{:S(2)}) collective-permute-start(bf16[16,6784]{1,0:T(8,128)(2,1)S(1)} %collective-permute-done.2.refs_2_), channel_id=1, source_target_pairs={{0,4},{4,8},{8,12},{12,14},{14,10},{10,6},{6,2},{2,0},{1,5},{5,9},... | collective-permute-start | bytes 651272 | tf_op jit(solution)/shard_map/ppermute | solution.py:410
  32.3 0.5 collective-permute-start.6
  32.8 4.0 %collective-permute-done.3.refs_3_ = bf16[16,6784]{1,0:T(8,128)(2,1)S(1)} collective-permute-done((bf16[16,6784]{1,0:T(8,128)(2,1)S(1)}, bf16[16,6784]{1,0:T(8,128)(2,1)S(1)}, u32[]{:S(2)}, u32[]{:S(2)}) %collective-permute-start.3) | collective-permute-done | bytes 217120 | tf_op jit(solution)/shard_map/ppermute | solution.py:410
  36.8 1.4 %collective-permute-start.7 = (bf16[16,3456]{1,0:T(8,128)(2,1)S(1)}, bf16[16,3456]{1,0:T(8,128)(2,1)S(1)}, u32[]{:S(2)}, u32[]{:S(2)}) collective-permute-start(bf16[16,3456]{1,0:T(8,128)(2,1)S(1)} %slice.32), channel_id=1, source_target_pairs={{0,4},{4,8},{8,12},{12,14},{14,10},{10,6},{6,2},{2,0},{1,5},{5,9},... | collective-permute-start | bytes 331784 | tf_op jit(solution)/shard_map/ppermute | solution.py:412
  38.3 0.7 collective-permute-start.8
  38.9 4.1 %collective-permute-done.8.refs_8_ = bf16[16,3328]{1,0:T(8,128)(2,1)S(1)} collective-permute-done((bf16[16,3328]{1,0:T(8,128)(2,1)S(1)}, bf16[16,3328]{1,0:T(8,128)(2,1)S(1)}, u32[]{:S(2)}, u32[]{:S(2)}) %collective-permute-start.8) | collective-permute-done | bytes 106528 | tf_op jit(solution)/shard_map/ppermute | solution.py:413
  43.0 4.2 %shard_map.160 = (bf16[16,4608]{1,0:T(8,128)(2,1)S(1)}, bf16[16,4608]{1,0:T(8,128)(2,1)S(1)}, bf16[16,4608]{1,0:T(8,128)(2,1)S(1)}, bf16[16,4608]{1,0:T(8,128)(2...) custom-call(bf16[16,6784]{1,0:T(8,128)(2,1)S(1)} %shard_map.159.refs, ...), custom_call_target="tpu_custom_call" | custom-call | flops 2000000000 | bytes 12000000 | tf_op jit(solution)/shard_map/pallas_call | solution.py:318
  47.3 0.0 copy-start.27
  47.4 0.0 copy-start.15
  47.4 0.7 collective-permute-start.13
  48.1 1.4 %collective-permute-start.9 = (bf16[16,2304]{1,0:T(8,128)(2,1)S(1)}, bf16[16,2304]{1,0:T(8,128)(2,1)S(1)}, u32[]{:S(2)}, u32[]{:S(2)}) collective-permute-start(bf16[16,2304]{1,0:T(8,128)(2,1)S(1)} %get-tuple-element.31), channel_id=1, source_target_pairs={{0,4},{4,8},{8,12},{12,14},{14,10},{10,6},{6,2},{2,0},{1,5},{5,9},... | collective-permute-start | bytes 221192 | tf_op jit(solution)/shard_map/ppermute | solution.py:454
  49.5 2.3 %collective-permute-done.13 = bf16[16,2304]{1,0:T(8,128)(2,1)S(1)} collective-permute-done((bf16[16,2304]{1,0:T(8,128)(2,1)S(1)}, bf16[16,2304]{1,0:T(8,128)(2,1)S(1)}, u32[]{:S(2)}, u32[]{:S(2)}) %collective-permute-start.13) | collective-permute-done | bytes 73760 | tf_op jit(solution)/shard_map/ppermute | solution.py:455
  51.9 1.0 %collective-permute-start.14 = (bf16[16,4608]{1,0:T(8,128)(2,1)S(1)}, bf16[16,4608]{1,0:T(8,128)(2,1)S(1)}, u32[]{:S(2)}, u32[]{:S(2)}) collective-permute-start(bf16[16,4608]{1,0:T(8,128)(2,1)S(1)} %pad_maximum_fusion.1), channel_id=1, source_target_pairs={{4,0},{8,4},{12,8},{14,12},{10,14},{6,10},{2,6},{0,2},{5,1},{9,5},... | collective-permute-start | bytes 442376 | tf_op jit(solution)/shard_map/ppermute | solution.py:463
  52.9 1.2 %collective-permute-start.10 = (bf16[16,4608]{1,0:T(8,128)(2,1)S(1)}, bf16[16,4608]{1,0:T(8,128)(2,1)S(1)}, u32[]{:S(2)}, u32[]{:S(2)}) collective-permute-start(bf16[16,4608]{1,0:T(8,128)(2,1)S(1)} %pad_maximum_fusion), channel_id=1, source_target_pairs={{0,4},{4,8},{8,12},{12,14},{14,10},{10,6},{6,2},{2,0},{1,5},{5,9},... | collective-permute-start | bytes 442376 | tf_op jit(solution)/shard_map/ppermute | solution.py:462
  54.1 3.0 %collective-permute-done.14 = bf16[16,4608]{1,0:T(8,128)(2,1)S(1)} collective-permute-done((bf16[16,4608]{1,0:T(8,128)(2,1)S(1)}, bf16[16,4608]{1,0:T(8,128)(2,1)S(1)}, u32[]{:S(2)}, u32[]{:S(2)}) %collective-permute-start.14) | collective-permute-done | bytes 147488 | tf_op jit(solution)/shard_map/ppermute | solution.py:463
  57.1 1.2 %collective-permute-start.15 = (bf16[16,4608]{1,0:T(8,128)(2,1)S(1)}, bf16[16,4608]{1,0:T(8,128)(2,1)S(1)}, u32[]{:S(2)}, u32[]{:S(2)}) collective-permute-start(bf16[16,4608]{1,0:T(8,128)(2,1)S(1)} %add_convert_fusion.1), channel_id=1, source_target_pairs={{4,0},{8,4},{12,8},{14,12},{10,14},{6,10},{2,6},{0,2},{5,1},{9,5},... | collective-permute-start | bytes 442376 | tf_op jit(solution)/shard_map/ppermute | solution.py:463
  58.3 1.0 %collective-permute-start.11 = (bf16[16,4608]{1,0:T(8,128)(2,1)S(1)}, bf16[16,4608]{1,0:T(8,128)(2,1)S(1)}, u32[]{:S(2)}, u32[]{:S(2)}) collective-permute-start(bf16[16,4608]{1,0:T(8,128)(2,1)S(1)} %add_convert_fusion.3), channel_id=1, source_target_pairs={{0,4},{4,8},{8,12},{12,14},{14,10},{10,6},{6,2},{2,0},{1,5},{5,9},... | collective-permute-start | bytes 442376 | tf_op jit(solution)/shard_map/ppermute | solution.py:462
  59.3 3.0 %collective-permute-done.15 = bf16[16,4608]{1,0:T(8,128)(2,1)S(1)} collective-permute-done((bf16[16,4608]{1,0:T(8,128)(2,1)S(1)}, bf16[16,4608]{1,0:T(8,128)(2,1)S(1)}, u32[]{:S(2)}, u32[]{:S(2)}) %collective-permute-start.15) | collective-permute-done | bytes 147488 | tf_op jit(solution)/shard_map/ppermute | solution.py:463
  62.4 1.2 %collective-permute-start.16 = (bf16[16,4608]{1,0:T(8,128)(2,1)S(1)}, bf16[16,4608]{1,0:T(8,128)(2,1)S(1)}, u32[]{:S(2)}, u32[]{:S(2)}) collective-permute-start(bf16[16,4608]{1,0:T(8,128)(2,1)S(1)} %add_convert_fusion), channel_id=1, source_target_pairs={{4,0},{8,4},{12,8},{14,12},{10,14},{6,10},{2,6},{0,2},{5,1},{9,5},... | collective-permute-start | bytes 442376 | tf_op jit(solution)/shard_map/ppermute | solution.py:463
  63.6 1.0 %collective-permute-start.12 = (bf16[16,4608]{1,0:T(8,128)(2,1)S(1)}, bf16[16,4608]{1,0:T(8,128)(2,1)S(1)}, u32[]{:S(2)}, u32[]{:S(2)}) collective-permute-start(bf16[16,4608]{1,0:T(8,128)(2,1)S(1)} %add_convert_fusion.2), channel_id=1, source_target_pairs={{0,4},{4,8},{8,12},{12,14},{14,10},{10,6},{6,2},{2,0},{1,5},{5,9},... | collective-permute-start | bytes 442376 | tf_op jit(solution)/shard_map/ppermute | solution.py:462
  64.6 3.0 %collective-permute-done.16.from_right = bf16[16,4608]{1,0:T(8,128)(2,1)S(1)} collective-permute-done((bf16[16,4608]{1,0:T(8,128)(2,1)S(1)}, bf16[16,4608]{1,0:T(8,128)(2,1)S(1)}, u32[]{:S(2)}, u32[]{:S(2)}) %collective-permute-start.16) | collective-permute-done | bytes 147488 | tf_op jit(solution)/shard_map/ppermute | solution.py:463
  67.6 1.2 %collective-permute-done.12.from_left = bf16[16,4608]{1,0:T(8,128)(2,1)S(1)} collective-permute-done((bf16[16,4608]{1,0:T(8,128)(2,1)S(1)}, bf16[16,4608]{1,0:T(8,128)(2,1)S(1)}, u32[]{:S(2)}, u32[]{:S(2)}) %collective-permute-start.12) | collective-permute-done | bytes 147488 | tf_op jit(solution)/shard_map/ppermute | solution.py:462
  68.8 0.1 shard_map.161
  68.8 0.1 collective-permute-start.17
  68.9 0.1 copy.19.gates
  69.1 1.5 %shard_map.163 = bf16[2,16,1024]{2,1,0:T(8,128)(2,1)} custom-call(bf16[16,6784]{1,0:T(8,128)(2,1)S(1)} %shard_map.159.refs_0_, bf16[16,6784]{1,0:T(8,128)(2,1)S(1)} %copy-done.7, bf16[16,6784]{1,0:T(8,128)(2,1)S(1)} %copy-done.11, bf16[16,6784]{1,0:T(8,128)(2,1)S(1)} %copy-done.3, bf16[16,6784]{1,0:T(8,128)(2,1)S(1)} %copy-done.9, ...), custom_call_target="tpu_custom_call" | custom-call | flops 100000 | bytes 2000000 | tf_op jit(solution)/shard_map/pallas_call | solution.py:318
  70.7 1.4 %shard_map.162 = bf16[32,3072]{1,0:T(8,128)(2,1)} custom-call(f32[32,3072]{1,0:T(8,128)S(1)} %copy-done.17, bf16[8,4608]{1,0:T(8,128)(2,1)S(1)} %get-tuple-element.26.mine, bf16[8,4608]{1,0:T(8,128)(2,1)S(1)} %collective-permute-done.17.theirs, s32[32,2]{1,0:T(8,128)S(1)} %copy.17.routes, f32[32,2]{1,0:T(8,128)S(1)} %copy.19.gates), custom_call_target="tpu_custom_call" | custom-call | flops 20000000 | bytes 800000 | tf_op jit(solution)/shard_map/pallas_call | solution.py:318
  (66 shorter events, 0.4 us)
Async XLA Ops:
  0.6 42.4 %copy-start = (bf16[1,6144,256]{2,1,0:T(8,128)(2,1)S(1)}, bf16[1,6144,256]{2,1,0:T(8,128)(2,1)}, u32[]{:S(2)}) copy-start(bf16[1,6144,256]{2,1,0:T(8,128)(2,1)} %param.25) | copy-start | bytes 9437188
  1.6 1.7 %copy-start.1 = (bf16[72,16,1024]{2,1,0:T(8,128)(2,1)S(1)}, bf16[72,16,1024]{2,1,0:T(8,128)(2,1)}, u32[]{:S(2)}) copy-start(bf16[72,16,1024]{2,1,0:T(8,128)(2,1)} %param.17) | copy-start | bytes 7077892
  3.3 0.9 %copy-start.18 = (bf16[32,3072]{1,0:T(8,128)(2,1)S(1)}, bf16[32,3072]{1,0:T(8,128)(2,1)}, u32[]{:S(2)}) copy-start(bf16[32,3072]{1,0:T(8,128)(2,1)} %queries.1) | copy-start | bytes 589828
  4.2 0.9 %copy-start.19 = (bf16[32,3072]{1,0:T(8,128)(2,1)S(1)}, bf16[32,3072]{1,0:T(8,128)(2,1)}, u32[]{:S(2)}) copy-start(bf16[32,3072]{1,0:T(8,128)(2,1)} %residual.1) | copy-start | bytes 589828
  5.1 0.8 %copy-start.20 = (bf16[32,1024]{1,0:T(8,128)(2,1)S(1)}, bf16[32,1024]{1,0:T(8,128)(2,1)}, u32[]{:S(2)}) copy-start(bf16[32,1024]{1,0:T(8,128)(2,1)} %new_kv.1) | copy-start | bytes 196612
  6.0 0.7 copy-start.21
  6.7 0.7 copy-start.22
  7.3 0.7 copy-start.23
  8.0 0.7 copy-start.24
  8.6 0.7 copy-start.25
  9.3 0.7 copy-start.26
  13.7 29.3 %copy-start.16 = (f32[32,3072]{1,0:T(8,128)}, f32[32,3072]{1,0:T(8,128)S(1)}, u32[]{:S(2)}) copy-start(f32[32,3072]{1,0:T(8,128)S(1)} %get-tuple-element.15.hidden) | copy-start | bytes 1179652
  13.8 1.4 %collective-permute-start = (bf16[8,4736]{1,0:T(8,128)(2,1)S(1)}, bf16[8,4736]{1,0:T(8,128)(2,1)S(1)}, u32[]{:S(2)}, u32[]{:S(2)}) collective-permute-start(bf16[8,4736]{1,0:T(8,128)(2,1)S(1)} %get-tuple-element.28), channel_id=1, source_target_pairs={{0,1},{1,0},{2,3},{3,2},{4,5},{5,4},{6,7},{7,6},{8,9},{9,8},{10,11... | collective-permute-start | bytes 227336 | tf_op jit(solution)/shard_map/ppermute | solution.py:395
  15.3 8.6 %collective-permute-start.1 = (bf16[16,6784]{1,0:T(8,128)(2,1)S(1)}, bf16[16,6784]{1,0:T(8,128)(2,1)S(1)}, u32[]{:S(2)}, u32[]{:S(2)}) collective-permute-start(bf16[16,6784]{1,0:T(8,128)(2,1)S(1)} %shard_map.159.refs_0_), channel_id=1, source_target_pairs={{0,4},{4,8},{8,12},{12,14},{14,10},{10,6},{6,2},{2,0},{1,5},{5,9},... | collective-permute-start | bytes 651272 | tf_op jit(solution)/shard_map/ppermute | solution.py:410
  18.3 7.4 %collective-permute-start.4 = (bf16[16,6784]{1,0:T(8,128)(2,1)S(1)}, bf16[16,6784]{1,0:T(8,128)(2,1)S(1)}, u32[]{:S(2)}, u32[]{:S(2)}) collective-permute-start(bf16[16,6784]{1,0:T(8,128)(2,1)S(1)} %shard_map.159.refs_0_), channel_id=1, source_target_pairs={{4,0},{8,4},{12,8},{14,12},{10,14},{6,10},{2,6},{0,2},{5,1},{9,5},... | collective-permute-start | bytes 651272 | tf_op jit(solution)/shard_map/ppermute | solution.py:411
  23.9 23.3 %copy-start.6 = (bf16[16,6784]{1,0:T(8,128)(2,1)}, bf16[16,6784]{1,0:T(8,128)(2,1)S(1)}, u32[]{:S(2)}) copy-start(bf16[16,6784]{1,0:T(8,128)(2,1)S(1)} %collective-permute-done.1.refs_1_) | copy-start | bytes 651268
  23.9 6.9 %collective-permute-start.2 = (bf16[16,6784]{1,0:T(8,128)(2,1)S(1)}, bf16[16,6784]{1,0:T(8,128)(2,1)S(1)}, u32[]{:S(2)}, u32[]{:S(2)}) collective-permute-start(bf16[16,6784]{1,0:T(8,128)(2,1)S(1)} %collective-permute-done.1.refs_1_), channel_id=1, source_target_pairs={{0,4},{4,8},{8,12},{12,14},{14,10},{10,6},{6,2},{2,0},{1,5},{5,9},... | collective-permute-start | bytes 651272 | tf_op jit(solution)/shard_map/ppermute | solution.py:410
  25.7 21.6 %copy-start.8 = (bf16[16,6784]{1,0:T(8,128)(2,1)}, bf16[16,6784]{1,0:T(8,128)(2,1)S(1)}, u32[]{:S(2)}) copy-start(bf16[16,6784]{1,0:T(8,128)(2,1)S(1)} %collective-permute-done.4.refs_4_) | copy-start | bytes 651268
  25.7 6.6 %collective-permute-start.5 = (bf16[16,6784]{1,0:T(8,128)(2,1)S(1)}, bf16[16,6784]{1,0:T(8,128)(2,1)S(1)}, u32[]{:S(2)}, u32[]{:S(2)}) collective-permute-start(bf16[16,6784]{1,0:T(8,128)(2,1)S(1)} %collective-permute-done.4.refs_4_), channel_id=1, source_target_pairs={{4,0},{8,4},{12,8},{14,12},{10,14},{6,10},{2,6},{0,2},{5,1},{9,5},... | collective-permute-start | bytes 651272 | tf_op jit(solution)/shard_map/ppermute | solution.py:411
  30.8 16.5 %copy-start.10 = (bf16[16,6784]{1,0:T(8,128)(2,1)}, bf16[16,6784]{1,0:T(8,128)(2,1)S(1)}, u32[]{:S(2)}) copy-start(bf16[16,6784]{1,0:T(8,128)(2,1)S(1)} %collective-permute-done.2.refs_2_) | copy-start | bytes 651268
  30.8 6.0 %collective-permute-start.3 = (bf16[16,6784]{1,0:T(8,128)(2,1)S(1)}, bf16[16,6784]{1,0:T(8,128)(2,1)S(1)}, u32[]{:S(2)}, u32[]{:S(2)}) collective-permute-start(bf16[16,6784]{1,0:T(8,128)(2,1)S(1)} %collective-permute-done.2.refs_2_), channel_id=1, source_target_pairs={{0,4},{4,8},{8,12},{12,14},{14,10},{10,6},{6,2},{2,0},{1,5},{5,9},... | collective-permute-start | bytes 651272 | tf_op jit(solution)/shard_map/ppermute | solution.py:410
  32.3 15.0 %copy-start.12 = (bf16[16,6784]{1,0:T(8,128)(2,1)}, bf16[16,6784]{1,0:T(8,128)(2,1)S(1)}, u32[]{:S(2)}) copy-start(bf16[16,6784]{1,0:T(8,128)(2,1)S(1)} %collective-permute-done.5.refs_5_) | copy-start | bytes 651268
  32.3 6.0 %collective-permute-start.6 = (bf16[16,6784]{1,0:T(8,128)(2,1)S(1)}, bf16[16,6784]{1,0:T(8,128)(2,1)S(1)}, u32[]{:S(2)}, u32[]{:S(2)}) collective-permute-start(bf16[16,6784]{1,0:T(8,128)(2,1)S(1)} %collective-permute-done.5.refs_5_), channel_id=1, source_target_pairs={{4,0},{8,4},{12,8},{14,12},{10,14},{6,10},{2,6},{0,2},{5,1},{9,5},... | collective-permute-start | bytes 651272 | tf_op jit(solution)/shard_map/ppermute | solution.py:411
  36.8 10.5 %copy-start.2 = (bf16[16,6784]{1,0:T(8,128)(2,1)}, bf16[16,6784]{1,0:T(8,128)(2,1)S(1)}, u32[]{:S(2)}) copy-start(bf16[16,6784]{1,0:T(8,128)(2,1)S(1)} %collective-permute-done.3.refs_3_) | copy-start | bytes 651268
  36.8 6.2 %collective-permute-start.7 = (bf16[16,3456]{1,0:T(8,128)(2,1)S(1)}, bf16[16,3456]{1,0:T(8,128)(2,1)S(1)}, u32[]{:S(2)}, u32[]{:S(2)}) collective-permute-start(bf16[16,3456]{1,0:T(8,128)(2,1)S(1)} %slice.32), channel_id=1, source_target_pairs={{0,4},{4,8},{8,12},{12,14},{14,10},{10,6},{6,2},{2,0},{1,5},{5,9},... | collective-permute-start | bytes 331784 | tf_op jit(solution)/shard_map/ppermute | solution.py:412
  38.2 9.0 %copy-start.4 = (bf16[16,6784]{1,0:T(8,128)(2,1)}, bf16[16,6784]{1,0:T(8,128)(2,1)S(1)}, u32[]{:S(2)}) copy-start(bf16[16,6784]{1,0:T(8,128)(2,1)S(1)} %collective-permute-done.6.refs_6_) | copy-start | bytes 651268
  38.3 4.8 %collective-permute-start.8 = (bf16[16,3328]{1,0:T(8,128)(2,1)S(1)}, bf16[16,3328]{1,0:T(8,128)(2,1)S(1)}, u32[]{:S(2)}, u32[]{:S(2)}) collective-permute-start(bf16[16,3328]{1,0:T(8,128)(2,1)S(1)} %slice.33), channel_id=1, source_target_pairs={{4,0},{8,4},{12,8},{14,12},{10,14},{6,10},{2,6},{0,2},{5,1},{9,5},... | collective-permute-start | bytes 319496 | tf_op jit(solution)/shard_map/ppermute | solution.py:413
  43.0 4.3 %copy-start.14 = (bf16[16,3328]{1,0:T(8,128)(2,1)}, bf16[16,3328]{1,0:T(8,128)(2,1)S(1)}, u32[]{:S(2)}) copy-start(bf16[16,3328]{1,0:T(8,128)(2,1)S(1)} %collective-permute-done.8.refs_8_) | copy-start | bytes 319492
  47.3 21.6 %copy-start.27 = (f32[32,2]{0,1:T(2,128)S(1)}, f32[32,2]{0,1:T(2,128)}, u32[]{:S(2)}) copy-start(f32[32,2]{0,1:T(2,128)} %param.24) | copy-start | bytes 772
  47.3 23.3 %copy-start.17 = (f32[32,3072]{1,0:T(8,128)S(1)}, f32[32,3072]{1,0:T(8,128)}, u32[]{:S(2)}) copy-start(f32[32,3072]{1,0:T(8,128)} %copy-done.16) | copy-start | bytes 1179652
  47.3 21.7 %copy-start.3 = (bf16[16,6784]{1,0:T(8,128)(2,1)S(1)}, bf16[16,6784]{1,0:T(8,128)(2,1)}, u32[]{:S(2)}) copy-start(bf16[16,6784]{1,0:T(8,128)(2,1)} %copy-done.2) | copy-start | bytes 651268
  47.3 21.7 %copy-start.5 = (bf16[16,6784]{1,0:T(8,128)(2,1)S(1)}, bf16[16,6784]{1,0:T(8,128)(2,1)}, u32[]{:S(2)}) copy-start(bf16[16,6784]{1,0:T(8,128)(2,1)} %copy-done.4) | copy-start | bytes 651268
  47.3 21.7 %copy-start.7 = (bf16[16,6784]{1,0:T(8,128)(2,1)S(1)}, bf16[16,6784]{1,0:T(8,128)(2,1)}, u32[]{:S(2)}) copy-start(bf16[16,6784]{1,0:T(8,128)(2,1)} %copy-done.6) | copy-start | bytes 651268
  47.4 21.7 %copy-start.9 = (bf16[16,6784]{1,0:T(8,128)(2,1)S(1)}, bf16[16,6784]{1,0:T(8,128)(2,1)}, u32[]{:S(2)}) copy-start(bf16[16,6784]{1,0:T(8,128)(2,1)} %copy-done.8) | copy-start | bytes 651268
  47.4 21.7 %copy-start.11 = (bf16[16,6784]{1,0:T(8,128)(2,1)S(1)}, bf16[16,6784]{1,0:T(8,128)(2,1)}, u32[]{:S(2)}) copy-start(bf16[16,6784]{1,0:T(8,128)(2,1)} %copy-done.10) | copy-start | bytes 651268
  47.4 21.7 %copy-start.13 = (bf16[16,6784]{1,0:T(8,128)(2,1)S(1)}, bf16[16,6784]{1,0:T(8,128)(2,1)}, u32[]{:S(2)}) copy-start(bf16[16,6784]{1,0:T(8,128)(2,1)} %copy-done.12) | copy-start | bytes 651268
  47.4 21.7 %copy-start.15 = (bf16[16,3328]{1,0:T(8,128)(2,1)S(1)}, bf16[16,3328]{1,0:T(8,128)(2,1)}, u32[]{:S(2)}) copy-start(bf16[16,3328]{1,0:T(8,128)(2,1)} %copy-done.14) | copy-start | bytes 319492
  47.4 4.4 %collective-permute-start.13 = (bf16[16,2304]{1,0:T(8,128)(2,1)S(1)}, bf16[16,2304]{1,0:T(8,128)(2,1)S(1)}, u32[]{:S(2)}, u32[]{:S(2)}) collective-permute-start(bf16[16,2304]{1,0:T(8,128)(2,1)S(1)} %get-tuple-element.30), channel_id=1, source_target_pairs={{4,0},{8,4},{12,8},{14,12},{10,14},{6,10},{2,6},{0,2},{5,1},{9,5},... | collective-permute-start | bytes 221192 | tf_op jit(solution)/shard_map/ppermute | solution.py:455
  48.1 4.8 %collective-permute-start.9 = (bf16[16,2304]{1,0:T(8,128)(2,1)S(1)}, bf16[16,2304]{1,0:T(8,128)(2,1)S(1)}, u32[]{:S(2)}, u32[]{:S(2)}) collective-permute-start(bf16[16,2304]{1,0:T(8,128)(2,1)S(1)} %get-tuple-element.31), channel_id=1, source_target_pairs={{0,4},{4,8},{8,12},{12,14},{14,10},{10,6},{6,2},{2,0},{1,5},{5,9},... | collective-permute-start | bytes 221192 | tf_op jit(solution)/shard_map/ppermute | solution.py:454
  51.9 5.2 %collective-permute-start.14 = (bf16[16,4608]{1,0:T(8,128)(2,1)S(1)}, bf16[16,4608]{1,0:T(8,128)(2,1)S(1)}, u32[]{:S(2)}, u32[]{:S(2)}) collective-permute-start(bf16[16,4608]{1,0:T(8,128)(2,1)S(1)} %pad_maximum_fusion.1), channel_id=1, source_target_pairs={{4,0},{8,4},{12,8},{14,12},{10,14},{6,10},{2,6},{0,2},{5,1},{9,5},... | collective-permute-start | bytes 442376 | tf_op jit(solution)/shard_map/ppermute | solution.py:463
  52.9 5.4 %collective-permute-start.10 = (bf16[16,4608]{1,0:T(8,128)(2,1)S(1)}, bf16[16,4608]{1,0:T(8,128)(2,1)S(1)}, u32[]{:S(2)}, u32[]{:S(2)}) collective-permute-start(bf16[16,4608]{1,0:T(8,128)(2,1)S(1)} %pad_maximum_fusion), channel_id=1, source_target_pairs={{0,4},{4,8},{8,12},{12,14},{14,10},{10,6},{6,2},{2,0},{1,5},{5,9},... | collective-permute-start | bytes 442376 | tf_op jit(solution)/shard_map/ppermute | solution.py:462
  57.1 5.2 %collective-permute-start.15 = (bf16[16,4608]{1,0:T(8,128)(2,1)S(1)}, bf16[16,4608]{1,0:T(8,128)(2,1)S(1)}, u32[]{:S(2)}, u32[]{:S(2)}) collective-permute-start(bf16[16,4608]{1,0:T(8,128)(2,1)S(1)} %add_convert_fusion.1), channel_id=1, source_target_pairs={{4,0},{8,4},{12,8},{14,12},{10,14},{6,10},{2,6},{0,2},{5,1},{9,5},... | collective-permute-start | bytes 442376 | tf_op jit(solution)/shard_map/ppermute | solution.py:463
  58.3 5.2 %collective-permute-start.11 = (bf16[16,4608]{1,0:T(8,128)(2,1)S(1)}, bf16[16,4608]{1,0:T(8,128)(2,1)S(1)}, u32[]{:S(2)}, u32[]{:S(2)}) collective-permute-start(bf16[16,4608]{1,0:T(8,128)(2,1)S(1)} %add_convert_fusion.3), channel_id=1, source_target_pairs={{0,4},{4,8},{8,12},{12,14},{14,10},{10,6},{6,2},{2,0},{1,5},{5,9},... | collective-permute-start | bytes 442376 | tf_op jit(solution)/shard_map/ppermute | solution.py:462
  62.4 5.2 %collective-permute-start.16 = (bf16[16,4608]{1,0:T(8,128)(2,1)S(1)}, bf16[16,4608]{1,0:T(8,128)(2,1)S(1)}, u32[]{:S(2)}, u32[]{:S(2)}) collective-permute-start(bf16[16,4608]{1,0:T(8,128)(2,1)S(1)} %add_convert_fusion), channel_id=1, source_target_pairs={{4,0},{8,4},{12,8},{14,12},{10,14},{6,10},{2,6},{0,2},{5,1},{9,5},... | collective-permute-start | bytes 442376 | tf_op jit(solution)/shard_map/ppermute | solution.py:463
  63.6 5.2 %collective-permute-start.12 = (bf16[16,4608]{1,0:T(8,128)(2,1)S(1)}, bf16[16,4608]{1,0:T(8,128)(2,1)S(1)}, u32[]{:S(2)}, u32[]{:S(2)}) collective-permute-start(bf16[16,4608]{1,0:T(8,128)(2,1)S(1)} %add_convert_fusion.2), channel_id=1, source_target_pairs={{0,4},{4,8},{8,12},{12,14},{14,10},{10,6},{6,2},{2,0},{1,5},{5,9},... | collective-permute-start | bytes 442376 | tf_op jit(solution)/shard_map/ppermute | solution.py:462
  68.8 1.8 %collective-permute-start.17 = (bf16[8,4608]{1,0:T(8,128)(2,1)S(1)}, bf16[8,4608]{1,0:T(8,128)(2,1)S(1)}, u32[]{:S(2)}, u32[]{:S(2)}) collective-permute-start(bf16[8,4608]{1,0:T(8,128)(2,1)S(1)} %get-tuple-element.27), channel_id=1, source_target_pairs={{0,1},{1,0},{2,3},{3,2},{4,5},{5,4},{6,7},{7,6},{8,9},{9,8},{10,11... | collective-permute-start | bytes 221192 | tf_op jit(solution)/shard_map/ppermute | solution.py:472

commit v2 on v1

--- a/solution.py
+++ b/solution.py
@@ -18,12 +18,12 @@
 SLOT_COLS = HALF + QUARTER
 LANES = 128
 SCORE_SCALE = HD ** (-0.5)
-NEG = -1e30
+NEG = -(2.0**100)
 F32 = jnp.float32
 BF16 = jnp.bfloat16
 VMEM = pl.BlockSpec(memory_space=pltpu.VMEM)
 SMEM = pl.BlockSpec(memory_space=pltpu.SMEM)
-ANY = pl.BlockSpec(memory_space=pl.ANY)
+HBM = pl.BlockSpec(memory_space=pltpu.HBM)
 
 
 def iota(shape, dim):
@@ -51,8 +51,7 @@
 
 
 def members(routes, expert):
-    chosen = (routes[:, 0:1] == expert) | (routes[:, 1:2] == expert)
-    return jnp.where(chosen, 1.0, 0.0)
+    return jnp.max(jnp.where(routes == expert, 1.0, 0.0), axis=0, keepdims=True)
 
 
 def mix_slots(shape, dim, part):
@@ -69,15 +68,27 @@
     return high.astype(F32), middle.astype(F32), low.astype(F32)
 
 
-def attend_kernel(
-    hosted, queries, new_kv, pool, counts, tails, order, residual, gain, routes, mig_pages, mig_dest, hidden, slots, moved
-):
+def attend_kernel(hosted, *refs):
+    sources, (hidden, kept, other), held_here, sems = refs[:11], refs[11:14], refs[14:25], refs[25]
+    counts, tails, order, routes, mig_pages, mig_dest, queries, new_kv, residual, gain, pool = held_here
     rows = queries.shape[0]
     tokens = pool.shape[0]
     pages = tokens // PAGE
     heads_here = pool.shape[1] // (2 * HD)
     group = queries.shape[1] // (heads_here * HD)
-    width = queries.shape[1]
+
+    copies = [
+        pltpu.make_async_copy(a, b, sems.at[k]) for k, (a, b) in enumerate(zip(sources[:-1], held_here[:-1]))
+    ]
+    for head in range(heads_here):
+        columns = pl.ds(2 * head * HD, 2 * HD)
+        copies.append(
+            pltpu.make_async_copy(sources[-1].at[:, columns], pool.at[:, columns], sems.at[len(sources) - 1 + head])
+        )
+    for copy in copies[:8] + copies[10:] + copies[8:10]:
+        copy.start()
+    for copy in copies[:6]:
+        copy.wait()
 
     counts_row = counts[...].astype(F32)
     row_a, row_b = iota((rows, rows), 0), iota((rows, rows), 1)
@@ -92,41 +103,60 @@
     placed = jnp.where(page_at == page_of, 1.0, 0.0).astype(BF16)
     limit = dot(held.astype(BF16), placed)
     visible = (iota((rows, tokens), 1) % PAGE).astype(F32) < limit
+    copies[6].wait()
+    copies[7].wait()
+    squares = jnp.zeros((rows, HD), F32)
     penalty = jnp.where(visible, 0.0, NEG)[None]
     own_penalty = jnp.where(eye(rows), 0.0, NEG)[None]
-
-    squares = jnp.zeros((rows, HD), F32)
-    for head in range(heads_here):
+    def qk(head):
         base = head * group * HD
         query = jnp.concatenate(
             [queries[:, base + g * HD : base + (g + 1) * HD] for g in range(group)], axis=0
         )
-        key_at, value_at = 2 * head * HD, (2 * head + 1) * HD
-        scores = dot_t(query, pool[:, key_at : key_at + HD]) * SCORE_SCALE
-        own = dot_t(query, new_kv[:, key_at : key_at + HD]) * SCORE_SCALE
+        keys = slice(2 * head * HD, (2 * head + 1) * HD)
+        scores = dot_t(query, pool[:, keys])
+        own = dot_t(query, new_kv[:, keys])
         scores = (scores.reshape(group, rows, tokens) + penalty).reshape(group * rows, tokens)
         own = (own.reshape(group, rows, rows) + own_penalty).reshape(group * rows, rows)
+        return scores, own
+    def soft(so):
+        scores, own = so
         top = jnp.maximum(
             jnp.max(scores, axis=1, keepdims=True), jnp.max(own, axis=1, keepdims=True)
         )
-        weights = jnp.exp(scores - top)
-        own_weights = jnp.exp(own - top)
+        weights = jnp.exp((scores - top) * SCORE_SCALE)
+        own_weights = jnp.exp((own - top) * SCORE_SCALE)
         total = jnp.sum(weights, axis=1, keepdims=True) + jnp.sum(own_weights, axis=1, keepdims=True)
         inverse = 1.0 / total
-        mixed = dot((weights * inverse).astype(BF16), pool[:, value_at : value_at + HD])
-        mixed = mixed + dot((own_weights * inverse).astype(BF16), new_kv[:, value_at : value_at + HD])
+        return (weights * inverse).astype(BF16), (own_weights * inverse).astype(BF16)
+    def pv(head, w, squares):
+        base = head * group * HD
+        values = slice((2 * head + 1) * HD, (2 * head + 2) * HD)
+        mixed = dot(w[0], pool[:, values])
+        mixed = mixed + dot(w[1], new_kv[:, values])
         for g in range(group):
             columns = slice(base + g * HD, base + (g + 1) * HD)
             part = residual[:, columns].astype(F32) + mixed[g * rows : (g + 1) * rows]
             hidden[:, columns] = part
             squares = squares + part * part
+        return squares
+    s = []
+    for head in range(heads_here):
+        if head % 2 == 0:
+            copies[10 + head].wait()
+            copies[11 + head].wait()
+        s.append(qk(head))
+    copies[8].wait()
+    copies[9].wait()
+    for head in range(heads_here):
+        squares = pv(head, soft(s[head]), squares)
     square_row = to_row(jnp.sum(squares, axis=1, keepdims=True), rows)
 
     scaled = (hidden[...] * gain[...]).astype(BF16)
     lows, mixes = [], []
     for expert in range(hosted):
-        member = members(routes[...], expert)
-        member_row = to_row(member, rows)
+        member_row = members(routes[...], expert)
+        member = to_column(member_row, rows)
         rank = jnp.sum(jnp.where(row_a <= row_b, member, 0.0), axis=0, keepdims=True) - 1.0
         rank = jnp.where(member_row > 0.0, rank, -2.0)
         lows.append(rank == iota((LO, rows), 0).astype(F32))
@@ -137,6 +167,7 @@
         stacked = jnp.concatenate(maps, axis=0).astype(BF16)
         picked.append(dot(stacked, scaled[:, part * QUARTER : (part + 1) * QUARTER]))
     lane = iota((LO, LANES), 1)
+    by_expert = []
     for expert in range(hosted):
         low_at, mix_at = expert * LO, (hosted + expert) * LO
         low_sum = jnp.sum(jnp.where(lows[expert], square_row, 0.0), axis=1, keepdims=True)
@@ -145,12 +176,14 @@
         extra = jnp.zeros((LO, LANES), F32)
         for at, piece in enumerate(split_three(low_sum) + split_three(mix_sum)):
             extra = jnp.where(lane == at, piece, extra)
-        for part in range(2):
-            columns = slice(part * QUARTER, (part + 1) * QUARTER)
-            slots[expert, :, columns] = picked[part][low_at : low_at + LO].astype(BF16)
+        low_rows = [picked[part][low_at : low_at + LO] for part in range(2)]
         mixed_rows = picked[0][mix_at : mix_at + LO] + picked[1][mix_at : mix_at + LO]
-        slots[expert, :, HALF:SLOT_COLS] = mixed_rows.astype(BF16)
-        slots[expert, :, SLOT_COLS:] = extra.astype(BF16)
+        by_expert.append(jnp.concatenate(low_rows + [mixed_rows, extra], axis=1))
+    first_half = lax.axis_index("expert") == 0
+    extra_at = SLOT_COLS + LANES
+    mine = jnp.where(first_half, by_expert[0], by_expert[1])
+    kept[:, :extra_at] = jnp.concatenate([mine, jnp.zeros_like(mine)], axis=0).astype(BF16)
+    other[...] = jnp.where(first_half, by_expert[1], by_expert[0]).astype(BF16)
 
     entries = mig_pages.shape[1]
     page_width = pool.shape[1]
@@ -158,40 +191,38 @@
     notes = jnp.where(lane == entries, lax.axis_index("attn").astype(F32), 0.0)
     for entry in range(entries):
         start = pl.multiple_of(mig_pages[0, entry] * PAGE, PAGE)
-        moved[:, entry * page_width : (entry + 1) * page_width] = pool[pl.ds(start, PAGE), :]
+        at = extra_at + entry * page_width
+        kept[:, at : at + page_width] = pool[pl.ds(start, PAGE), :]
         notes = jnp.where(lane == entry, mig_dest[0, entry].astype(F32), notes)
-    moved[:, entries * page_width :] = notes.astype(BF16)
-
-
-def pack_kernel(mine, theirs, moved, message):
+    kept[:, extra_at + entries * page_width :] = notes.astype(BF16)
+
+
+def pack_kernel(kept, theirs, message):
     lane = iota((LO, LANES), 1)
-    extra = mine[:, SLOT_COLS:].astype(F32) + theirs[:, SLOT_COLS:].astype(F32)
+    mine = kept[:, : SLOT_COLS + LANES].astype(F32)[:LO]
+    extra = mine[:, SLOT_COLS:] + theirs[:, SLOT_COLS:].astype(F32)
     low_scale = lax.rsqrt(jnp.sum(jnp.where(lane < 3, extra, 0.0), axis=1, keepdims=True) / D + EPSILON)
     mix_sum = jnp.sum(jnp.where((lane >= 3) & (lane < 6), extra, 0.0), axis=1, keepdims=True)
     mix_scale = lax.rsqrt(mix_sum / D + EPSILON)
     first_half = lax.axis_index("expert") == 0
     for columns, scale in ((slice(0, HALF), low_scale), (slice(HALF, SLOT_COLS), mix_scale)):
-        a = mine[:, columns].astype(F32) * scale
+        a = mine[:, columns] * scale
         b = theirs[:, columns].astype(F32) * scale
         both = jnp.concatenate([jnp.where(first_half, a, b), jnp.where(first_half, b, a)], axis=0)
         message[:, columns] = both.astype(BF16)
-    message[:, SLOT_COLS:] = moved[...]
+    message[:, SLOT_COLS:] = kept[:, SLOT_COLS + LANES :]
+
+
+def fetch_kernel(source, out, sem):
+    copy = pltpu.make_async_copy(source, out, sem)
+    copy.start()
+    copy.wait()
 
 
 def ffn_kernel(n, cut, *refs):
-    blocks, (gate_hbm, up_hbm, down_hbm) = refs[: n + 1], refs[n + 1 : n + 4]
+    blocks, (gate, up, down) = refs[: n + 1], refs[n + 1 : n + 4]
     outs = refs[n + 4 : 2 * n + 4]
-    low_rows, mix_rows, gate, up, down, gate_sum, up_sum, sems = refs[2 * n + 4 :]
-    copies = []
-    for q in range(4):
-        part = pl.ds(q * QUARTER, QUARTER)
-        copies.append(pltpu.make_async_copy(gate_hbm.at[part, :], gate.at[part, :], sems.at[0, q]))
-        copies.append(pltpu.make_async_copy(up_hbm.at[part, :], up.at[part, :], sems.at[1, q]))
-    for q in range(4):
-        part = pl.ds(q * QUARTER, QUARTER)
-        copies.append(pltpu.make_async_copy(down_hbm.at[:, part], down.at[:, part], sems.at[2, q]))
-    for copy in copies:
-        copy.start()
+    low_rows, mix_rows, gate_sum, up_sum = refs[2 * n + 4 :]
     for j in range(n - 1):
         low_rows[16 * j : 16 * j + 16, :] = blocks[j][:, :HALF]
         mix_rows[16 * j : 16 * j + 16, :] = blocks[j][:, HALF:SLOT_COLS]
@@ -204,8 +235,6 @@
     span = 16 * size
     row = iota((span, 1), 0) % 16
     for q in range(4):
-        copies[2 * q].wait()
-        copies[2 * q + 1].wait()
         low_here, mix_here = (row // 8) == q // 2, (row // 4) == q
         part = slice(q * QUARTER, (q + 1) * QUARTER)
         within = slice((q % 2) * QUARTER, (q % 2 + 1) * QUARTER)
@@ -222,8 +251,6 @@
                     total[0, at : at + span, :] += low
                     total[1, at : at + span, :] += mix
 
-    for copy in copies[8:]:
-        copy.wait()
     lower = iota((8 * size, 1), 0) % 8 < 4
     width = gate.shape[1]
 
@@ -254,7 +281,7 @@
 
 
 def arrive_kernel(n, cut, page_width, *refs):
-    blocks, arrived, board, board_smem, sem = refs[: n + 1], refs[n + 1], refs[n + 2], refs[n + 3], refs[n + 4]
+    blocks, (arrived, board, board_smem, sem) = refs[: n + 1], refs[n + 1 :]
     entries = arrived.shape[0]
     notes_at = SLOT_COLS + entries * page_width
     heads = [block[:, notes_at:].astype(F32)[0:1] for block in blocks[: n - 1]]
@@ -277,7 +304,7 @@
             slot = board_smem[j, entry]
             at = SLOT_COLS + entry * page_width - shift
 
-            @pl.when(slot >= 0)
+            @pl.when((slot >= 0) & (slot < entries))
             def _():
                 arrived[slot] = block[:, at : at + page_width]
 
@@ -299,9 +326,10 @@
     terms = [[], []]
     for expert in range(hosted):
         member = members(routes[...], expert)
-        share = jnp.sum(jnp.where(routes[...] == expert, gates[...], 0.0), axis=1, keepdims=True)
-        rank = jnp.sum(jnp.where(row_b <= row_a, to_row(member, rows), 0.0), axis=1, keepdims=True) - 1.0
-        rank = jnp.where(member > 0.0, rank, -2.0)
+        share = jnp.sum(jnp.where(routes[...] == expert, gates[...], 0.0), axis=0, keepdims=True)
+        share = to_column(share, rows)
+        rank = jnp.sum(jnp.where(row_b <= row_a, member, 0.0), axis=1, keepdims=True) - 1.0
+        rank = jnp.where(to_column(member, rows) > 0.0, rank, -2.0)
         low = jnp.where(rank == iota((rows, LO), 1).astype(F32), 1.0, 0.0).astype(BF16)
         for part in range(2):
             columns = slice(part * QUARTER, (part + 1) * QUARTER)
@@ -313,7 +341,7 @@
         layer_out[:, columns] = (hidden[:, columns] + (terms[part][0] + terms[part][1])).astype(BF16)
 
 
-def call(kernel, outs, in_specs, args, scratch=(), flops=0, bytes_accessed=0, vmem=32 << 20):
+def call(kernel, outs, in_specs, args, scratch=(), flops=0, bytes_accessed=0, vmem=16 << 20):
     many = isinstance(outs, (list, tuple))
     return pl.pallas_call(
         kernel,
@@ -328,6 +356,17 @@
 
 def ring_order(n):
     return [0, 2, 4, 6, 7, 5, 3, 1] if n == 8 else list(range(n))
+
+
+def fetch_weight(shape, weight):
+    return call(
+        fetch_kernel,
+        shape(weight.shape, BF16),
+        [HBM],
+        (weight,),
+        scratch=(pltpu.SemaphoreType.DMA,),
+        bytes_accessed=6_400_000,
+    )
 
 
 def add(a, b):
@@ -364,53 +403,62 @@
     shape = jax.ShapeDtypeStruct
 
     moved_cols = entries * page_width + LANES
-    hidden, slots, moved = call(
+    sources = (
+        page_counts,
+        tail_tokens.reshape(1, -1),
+        page_order,
+        routes.T,
+        mig_pages,
+        mig_dest,
+        queries,
+        new_kv,
+        residual,
+        norm_gain.reshape(1, -1),
+        pool,
+    )
+    spaces = [pltpu.VMEM] * 4 + [pltpu.SMEM] * 2 + [pltpu.VMEM] * 5
+    hidden, kept, other = call(
         functools.partial(attend_kernel, hosted),
         [
             shape((rows, width), F32),
-            shape((hosted, LO, SLOT_COLS + LANES), BF16),
-            shape((PAGE, moved_cols), BF16),
+            shape((2 * LO, SLOT_COLS + LANES + moved_cols), BF16),
+            shape((LO, SLOT_COLS + LANES), BF16),
         ],
-        [VMEM] * 9 + [SMEM] * 2,
-        (
-            queries,
-            new_kv,
-            pool,
-            page_counts,
-            tail_tokens.reshape(1, -1),
-            page_order,
-            residual,
-            norm_gain.reshape(1, -1),
-            routes,
-            mig_pages,
-            mig_dest,
-        ),
+        [HBM] * len(sources),
+        sources,
+        scratch=[space(x.shape, x.dtype) for space, x in zip(spaces, sources)]
+        + [pltpu.SemaphoreType.DMA((len(sources) + page_width // (2 * HD),))],
         flops=500_000_000,
         bytes_accessed=3_500_000,
-    )
-
-    own_expert = lax.axis_index("expert")
-    mine = lax.dynamic_index_in_dim(slots, own_expert, 0, keepdims=False)
-    other = lax.dynamic_index_in_dim(slots, 1 - own_expert, 0, keepdims=False)
+        vmem=60 << 20,
+    )
     theirs = lax.ppermute(other, "expert", swap)
-    cols = SLOT_COLS + moved_cols
     message = call(
         pack_kernel,
-        shape((2 * LO, cols), BF16),
-        [VMEM] * 3,
-        (mine, theirs, moved),
+        shape((2 * LO, SLOT_COLS + moved_cols), BF16),
+        [VMEM] * 2,
+        (kept, theirs),
         flops=500_000,
         bytes_accessed=500_000,
     )
 
     far = n // 2
     cut = HALF + 3 * LANES
+    tie = lax.optimization_barrier
+    fetch = functools.partial(fetch_weight, shape)
     from_left, from_right = [message], [message]
-    for _ in range(far - 1):
-        from_left.append(lax.ppermute(from_left[-1], "attn", right))
-        from_right.append(lax.ppermute(from_right[-1], "attn", left))
-    last_a = lax.ppermute(from_left[-1][:, :cut], "attn", right)
-    last_b = lax.ppermute(from_right[-1][:, cut:], "attn", left)
+    weights, stored = [], [w_gate[0], w_up[0], w_down[0]]
+    for step in range(far):
+        a, b = from_left[-1], from_right[-1]
+        if step == far - 1:
+            a, b = a[:, :cut], b[:, cut:]
+        a, b = lax.ppermute(a, "attn", right), lax.ppermute(b, "attn", left)
+        if step < len(stored):
+            weights.append(fetch(stored[step]))
+            a, weights[-1] = tie((a, weights[-1]))
+        from_left.append(a)
+        from_right.append(b)
+    last_a, last_b = from_left.pop(), from_right.pop()
     blocks = [message] + from_left[1:] + from_right[1:] + [last_a, last_b]
 
     ff = w_gate.shape[2]
@@ -418,22 +466,23 @@
     outs = call(
         functools.partial(ffn_kernel, n, cut),
         [shape((2 * LO, SLOT_COLS), BF16)] * n,
-        [VMEM] * (n + 1) + [ANY] * 3,
-        (*blocks, w_gate[0], w_up[0], w_down[0]),
+        [VMEM] * (n + 4),
+        (*blocks, *weights),
         scratch=(
             pltpu.VMEM((size, HALF), BF16),
             pltpu.VMEM((size, QUARTER), BF16),
-            pltpu.VMEM((D, ff), BF16),
-            pltpu.VMEM((D, ff), BF16),
-            pltpu.VMEM((ff, D), BF16),
             pltpu.VMEM((2, size, ff), F32),
             pltpu.VMEM((2, size, ff), F32),
-            pltpu.SemaphoreType.DMA((3, 4)),
         ),
         flops=2_000_000_000,
         bytes_accessed=12_000_000,
-        vmem=48 << 20,
-    )
+    )
+
+    to_left = {k: outs[k] for k in range(1, far)}
+    to_right = {k: outs[far - 1 + k] for k in range(1, far)}
+    split = SLOT_COLS // 2
+    going_right = lax.ppermute(outs[n - 1][:, :split], "attn", right)
+    going_left = lax.ppermute(outs[n - 1][:, split:], "attn", left)
     arrived = call(
         functools.partial(arrive_kernel, n, cut, page_width),
         shape((entries, PAGE, page_width), BF16),
@@ -447,12 +496,7 @@
         flops=100_000,
         bytes_accessed=2_000_000,
     )
-
-    to_left = {k: outs[k] for k in range(1, far)}
-    to_right = {k: outs[far - 1 + k] for k in range(1, far)}
-    split = SLOT_COLS // 2
-    going_right = lax.ppermute(outs[n - 1][:, :split], "attn", right)
-    going_left = lax.ppermute(outs[n - 1][:, split:], "attn", left)
+    going_right, arrived = tie((going_right, arrived))
     for k in range(far - 1, 0, -1):
         if k == far - 1:
             send_right = jnp.concatenate([add(to_right[k][:, :split], going_right), to_right[k][:, split:]], axis=1)
@@ -474,7 +518,7 @@
         functools.partial(combine_kernel, hosted),
         shape((rows, width), BF16),
         [VMEM] * 5,
-        (hidden, kept, returned, routes, route_gates),
+        (hidden, kept, returned, routes.T, route_gates.T),
         flops=20_000_000,
         bytes_accessed=800_000,
     )

time: 72.4 us -> 63.2 us (0.87)
  local copies, waits for them, and re-layouts: 9.52 us -> 1 us
    unnamed x58 -> x14, local copies, waits for them, and re-layouts: 9.45 us -> 0.96 us
    ppermute x3, waiting for transfers between devices: 1.21 us -> 9.05 us  [per_device(): going_right = lax.ppermute(send_right, 'attn', right)]
    ppermute x3, waiting for transfers between devices: 9.04 us -> 1.69 us  [per_device(): going_left = lax.ppermute(send_left, 'attn', left)]
    ppermute x1, waiting for transfers between devices: 2.34 us -> 0.01 us  [per_device(): going_left = lax.ppermute(outs[n - 1][:, split:], 'attn', left)]
    ppermute x3, starting transfers between devices: 3.29 us -> 1.5 us  [per_device(): going_left = lax.ppermute(send_left, 'attn', left)]
    ppermute x3, starting transfers between devices: 3.11 us -> 4.89 us  [per_device(): going_right = lax.ppermute(send_right, 'attn', right)]
    ppermute x1, waiting for transfers between devices: 0.01 us -> 1.25 us  [per_device(): returned = lax.ppermute(other_half, 'expert', swap)]
    pallas_call x6 -> x9, Pallas kernels: 11.1 us -> 11.1 us  [call(): pl.pallas_call(kernel, out_shape=outs, in_specs=in_specs, out_specs=[VMEM...]
  transfers between devices with their start and end apart: 18 -> 18, of which waited for: 10 -> 11; matrix products, arithmetic and copies ran while one was open for 0% -> 0% of each run, Pallas kernels for 2% -> 4%
where the time goes in v2:
time: 63.2 us; the launch traced here: 63 us
  waiting for transfers between devices  31.7 us (50%)
  starting transfers between devices  18.3 us (29%)
  Pallas kernels  11.1 us (18%)
  local copies, waits for them, and re-layouts  1 us (2%)
  between operations  0.81 us (1%)
    ppermute x8, waiting for transfers between devices, per_device(): a, b = (lax.ppermute(a, 'attn', right), lax.ppermute(b, 'attn', left))  17.8 us
    pallas_call x9, Pallas kernels, call(): pl.pallas_call(kernel, out_shape=outs, in_specs=in_specs, out_specs=[VMEM...  11.1 us
    ppermute x8, starting transfers between devices, per_device(): a, b = (lax.ppermute(a, 'attn', right), lax.ppermute(b, 'attn', left))  9.16 us
    ppermute x3, waiting for transfers between devices, per_device(): going_right = lax.ppermute(send_right, 'attn', right)  9.05 us
    ppermute x3, starting transfers between devices, per_device(): going_right = lax.ppermute(send_right, 'attn', right)  4.89 us
    ppermute x3, waiting for transfers between devices, per_device(): going_left = lax.ppermute(send_left, 'attn', left)  1.69 us
    ppermute x1, starting transfers between devices, per_device(): going_right = lax.ppermute(outs[n - 1][:, :split], 'attn', right)  1.62 us
    ppermute x3, starting transfers between devices, per_device(): going_left = lax.ppermute(send_left, 'attn', left)  1.5 us
  transfers between devices with their start and end apart: 18, of which 11 were waited for; matrix products, arithmetic and copies ran while one was open for 0% of the time, Pallas kernels for 4%

profile of v2, /device:TPU:0, one launch (start us, length us, event | category | flops | bytes accessed | tf_op | source)
XLA Modules:
  0.0 63.0 jit_solution(18279818531306255294)
XLA Ops:
  0.6 5.1 %shard_map.158 = (f32[32,3072]{1,0:T(8,128)}, bf16[16,6912]{1,0:T(8,128)(2,1)}, bf16[8,4736]{1,0:T(8,128)(2,1)}) custom-call(s32[1,32]{1,0:T(1,128)} %refs_0_.1, s32[1,32]{1,0:T(1,128)} %bitcast.16, s32[1,72]{1,0:T(1,128)} %refs_2_.1, s32[2,32]{1,0:T(2,128)} %bitcast.11, s32[1,2]{1,0:T(1,128)} %refs_4_.1, s32[1,2]{1,0:T(1,128)} %refs_5_.1, ...), custom_call_target="tpu_custom_call" | custom-call | flops 500000000 | bytes 3500000 | tf_op jit(solution)/shard_map/pallas_call | solution.py:346
  5.8 0.5 collective-permute-start
  6.3 1.1 %collective-permute-done.theirs = bf16[8,4736]{1,0:T(8,128)(2,1)S(1)} collective-permute-done((bf16[8,4736]{1,0:T(8,128)(2,1)}, bf16[8,4736]{1,0:T(8,128)(2,1)S(1)}, u32[]{:S(2)}, u32[]{:S(2)}) %collective-permute-start) | collective-permute-done | bytes 75808 | tf_op jit(solution)/shard_map/ppermute | solution.py:435
  7.4 0.9 %copy-done.4 = bf16[16,6912]{1,0:T(8,128)(2,1)S(1)} copy-done((bf16[16,6912]{1,0:T(8,128)(2,1)S(1)}, bf16[16,6912]{1,0:T(8,128)(2,1)}, u32[]{:S(2)}) %copy-start.4) | copy-done | bytes 221208
  8.4 0.1 shard_map.159.refs_0_
  8.5 3.0 %collective-permute-start.1 = (bf16[16,6784]{1,0:T(8,128)(2,1)S(1)}, bf16[16,6784]{1,0:T(8,128)(2,1)S(1)}, u32[]{:S(2)}, u32[]{:S(2)}) collective-permute-start(bf16[16,6784]{1,0:T(8,128)(2,1)S(1)} %shard_map.159.refs_0_), channel_id=1, source_target_pairs={{0,4},{4,8},{8,12},{12,14},{14,10},{10,6},{6,2},{2,0},{1,5},{5,9},... | collective-permute-start | bytes 651272 | tf_op jit(solution)/shard_map/ppermute | solution.py:455
  11.5 0.0 collective-permute-start.4
  11.5 0.2 shard_map.160.refs_9_
  11.7 5.4 %collective-permute-done.1.refs_1_ = bf16[16,6784]{1,0:T(8,128)(2,1)S(1)} collective-permute-done((bf16[16,6784]{1,0:T(8,128)(2,1)S(1)}, bf16[16,6784]{1,0:T(8,128)(2,1)S(1)}, u32[]{:S(2)}, u32[]{:S(2)}) %collective-permute-start.1) | collective-permute-done | bytes 217120 | tf_op jit(solution)/shard_map/ppermute | solution.py:455
  17.1 1.8 %collective-permute-start.2 = (bf16[16,6784]{1,0:T(8,128)(2,1)S(1)}, bf16[16,6784]{1,0:T(8,128)(2,1)S(1)}, u32[]{:S(2)}, u32[]{:S(2)}) collective-permute-start(bf16[16,6784]{1,0:T(8,128)(2,1)S(1)} %collective-permute-done.1.refs_1_), channel_id=1, source_target_pairs={{0,4},{4,8},{8,12},{12,14},{14,10},{10,6},{6,2},{2,0},{1,5},{5,9},... | collective-permute-start | bytes 651272 | tf_op jit(solution)/shard_map/ppermute | solution.py:455
  18.9 0.0 collective-permute-done.4.refs_4_
  18.9 0.2 collective-permute-start.5
  19.1 0.2 shard_map.161.refs_10_
  19.3 4.6 %collective-permute-done.2.refs_2_ = bf16[16,6784]{1,0:T(8,128)(2,1)S(1)} collective-permute-done((bf16[16,6784]{1,0:T(8,128)(2,1)S(1)}, bf16[16,6784]{1,0:T(8,128)(2,1)S(1)}, u32[]{:S(2)}, u32[]{:S(2)}) %collective-permute-start.2) | collective-permute-done | bytes 217120 | tf_op jit(solution)/shard_map/ppermute | solution.py:455
  24.0 1.5 %collective-permute-start.3 = (bf16[16,6784]{1,0:T(8,128)(2,1)S(1)}, bf16[16,6784]{1,0:T(8,128)(2,1)S(1)}, u32[]{:S(2)}, u32[]{:S(2)}) collective-permute-start(bf16[16,6784]{1,0:T(8,128)(2,1)S(1)} %collective-permute-done.2.refs_2_), channel_id=1, source_target_pairs={{0,4},{4,8},{8,12},{12,14},{14,10},{10,6},{6,2},{2,0},{1,5},{5,9},... | collective-permute-start | bytes 651272 | tf_op jit(solution)/shard_map/ppermute | solution.py:455
  25.5 0.0 collective-permute-done.5.refs_5_
  25.5 0.5 collective-permute-start.6
  26.0 0.2 shard_map.162.refs_11_
  26.2 3.7 %collective-permute-done.3.refs_3_ = bf16[16,6784]{1,0:T(8,128)(2,1)S(1)} collective-permute-done((bf16[16,6784]{1,0:T(8,128)(2,1)S(1)}, bf16[16,6784]{1,0:T(8,128)(2,1)S(1)}, u32[]{:S(2)}, u32[]{:S(2)}) %collective-permute-start.3) | collective-permute-done | bytes 217120 | tf_op jit(solution)/shard_map/ppermute | solution.py:455
  30.0 1.5 %collective-permute-start.7 = (bf16[16,3456]{1,0:T(8,128)(2,1)S(1)}, bf16[16,3456]{1,0:T(8,128)(2,1)S(1)}, u32[]{:S(2)}, u32[]{:S(2)}) collective-permute-start(bf16[16,3456]{1,0:T(8,128)(2,1)S(1)} %slice.24), channel_id=1, source_target_pairs={{0,4},{4,8},{8,12},{12,14},{14,10},{10,6},{6,2},{2,0},{1,5},{5,9},... | collective-permute-start | bytes 331784 | tf_op jit(solution)/shard_map/ppermute | solution.py:455
  31.4 0.0 collective-permute-done.6.refs_6_
  31.4 0.7 %collective-permute-start.8 = (bf16[16,3328]{1,0:T(8,128)(2,1)S(1)}, bf16[16,3328]{1,0:T(8,128)(2,1)S(1)}, u32[]{:S(2)}, u32[]{:S(2)}) collective-permute-start(bf16[16,3328]{1,0:T(8,128)(2,1)S(1)} %slice.32), channel_id=1, source_target_pairs={{4,0},{8,4},{12,8},{14,12},{10,14},{6,10},{2,6},{0,2},{5,1},{9,5},... | collective-permute-start | bytes 319496 | tf_op jit(solution)/shard_map/ppermute | solution.py:455
  32.1 4.1 %collective-permute-done.8.refs_8_ = bf16[16,3328]{1,0:T(8,128)(2,1)S(1)} collective-permute-done((bf16[16,3328]{1,0:T(8,128)(2,1)S(1)}, bf16[16,3328]{1,0:T(8,128)(2,1)S(1)}, u32[]{:S(2)}, u32[]{:S(2)}) %collective-permute-start.8) | collective-permute-done | bytes 106528 | tf_op jit(solution)/shard_map/ppermute | solution.py:455
  36.2 0.0 collective-permute-done.7.refs_7_
  36.2 2.4 %shard_map.163 = (bf16[16,4608]{1,0:T(8,128)(2,1)S(1)}, bf16[16,4608]{1,0:T(8,128)(2,1)S(1)}, bf16[16,4608]{1,0:T(8,128)(2,1)S(1)}, bf16[16,4608]{1,0:T(8,128)(2...) custom-call(bf16[16,6784]{1,0:T(8,128)(2,1)S(1)} %shard_map.159.refs, ...), custom_call_target="tpu_custom_call" | custom-call | flops 2000000000 | bytes 12000000 | tf_op jit(solution)/shard_map/pallas_call | solution.py:346
  38.6 0.0 copy-start.5
  38.6 0.0 copy-start.6
  38.7 1.6 %collective-permute-start.9 = (bf16[16,2304]{1,0:T(8,128)(2,1)S(1)}, bf16[16,2304]{1,0:T(8,128)(2,1)S(1)}, u32[]{:S(2)}, u32[]{:S(2)}) collective-permute-start(bf16[16,2304]{1,0:T(8,128)(2,1)S(1)} %get-tuple-element.45), channel_id=1, source_target_pairs={{0,4},{4,8},{8,12},{12,14},{14,10},{10,6},{6,2},{2,0},{1,5},{5,9},... | collective-permute-start | bytes 221192 | tf_op jit(solution)/shard_map/ppermute | solution.py:484
  40.3 0.5 collective-permute-start.13
  40.8 1.6 %shard_map.164 = bf16[2,16,1024]{2,1,0:T(8,128)(2,1)} custom-call(bf16[16,6784]{1,0:T(8,128)(2,1)S(1)} %shard_map.159.refs_0_, bf16[16,6784]{1,0:T(8,128)(2,1)S(1)} %collective-permute-done.1.refs_1_, bf16[16,6784]{1,0:T(8,128)(2,1)S(1)} %collective-permute-done.2.refs_2_, bf16[16,6784]{1,0:T(8,128)(2,1)S(1)} %collective-permute-done.3.refs_3_, ...), custom_call_target="tpu_custom_call" | custom-call | flops 100000 | bytes 2000000 | tf_op jit(solution)/shard_map/pallas_call | solution.py:346
  42.4 0.7 %collective-permute-done.9 = bf16[16,2304]{1,0:T(8,128)(2,1)S(1)} collective-permute-done((bf16[16,2304]{1,0:T(8,128)(2,1)S(1)}, bf16[16,2304]{1,0:T(8,128)(2,1)S(1)}, u32[]{:S(2)}, u32[]{:S(2)}) %collective-permute-start.9) | collective-permute-done | bytes 73760 | tf_op jit(solution)/shard_map/ppermute | solution.py:484
  43.2 1.6 %collective-permute-start.10 = (bf16[16,4608]{1,0:T(8,128)(2,1)S(1)}, bf16[16,4608]{1,0:T(8,128)(2,1)S(1)}, u32[]{:S(2)}, u32[]{:S(2)}) collective-permute-start(bf16[16,4608]{1,0:T(8,128)(2,1)S(1)} %pad_maximum_fusion), channel_id=1, source_target_pairs={{0,4},{4,8},{8,12},{12,14},{14,10},{10,6},{6,2},{2,0},{1,5},{5,9},... | collective-permute-start | bytes 442376 | tf_op jit(solution)/shard_map/ppermute | solution.py:506
  44.8 0.0 collective-permute-done.13
  44.8 0.5 collective-permute-start.14
  45.3 3.0 %collective-permute-done.10 = bf16[16,4608]{1,0:T(8,128)(2,1)S(1)} collective-permute-done((bf16[16,4608]{1,0:T(8,128)(2,1)S(1)}, bf16[16,4608]{1,0:T(8,128)(2,1)S(1)}, u32[]{:S(2)}, u32[]{:S(2)}) %collective-permute-start.10) | collective-permute-done | bytes 147488 | tf_op jit(solution)/shard_map/ppermute | solution.py:506
  48.4 1.6 %collective-permute-start.11 = (bf16[16,4608]{1,0:T(8,128)(2,1)S(1)}, bf16[16,4608]{1,0:T(8,128)(2,1)S(1)}, u32[]{:S(2)}, u32[]{:S(2)}) collective-permute-start(bf16[16,4608]{1,0:T(8,128)(2,1)S(1)} %add_convert_fusion.3), channel_id=1, source_target_pairs={{0,4},{4,8},{8,12},{12,14},{14,10},{10,6},{6,2},{2,0},{1,5},{5,9},... | collective-permute-start | bytes 442376 | tf_op jit(solution)/shard_map/ppermute | solution.py:506
  50.0 0.0 collective-permute-done.14
  50.1 0.5 collective-permute-start.15
  50.6 3.0 %collective-permute-done.11 = bf16[16,4608]{1,0:T(8,128)(2,1)S(1)} collective-permute-done((bf16[16,4608]{1,0:T(8,128)(2,1)S(1)}, bf16[16,4608]{1,0:T(8,128)(2,1)S(1)}, u32[]{:S(2)}, u32[]{:S(2)}) %collective-permute-start.11) | collective-permute-done | bytes 147488 | tf_op jit(solution)/shard_map/ppermute | solution.py:506
  53.6 1.6 %collective-permute-start.12 = (bf16[16,4608]{1,0:T(8,128)(2,1)S(1)}, bf16[16,4608]{1,0:T(8,128)(2,1)S(1)}, u32[]{:S(2)}, u32[]{:S(2)}) collective-permute-start(bf16[16,4608]{1,0:T(8,128)(2,1)S(1)} %add_convert_fusion.2), channel_id=1, source_target_pairs={{0,4},{4,8},{8,12},{12,14},{14,10},{10,6},{6,2},{2,0},{1,5},{5,9},... | collective-permute-start | bytes 442376 | tf_op jit(solution)/shard_map/ppermute | solution.py:506
  55.3 0.0 collective-permute-done.15
  55.3 0.5 collective-permute-start.16
  55.8 3.0 %collective-permute-done.12.from_left = bf16[16,4608]{1,0:T(8,128)(2,1)S(1)} collective-permute-done((bf16[16,4608]{1,0:T(8,128)(2,1)S(1)}, bf16[16,4608]{1,0:T(8,128)(2,1)S(1)}, u32[]{:S(2)}, u32[]{:S(2)}) %collective-permute-start.12) | collective-permute-done | bytes 147488 | tf_op jit(solution)/shard_map/ppermute | solution.py:506
  58.8 1.7 %collective-permute-done.16.from_right = bf16[16,4608]{1,0:T(8,128)(2,1)S(1)} collective-permute-done((bf16[16,4608]{1,0:T(8,128)(2,1)S(1)}, bf16[16,4608]{1,0:T(8,128)(2,1)S(1)}, u32[]{:S(2)}, u32[]{:S(2)}) %collective-permute-start.16) | collective-permute-done | bytes 147488 | tf_op jit(solution)/shard_map/ppermute | solution.py:507
  60.5 0.1 shard_map.165
  60.6 0.1 collective-permute-start.17
  60.7 1.3 %collective-permute-done.17.theirs = bf16[8,4608]{1,0:T(8,128)(2,1)S(1)} collective-permute-done((bf16[8,4608]{1,0:T(8,128)(2,1)S(1)}, bf16[8,4608]{1,0:T(8,128)(2,1)S(1)}, u32[]{:S(2)}, u32[]{:S(2)}) %collective-permute-start.17) | collective-permute-done | bytes 73760 | tf_op jit(solution)/shard_map/ppermute | solution.py:516
  61.9 1.1 %shard_map.166 = bf16[32,3072]{1,0:T(8,128)(2,1)} custom-call(f32[32,3072]{1,0:T(8,128)S(1)} %copy-done.3, bf16[8,4608]{1,0:T(8,128)(2,1)S(1)} %get-tuple-element.41.mine, bf16[8,4608]{1,0:T(8,128)(2,1)S(1)} %collective-permute-done.17.theirs, s32[2,32]{1,0:T(2,128)S(1)} %bitcast.12, f32[2,32]{1,0:T(2,128)S(1)} %bitcast.13), custom_call_target="tpu_custom_call" | custom-call | flops 20000000 | bytes 800000 | tf_op jit(solution)/shard_map/pallas_call | solution.py:346
  (24 shorter events, 0.3 us)
Async XLA Ops:
  0.6 10.9 %copy-start = (bf16[1,6144,256]{2,1,0:T(8,128)(2,1)S(1)}, bf16[1,6144,256]{2,1,0:T(8,128)(2,1)}, u32[]{:S(2)}) copy-start(bf16[1,6144,256]{2,1,0:T(8,128)(2,1)} %param.25) | copy-start | bytes 9437188
  5.8 1.7 %collective-permute-start = (bf16[8,4736]{1,0:T(8,128)(2,1)}, bf16[8,4736]{1,0:T(8,128)(2,1)S(1)}, u32[]{:S(2)}, u32[]{:S(2)}) collective-permute-start(bf16[8,4736]{1,0:T(8,128)(2,1)} %get-tuple-element.25), channel_id=1, source_target_pairs={{0,1},{1,0},{2,3},{3,2},{4,5},{5,4},{6,7},{7,6},{8,9},{9,8},{10,11... | collective-permute-start | bytes 227336 | tf_op jit(solution)/shard_map/ppermute | solution.py:435
  7.4 0.9 %copy-start.4 = (bf16[16,6912]{1,0:T(8,128)(2,1)S(1)}, bf16[16,6912]{1,0:T(8,128)(2,1)}, u32[]{:S(2)}) copy-start(bf16[16,6912]{1,0:T(8,128)(2,1)} %get-tuple-element.24.kept) | copy-start | bytes 663556
  8.5 8.6 %collective-permute-start.1 = (bf16[16,6784]{1,0:T(8,128)(2,1)S(1)}, bf16[16,6784]{1,0:T(8,128)(2,1)S(1)}, u32[]{:S(2)}, u32[]{:S(2)}) collective-permute-start(bf16[16,6784]{1,0:T(8,128)(2,1)S(1)} %shard_map.159.refs_0_), channel_id=1, source_target_pairs={{0,4},{4,8},{8,12},{12,14},{14,10},{10,6},{6,2},{2,0},{1,5},{5,9},... | collective-permute-start | bytes 651272 | tf_op jit(solution)/shard_map/ppermute | solution.py:455
  11.5 7.4 %collective-permute-start.4 = (bf16[16,6784]{1,0:T(8,128)(2,1)S(1)}, bf16[16,6784]{1,0:T(8,128)(2,1)S(1)}, u32[]{:S(2)}, u32[]{:S(2)}) collective-permute-start(bf16[16,6784]{1,0:T(8,128)(2,1)S(1)} %shard_map.159.refs_0_), channel_id=1, source_target_pairs={{4,0},{8,4},{12,8},{14,12},{10,14},{6,10},{2,6},{0,2},{5,1},{9,5},... | collective-permute-start | bytes 651272 | tf_op jit(solution)/shard_map/ppermute | solution.py:455
  11.5 7.6 %copy-start.1 = (bf16[1,6144,256]{2,1,0:T(8,128)(2,1)S(1)}, bf16[1,6144,256]{2,1,0:T(8,128)(2,1)}, u32[]{:S(2)}) copy-start(bf16[1,6144,256]{2,1,0:T(8,128)(2,1)} %param.26) | copy-start | bytes 9437188
  17.1 6.9 %collective-permute-start.2 = (bf16[16,6784]{1,0:T(8,128)(2,1)S(1)}, bf16[16,6784]{1,0:T(8,128)(2,1)S(1)}, u32[]{:S(2)}, u32[]{:S(2)}) collective-permute-start(bf16[16,6784]{1,0:T(8,128)(2,1)S(1)} %collective-permute-done.1.refs_1_), channel_id=1, source_target_pairs={{0,4},{4,8},{8,12},{12,14},{14,10},{10,6},{6,2},{2,0},{1,5},{5,9},... | collective-permute-start | bytes 651272 | tf_op jit(solution)/shard_map/ppermute | solution.py:455
  18.9 6.6 %collective-permute-start.5 = (bf16[16,6784]{1,0:T(8,128)(2,1)S(1)}, bf16[16,6784]{1,0:T(8,128)(2,1)S(1)}, u32[]{:S(2)}, u32[]{:S(2)}) collective-permute-start(bf16[16,6784]{1,0:T(8,128)(2,1)S(1)} %collective-permute-done.4.refs_4_), channel_id=1, source_target_pairs={{4,0},{8,4},{12,8},{14,12},{10,14},{6,10},{2,6},{0,2},{5,1},{9,5},... | collective-permute-start | bytes 651272 | tf_op jit(solution)/shard_map/ppermute | solution.py:455
  19.1 6.9 %copy-start.2 = (bf16[1,256,6144]{2,1,0:T(8,128)(2,1)S(1)}, bf16[1,256,6144]{2,1,0:T(8,128)(2,1)}, u32[]{:S(2)}) copy-start(bf16[1,256,6144]{2,1,0:T(8,128)(2,1)} %param.27) | copy-start | bytes 9437188
  24.0 6.0 %collective-permute-start.3 = (bf16[16,6784]{1,0:T(8,128)(2,1)S(1)}, bf16[16,6784]{1,0:T(8,128)(2,1)S(1)}, u32[]{:S(2)}, u32[]{:S(2)}) collective-permute-start(bf16[16,6784]{1,0:T(8,128)(2,1)S(1)} %collective-permute-done.2.refs_2_), channel_id=1, source_target_pairs={{0,4},{4,8},{8,12},{12,14},{14,10},{10,6},{6,2},{2,0},{1,5},{5,9},... | collective-permute-start | bytes 651272 | tf_op jit(solution)/shard_map/ppermute | solution.py:455
  25.5 6.0 %collective-permute-start.6 = (bf16[16,6784]{1,0:T(8,128)(2,1)S(1)}, bf16[16,6784]{1,0:T(8,128)(2,1)S(1)}, u32[]{:S(2)}, u32[]{:S(2)}) collective-permute-start(bf16[16,6784]{1,0:T(8,128)(2,1)S(1)} %collective-permute-done.5.refs_5_), channel_id=1, source_target_pairs={{4,0},{8,4},{12,8},{14,12},{10,14},{6,10},{2,6},{0,2},{5,1},{9,5},... | collective-permute-start | bytes 651272 | tf_op jit(solution)/shard_map/ppermute | solution.py:455
  30.0 6.2 %collective-permute-start.7 = (bf16[16,3456]{1,0:T(8,128)(2,1)S(1)}, bf16[16,3456]{1,0:T(8,128)(2,1)S(1)}, u32[]{:S(2)}, u32[]{:S(2)}) collective-permute-start(bf16[16,3456]{1,0:T(8,128)(2,1)S(1)} %slice.24), channel_id=1, source_target_pairs={{0,4},{4,8},{8,12},{12,14},{14,10},{10,6},{6,2},{2,0},{1,5},{5,9},... | collective-permute-start | bytes 331784 | tf_op jit(solution)/shard_map/ppermute | solution.py:455
  31.4 4.8 %collective-permute-start.8 = (bf16[16,3328]{1,0:T(8,128)(2,1)S(1)}, bf16[16,3328]{1,0:T(8,128)(2,1)S(1)}, u32[]{:S(2)}, u32[]{:S(2)}) collective-permute-start(bf16[16,3328]{1,0:T(8,128)(2,1)S(1)} %slice.32), channel_id=1, source_target_pairs={{4,0},{8,4},{12,8},{14,12},{10,14},{6,10},{2,6},{0,2},{5,1},{9,5},... | collective-permute-start | bytes 319496 | tf_op jit(solution)/shard_map/ppermute | solution.py:455
  38.6 23.3 %copy-start.3 = (f32[32,3072]{1,0:T(8,128)S(1)}, f32[32,3072]{1,0:T(8,128)}, u32[]{:S(2)}) copy-start(f32[32,3072]{1,0:T(8,128)} %get-tuple-element.23.hidden) | copy-start | bytes 1179652
  38.6 23.3 %copy-start.5 = (s32[32,2]{0,1:T(2,128)S(1)}, s32[32,2]{0,1:T(2,128)}, u32[]{:S(2)}) copy-start(s32[32,2]{0,1:T(2,128)} %param.23) | copy-start | bytes 772
  38.6 23.3 %copy-start.6 = (f32[32,2]{0,1:T(2,128)S(1)}, f32[32,2]{0,1:T(2,128)}, u32[]{:S(2)}) copy-start(f32[32,2]{0,1:T(2,128)} %param.24) | copy-start | bytes 772
  38.7 4.4 %collective-permute-start.9 = (bf16[16,2304]{1,0:T(8,128)(2,1)S(1)}, bf16[16,2304]{1,0:T(8,128)(2,1)S(1)}, u32[]{:S(2)}, u32[]{:S(2)}) collective-permute-start(bf16[16,2304]{1,0:T(8,128)(2,1)S(1)} %get-tuple-element.45), channel_id=1, source_target_pairs={{0,4},{4,8},{8,12},{12,14},{14,10},{10,6},{6,2},{2,0},{1,5},{5,9},... | collective-permute-start | bytes 221192 | tf_op jit(solution)/shard_map/ppermute | solution.py:484
  40.3 4.5 %collective-permute-start.13 = (bf16[16,2304]{1,0:T(8,128)(2,1)S(1)}, bf16[16,2304]{1,0:T(8,128)(2,1)S(1)}, u32[]{:S(2)}, u32[]{:S(2)}) collective-permute-start(bf16[16,2304]{1,0:T(8,128)(2,1)S(1)} %get-tuple-element.44), channel_id=1, source_target_pairs={{4,0},{8,4},{12,8},{14,12},{10,14},{6,10},{2,6},{0,2},{5,1},{9,5},... | collective-permute-start | bytes 221192 | tf_op jit(solution)/shard_map/ppermute | solution.py:485
  43.2 5.2 %collective-permute-start.10 = (bf16[16,4608]{1,0:T(8,128)(2,1)S(1)}, bf16[16,4608]{1,0:T(8,128)(2,1)S(1)}, u32[]{:S(2)}, u32[]{:S(2)}) collective-permute-start(bf16[16,4608]{1,0:T(8,128)(2,1)S(1)} %pad_maximum_fusion), channel_id=1, source_target_pairs={{0,4},{4,8},{8,12},{12,14},{14,10},{10,6},{6,2},{2,0},{1,5},{5,9},... | collective-permute-start | bytes 442376 | tf_op jit(solution)/shard_map/ppermute | solution.py:506
  44.8 5.2 %collective-permute-start.14 = (bf16[16,4608]{1,0:T(8,128)(2,1)S(1)}, bf16[16,4608]{1,0:T(8,128)(2,1)S(1)}, u32[]{:S(2)}, u32[]{:S(2)}) collective-permute-start(bf16[16,4608]{1,0:T(8,128)(2,1)S(1)} %pad_maximum_fusion.1), channel_id=1, source_target_pairs={{4,0},{8,4},{12,8},{14,12},{10,14},{6,10},{2,6},{0,2},{5,1},{9,5},... | collective-permute-start | bytes 442376 | tf_op jit(solution)/shard_map/ppermute | solution.py:507
  48.4 5.2 %collective-permute-start.11 = (bf16[16,4608]{1,0:T(8,128)(2,1)S(1)}, bf16[16,4608]{1,0:T(8,128)(2,1)S(1)}, u32[]{:S(2)}, u32[]{:S(2)}) collective-permute-start(bf16[16,4608]{1,0:T(8,128)(2,1)S(1)} %add_convert_fusion.3), channel_id=1, source_target_pairs={{0,4},{4,8},{8,12},{12,14},{14,10},{10,6},{6,2},{2,0},{1,5},{5,9},... | collective-permute-start | bytes 442376 | tf_op jit(solution)/shard_map/ppermute | solution.py:506
  50.1 5.2 %collective-permute-start.15 = (bf16[16,4608]{1,0:T(8,128)(2,1)S(1)}, bf16[16,4608]{1,0:T(8,128)(2,1)S(1)}, u32[]{:S(2)}, u32[]{:S(2)}) collective-permute-start(bf16[16,4608]{1,0:T(8,128)(2,1)S(1)} %add_convert_fusion.1), channel_id=1, source_target_pairs={{4,0},{8,4},{12,8},{14,12},{10,14},{6,10},{2,6},{0,2},{5,1},{9,5},... | collective-permute-start | bytes 442376 | tf_op jit(solution)/shard_map/ppermute | solution.py:507
  53.6 5.2 %collective-permute-start.12 = (bf16[16,4608]{1,0:T(8,128)(2,1)S(1)}, bf16[16,4608]{1,0:T(8,128)(2,1)S(1)}, u32[]{:S(2)}, u32[]{:S(2)}) collective-permute-start(bf16[16,4608]{1,0:T(8,128)(2,1)S(1)} %add_convert_fusion.2), channel_id=1, source_target_pairs={{0,4},{4,8},{8,12},{12,14},{14,10},{10,6},{6,2},{2,0},{1,5},{5,9},... | collective-permute-start | bytes 442376 | tf_op jit(solution)/shard_map/ppermute | solution.py:506
  55.3 5.2 %collective-permute-start.16 = (bf16[16,4608]{1,0:T(8,128)(2,1)S(1)}, bf16[16,4608]{1,0:T(8,128)(2,1)S(1)}, u32[]{:S(2)}, u32[]{:S(2)}) collective-permute-start(bf16[16,4608]{1,0:T(8,128)(2,1)S(1)} %add_convert_fusion), channel_id=1, source_target_pairs={{4,0},{8,4},{12,8},{14,12},{10,14},{6,10},{2,6},{0,2},{5,1},{9,5},... | collective-permute-start | bytes 442376 | tf_op jit(solution)/shard_map/ppermute | solution.py:507
  60.6 1.3 %collective-permute-start.17 = (bf16[8,4608]{1,0:T(8,128)(2,1)S(1)}, bf16[8,4608]{1,0:T(8,128)(2,1)S(1)}, u32[]{:S(2)}, u32[]{:S(2)}) collective-permute-start(bf16[8,4608]{1,0:T(8,128)(2,1)S(1)} %get-tuple-element.42), channel_id=1, source_target_pairs={{0,1},{1,0},{2,3},{3,2},{4,5},{5,4},{6,7},{7,6},{8,9},{9,8},{10,11... | collective-permute-start | bytes 221192 | tf_op jit(solution)/shard_map/ppermute | solution.py:516

commit v3 on v2

--- a/solution.py
+++ b/solution.py
@@ -213,32 +213,40 @@
     message[:, SLOT_COLS:] = kept[:, SLOT_COLS + LANES :]
 
 
+def copy_kernel(source, out):
+    out[...] = source[...]
+
+
 def fetch_kernel(source, out, sem):
     copy = pltpu.make_async_copy(source, out, sem)
     copy.start()
     copy.wait()
 
 
-def ffn_kernel(n, cut, *refs):
-    blocks, (gate, up, down) = refs[: n + 1], refs[n + 1 : n + 4]
-    outs = refs[n + 4 : 2 * n + 4]
-    low_rows, mix_rows, gate_sum, up_sum = refs[2 * n + 4 :]
-    for j in range(n - 1):
-        low_rows[16 * j : 16 * j + 16, :] = blocks[j][:, :HALF]
-        mix_rows[16 * j : 16 * j + 16, :] = blocks[j][:, HALF:SLOT_COLS]
-    j = n - 1
-    low_rows[16 * j : 16 * j + 16, :] = blocks[j][:, :HALF]
-    mix_rows[16 * j : 16 * j + 16, : cut - HALF] = blocks[j][:, HALF:cut]
-    mix_rows[16 * j : 16 * j + 16, cut - HALF :] = blocks[n][:, : SLOT_COLS - cut]
-
-    size = min(n, 8)
-    span = 16 * size
-    row = iota((span, 1), 0) % 16
+def ffn_kernel(cut, *refs):
+    count = len(refs) // 2 - 3 if cut is None else 1
+    pieces = count if cut is None else 2
+    blocks, (gate, up, down) = refs[:pieces], refs[pieces : pieces + 3]
+    outs = refs[pieces + 3 : pieces + 3 + count]
+    low_rows, mix_rows, gate_sum, up_sum = refs[pieces + 3 + count :]
+    if cut is None:
+        for j in range(count):
+            low_rows[16 * j : 16 * j + 16, :] = blocks[j][:, :HALF]
+            mix_rows[16 * j : 16 * j + 16, :] = blocks[j][:, HALF:SLOT_COLS]
+    else:
+        low_rows[...] = blocks[0][:, :HALF]
+        mix_rows[:, : cut - HALF] = blocks[0][:, HALF:cut]
+        mix_rows[:, cut - HALF :] = blocks[1][:, : SLOT_COLS - cut]
+
+    groups = [(first, min(8, count - first)) for first in range(0, count, 8)]
+    width = gate.shape[1]
     for q in range(4):
-        low_here, mix_here = (row // 8) == q // 2, (row // 4) == q
         part = slice(q * QUARTER, (q + 1) * QUARTER)
         within = slice((q % 2) * QUARTER, (q % 2 + 1) * QUARTER)
-        for at in range(0, 16 * n, span):
+        for first, size in groups:
+            at, span = 16 * first, 16 * size
+            row = iota((span, 1), 0) % 16
+            low_here, mix_here = (row // 8) == q // 2, (row // 4) == q
             left = jnp.concatenate([low_rows[at : at + span, within], mix_rows[at : at + span, :]], axis=0)
             for weight, total in ((gate, gate_sum), (up, up_sum)):
                 product = dot(left, weight[part, :])
@@ -251,25 +259,24 @@
                     total[0, at : at + span, :] += low
                     total[1, at : at + span, :] += mix
 
-    lower = iota((8 * size, 1), 0) % 8 < 4
-    width = gate.shape[1]
-
-    def fold(total, at):
+    def fold(total, at, size):
         low, mix = [
-            jnp.sum(total[k, at : at + span, :].reshape(size, 2, 8, width), axis=1).reshape(8 * size, width)
+            jnp.sum(total[k, at : at + 16 * size, :].reshape(size, 2, 8, width), axis=1).reshape(8 * size, width)
             for k in range(2)
         ]
+        lower = iota((8 * size, 1), 0) % 8 < 4
         other = jnp.where(lower, pltpu.roll(mix, 8 * size - 4, 0), pltpu.roll(mix, 4, 0))
         return low, mix + other
 
     first_rows = iota((8, 1), 0) < 4
-    for at in range(0, 16 * n, span):
-        pieces = [jax.nn.silu(g) * u for g, u in zip(fold(gate_sum, at), fold(up_sum, at))]
+    for first, size in groups:
+        at = 16 * first
+        pieces = [jax.nn.silu(g) * u for g, u in zip(fold(gate_sum, at, size), fold(up_sum, at, size))]
         active = jnp.concatenate([p.reshape(size, 8, width) for p in pieces], axis=1)
-        active = active.reshape(span, width).astype(BF16)
+        active = active.reshape(16 * size, width).astype(BF16)
         quarters = [dot(active, down[:, q * QUARTER : (q + 1) * QUARTER]) for q in range(4)]
         for j in range(size):
-            out = outs[at // 16 + j]
+            out = outs[first + j]
             low_at, mix_at = slice(16 * j, 16 * j + 8), slice(16 * j + 8, 16 * j + 16)
             for part in range(2):
                 both = jnp.concatenate([quarters[part][low_at], quarters[2 + part][low_at]], axis=0)
@@ -432,7 +439,10 @@
         bytes_accessed=3_500_000,
         vmem=60 << 20,
     )
+    tie = lax.optimization_barrier
     theirs = lax.ppermute(other, "expert", swap)
+    kept = call(copy_kernel, shape(kept.shape, BF16), [VMEM], (kept,), bytes_accessed=3_000_000)
+    theirs, kept = tie((theirs, kept))
     message = call(
         pack_kernel,
         shape((2 * LO, SLOT_COLS + moved_cols), BF16),
@@ -444,7 +454,6 @@
 
     far = n // 2
     cut = HALF + 3 * LANES
-    tie = lax.optimization_barrier
     fetch = functools.partial(fetch_weight, shape)
     from_left, from_right = [message], [message]
     weights, stored = [], [w_gate[0], w_up[0], w_down[0]]
@@ -459,24 +468,28 @@
         from_left.append(a)
         from_right.append(b)
     last_a, last_b = from_left.pop(), from_right.pop()
-    blocks = [message] + from_left[1:] + from_right[1:] + [last_a, last_b]
-
+    blocks = [message] + from_left[1:] + from_right[1:]
     ff = w_gate.shape[2]
-    size = 16 * n
-    outs = call(
-        functools.partial(ffn_kernel, n, cut),
-        [shape((2 * LO, SLOT_COLS), BF16)] * n,
-        [VMEM] * (n + 4),
-        (*blocks, *weights),
-        scratch=(
-            pltpu.VMEM((size, HALF), BF16),
-            pltpu.VMEM((size, QUARTER), BF16),
-            pltpu.VMEM((2, size, ff), F32),
-            pltpu.VMEM((2, size, ff), F32),
-        ),
-        flops=2_000_000_000,
-        bytes_accessed=12_000_000,
-    )
+
+    def feed_forward(pieces, count, cut):
+        return call(
+            functools.partial(ffn_kernel, cut),
+            [shape((2 * LO, SLOT_COLS), BF16)] * count,
+            [VMEM] * (len(pieces) + 3),
+            (*pieces, *weights),
+            scratch=(
+                pltpu.VMEM((16 * count, HALF), BF16),
+                pltpu.VMEM((16 * count, QUARTER), BF16),
+                pltpu.VMEM((2, 16 * count, ff), F32),
+                pltpu.VMEM((2, 16 * count, ff), F32),
+            ),
+            flops=2_000_000_000,
+            bytes_accessed=8_000_000,
+        )
+
+    outs = list(feed_forward(blocks, n - 1, None))
+    last_a, outs[0] = tie((last_a, outs[0]))
+    outs = outs + list(feed_forward((last_a, last_b), 1, cut))
 
     to_left = {k: outs[k] for k in range(1, far)}
     to_right = {k: outs[far - 1 + k] for k in range(1, far)}
@@ -487,7 +500,7 @@
         functools.partial(arrive_kernel, n, cut, page_width),
         shape((entries, PAGE, page_width), BF16),
         [VMEM] * (n + 1),
-        tuple(blocks),
+        (*blocks, last_a, last_b),
         scratch=(
             pltpu.VMEM((n, LANES), jnp.int32),
             pltpu.SMEM((n, LANES), jnp.int32),

time: 63.2 us -> 61.8 us (0.978)
  waiting for transfers between devices: 31.7 us -> 28.6 us
  Pallas kernels: 11.1 us -> 12.6 us
    ppermute x8, waiting for transfers between devices: 17.8 us -> 15.5 us  [per_device(): a, b = (lax.ppermute(a, 'attn', right), lax.ppermute(b, 'attn', left))]
    pallas_call x9 -> x11, Pallas kernels: 11.1 us -> 12.6 us  [call(): pl.pallas_call(kernel, out_shape=outs, in_specs=in_specs, out_specs=[VMEM...]
    ppermute x1, waiting for transfers between devices: 1.13 us -> 0.17 us  [per_device(): theirs = lax.ppermute(other, 'expert', swap)]
    ppermute x3, starting transfers between devices: 1.5 us -> 0.62 us  [per_device(): going_left = lax.ppermute(send_left, 'attn', left)]
    ppermute x3, starting transfers between devices: 4.89 us -> 5.77 us  [per_device(): going_right = lax.ppermute(send_right, 'attn', right)]
  transfers between devices with their start and end apart: 18 -> 18, of which waited for: 11 -> 12; matrix products, arithmetic and copies ran while one was open for 0% -> 0% of each run, Pallas kernels for 4% -> 7%
where the time goes in v3:
time: 61.8 us; the launch traced here: 61.7 us
  waiting for transfers between devices  28.6 us (46%)
  starting transfers between devices  18.4 us (30%)
  Pallas kernels  12.6 us (20%)
  local copies, waits for them, and re-layouts  1.01 us (2%)
  between operations  0.8 us (1%)
    ppermute x8, waiting for transfers between devices, per_device(): a, b = (lax.ppermute(a, 'attn', right), lax.ppermute(b, 'attn', left))  15.5 us
    pallas_call x11, Pallas kernels, call(): pl.pallas_call(kernel, out_shape=outs, in_specs=in_specs, out_specs=[VMEM...  12.6 us
    ppermute x8, starting transfers between devices, per_device(): a, b = (lax.ppermute(a, 'attn', right), lax.ppermute(b, 'attn', left))  9.31 us
    ppermute x3, waiting for transfers between devices, per_device(): going_right = lax.ppermute(send_right, 'attn', right)  9.04 us
    ppermute x3, starting transfers between devices, per_device(): going_right = lax.ppermute(send_right, 'attn', right)  5.77 us
    ppermute x3, waiting for transfers between devices, per_device(): going_left = lax.ppermute(send_left, 'attn', left)  1.99 us
    ppermute x1, starting transfers between devices, per_device(): going_right = lax.ppermute(outs[n - 1][:, :split], 'attn', right)  1.94 us
    ppermute x1, waiting for transfers between devices, per_device(): returned = lax.ppermute(other_half, 'expert', swap)  1.25 us
  transfers between devices with their start and end apart: 18, of which 12 were waited for; matrix products, arithmetic and copies ran while one was open for 0% of the time, Pallas kernels for 7%

profile of v3, /device:TPU:0, one launch (start us, length us, event | category | flops | bytes accessed | tf_op | source)
XLA Modules:
  0.0 61.7 jit_solution(1887734453144537929)
XLA Ops:
  0.6 5.1 %shard_map.158 = (f32[32,3072]{1,0:T(8,128)}, bf16[16,6912]{1,0:T(8,128)(2,1)}, bf16[8,4736]{1,0:T(8,128)(2,1)}) custom-call(s32[1,32]{1,0:T(1,128)} %refs_0_.1, s32[1,32]{1,0:T(1,128)} %bitcast.16, s32[1,72]{1,0:T(1,128)} %refs_2_.1, s32[2,32]{1,0:T(2,128)} %bitcast.11, s32[1,2]{1,0:T(1,128)} %refs_4_.1, s32[1,2]{1,0:T(1,128)} %refs_5_.1, ...), custom_call_target="tpu_custom_call" | custom-call | flops 500000000 | bytes 3500000 | tf_op jit(solution)/shard_map/pallas_call | solution.py:353
  5.8 0.5 collective-permute-start
  6.3 0.9 %copy-done.4 = bf16[16,6912]{1,0:T(8,128)(2,1)S(1)} copy-done((bf16[16,6912]{1,0:T(8,128)(2,1)S(1)}, bf16[16,6912]{1,0:T(8,128)(2,1)}, u32[]{:S(2)}) %copy-start.4) | copy-done | bytes 221208
  7.3 0.2 collective-permute-done.theirs
  7.4 0.1 shard_map.160.refs_0_
  7.6 3.0 %collective-permute-start.1 = (bf16[16,6784]{1,0:T(8,128)(2,1)S(1)}, bf16[16,6784]{1,0:T(8,128)(2,1)S(1)}, u32[]{:S(2)}, u32[]{:S(2)}) collective-permute-start(bf16[16,6784]{1,0:T(8,128)(2,1)S(1)} %shard_map.160.refs_0_), channel_id=1, source_target_pairs={{0,4},{4,8},{8,12},{12,14},{14,10},{10,6},{6,2},{2,0},{1,5},{5,9},... | collective-permute-start | bytes 651272 | tf_op jit(solution)/shard_map/ppermute | solution.py:464
  10.5 0.0 collective-permute-start.5
  10.6 0.2 shard_map.161.refs_7_.refs_2_
  10.8 5.4 %collective-permute-done.1.refs_1_ = bf16[16,6784]{1,0:T(8,128)(2,1)S(1)} collective-permute-done((bf16[16,6784]{1,0:T(8,128)(2,1)S(1)}, bf16[16,6784]{1,0:T(8,128)(2,1)S(1)}, u32[]{:S(2)}, u32[]{:S(2)}) %collective-permute-start.1) | collective-permute-done | bytes 217120 | tf_op jit(solution)/shard_map/ppermute | solution.py:464
  16.1 1.5 %collective-permute-done.5.refs_4_ = bf16[16,6784]{1,0:T(8,128)(2,1)S(1)} collective-permute-done((bf16[16,6784]{1,0:T(8,128)(2,1)S(1)}, bf16[16,6784]{1,0:T(8,128)(2,1)S(1)}, u32[]{:S(2)}, u32[]{:S(2)}) %collective-permute-start.5) | collective-permute-done | bytes 217120 | tf_op jit(solution)/shard_map/ppermute | solution.py:464
  17.7 0.3 collective-permute-start.6
  18.0 1.7 %collective-permute-start.2 = (bf16[16,6784]{1,0:T(8,128)(2,1)S(1)}, bf16[16,6784]{1,0:T(8,128)(2,1)S(1)}, u32[]{:S(2)}, u32[]{:S(2)}) collective-permute-start(bf16[16,6784]{1,0:T(8,128)(2,1)S(1)} %collective-permute-done.1.refs_1_), channel_id=1, source_target_pairs={{0,4},{4,8},{8,12},{12,14},{14,10},{10,6},{6,2},{2,0},{1,5},{5,9},... | collective-permute-start | bytes 651272 | tf_op jit(solution)/shard_map/ppermute | solution.py:464
  19.7 0.2 shard_map.162.refs_8_.refs_3_
  19.9 4.0 %collective-permute-done.6.refs_5_ = bf16[16,6784]{1,0:T(8,128)(2,1)S(1)} collective-permute-done((bf16[16,6784]{1,0:T(8,128)(2,1)S(1)}, bf16[16,6784]{1,0:T(8,128)(2,1)S(1)}, u32[]{:S(2)}, u32[]{:S(2)}) %collective-permute-start.6) | collective-permute-done | bytes 217120 | tf_op jit(solution)/shard_map/ppermute | solution.py:464
  23.9 0.6 collective-permute-start.7
  24.5 0.0 collective-permute-done.2.refs_2_
  24.5 1.4 %collective-permute-start.3 = (bf16[16,6784]{1,0:T(8,128)(2,1)S(1)}, bf16[16,6784]{1,0:T(8,128)(2,1)S(1)}, u32[]{:S(2)}, u32[]{:S(2)}) collective-permute-start(bf16[16,6784]{1,0:T(8,128)(2,1)S(1)} %collective-permute-done.2.refs_2_), channel_id=1, source_target_pairs={{0,4},{4,8},{8,12},{12,14},{14,10},{10,6},{6,2},{2,0},{1,5},{5,9},... | collective-permute-start | bytes 651272 | tf_op jit(solution)/shard_map/ppermute | solution.py:464
  26.0 0.2 shard_map.163.refs_9_.refs_4_
  26.2 4.0 %collective-permute-done.7.refs_6_ = bf16[16,6784]{1,0:T(8,128)(2,1)S(1)} collective-permute-done((bf16[16,6784]{1,0:T(8,128)(2,1)S(1)}, bf16[16,6784]{1,0:T(8,128)(2,1)S(1)}, u32[]{:S(2)}, u32[]{:S(2)}) %collective-permute-start.7) | collective-permute-done | bytes 217120 | tf_op jit(solution)/shard_map/ppermute | solution.py:464
  30.2 0.3 collective-permute-start.8
  30.5 0.0 collective-permute-done.3.refs_3_
  30.5 1.9 %collective-permute-start.4 = (bf16[16,3456]{1,0:T(8,128)(2,1)S(1)}, bf16[16,3456]{1,0:T(8,128)(2,1)S(1)}, u32[]{:S(2)}, u32[]{:S(2)}) collective-permute-start(bf16[16,3456]{1,0:T(8,128)(2,1)S(1)} %slice.24), channel_id=1, source_target_pairs={{0,4},{4,8},{8,12},{12,14},{14,10},{10,6},{6,2},{2,0},{1,5},{5,9},... | collective-permute-start | bytes 331784 | tf_op jit(solution)/shard_map/ppermute | solution.py:464
  32.5 2.3 %shard_map.164 = (bf16[16,4608]{1,0:T(8,128)(2,1)S(1)}, bf16[16,4608]{1,0:T(8,128)(2,1)S(1)}, bf16[16,4608]{1,0:T(8,128)(2,1)S(1)}, bf16[16,4608]{1,0:T(8,128)(2...) custom-call(bf16[16,6784]{1,0:T(8,128)(2,1)S(1)} %shard_map.160.refs_0_, ...), custom_call_target="tpu_custom_call" | custom-call | flops 2000000000 | bytes 8000000 | tf_op jit(solution)/shard_map/pallas_call | solution.py:353
  34.7 0.6 collective-permute-done.4.refs_0_.refs_7_
  35.3 0.0 collective-permute-done.8.refs_1_.refs_8_
  35.3 1.7 %shard_map.165 = bf16[16,4608]{1,0:T(8,128)(2,1)S(1)} custom-call(bf16[16,3456]{1,0:T(8,128)(2,1)S(1)} %collective-permute-done.4.refs_0_.refs_7_, bf16[16,3328]{1,0:T(8,128)(2,1)S(1)} %collective-permute-done.8.refs_1_.refs_8_, bf16[6144,256]{1,0:T(8,128)(2,1)S(1)} %shard_map.161.refs_7_.refs_2_, bf16[6144,256]{1,0:T(8,128)(2,1)S(1)} %shard_map.162.refs_8_.refs_3_, ...), custom_call_target="tpu_custom_call" | custom-call | flops 2000000000 | bytes 8000000 | tf_op jit(solution)/shard_map/pallas_call | solution.py:353
  37.0 0.0 copy-start.6
  37.0 1.9 %collective-permute-start.9 = (bf16[16,2304]{1,0:T(8,128)(2,1)S(1)}, bf16[16,2304]{1,0:T(8,128)(2,1)S(1)}, u32[]{:S(2)}, u32[]{:S(2)}) collective-permute-start(bf16[16,2304]{1,0:T(8,128)(2,1)S(1)} %get-tuple-element.51), channel_id=1, source_target_pairs={{0,4},{4,8},{8,12},{12,14},{14,10},{10,6},{6,2},{2,0},{1,5},{5,9},... | collective-permute-start | bytes 221192 | tf_op jit(solution)/shard_map/ppermute | solution.py:497
  39.0 0.2 collective-permute-start.13
  39.2 1.6 %shard_map.166 = bf16[2,16,1024]{2,1,0:T(8,128)(2,1)} custom-call(bf16[16,6784]{1,0:T(8,128)(2,1)S(1)} %shard_map.160.refs_0_, bf16[16,6784]{1,0:T(8,128)(2,1)S(1)} %collective-permute-done.1.refs_1_, bf16[16,6784]{1,0:T(8,128)(2,1)S(1)} %collective-permute-done.2.refs_2_, bf16[16,6784]{1,0:T(8,128)(2,1)S(1)} %collective-permute-done.3.refs_3_, ...), custom_call_target="tpu_custom_call" | custom-call | flops 100000 | bytes 2000000 | tf_op jit(solution)/shard_map/pallas_call | solution.py:353
  40.8 0.7 %collective-permute-done.9 = bf16[16,2304]{1,0:T(8,128)(2,1)S(1)} collective-permute-done((bf16[16,2304]{1,0:T(8,128)(2,1)S(1)}, bf16[16,2304]{1,0:T(8,128)(2,1)S(1)}, u32[]{:S(2)}, u32[]{:S(2)}) %collective-permute-start.9) | collective-permute-done | bytes 73760 | tf_op jit(solution)/shard_map/ppermute | solution.py:497
  41.5 1.9 %collective-permute-start.10 = (bf16[16,4608]{1,0:T(8,128)(2,1)S(1)}, bf16[16,4608]{1,0:T(8,128)(2,1)S(1)}, u32[]{:S(2)}, u32[]{:S(2)}) collective-permute-start(bf16[16,4608]{1,0:T(8,128)(2,1)S(1)} %pad_maximum_fusion), channel_id=1, source_target_pairs={{0,4},{4,8},{8,12},{12,14},{14,10},{10,6},{6,2},{2,0},{1,5},{5,9},... | collective-permute-start | bytes 442376 | tf_op jit(solution)/shard_map/ppermute | solution.py:519
  43.4 0.0 collective-permute-done.13
  43.5 0.2 collective-permute-start.14
  43.7 3.0 %collective-permute-done.10 = bf16[16,4608]{1,0:T(8,128)(2,1)S(1)} collective-permute-done((bf16[16,4608]{1,0:T(8,128)(2,1)S(1)}, bf16[16,4608]{1,0:T(8,128)(2,1)S(1)}, u32[]{:S(2)}, u32[]{:S(2)}) %collective-permute-start.10) | collective-permute-done | bytes 147488 | tf_op jit(solution)/shard_map/ppermute | solution.py:519
  46.7 1.9 %collective-permute-start.11 = (bf16[16,4608]{1,0:T(8,128)(2,1)S(1)}, bf16[16,4608]{1,0:T(8,128)(2,1)S(1)}, u32[]{:S(2)}, u32[]{:S(2)}) collective-permute-start(bf16[16,4608]{1,0:T(8,128)(2,1)S(1)} %add_convert_fusion.3), channel_id=1, source_target_pairs={{0,4},{4,8},{8,12},{12,14},{14,10},{10,6},{6,2},{2,0},{1,5},{5,9},... | collective-permute-start | bytes 442376 | tf_op jit(solution)/shard_map/ppermute | solution.py:519
  48.7 0.0 collective-permute-done.14
  48.7 0.2 collective-permute-start.15
  48.9 3.0 %collective-permute-done.11 = bf16[16,4608]{1,0:T(8,128)(2,1)S(1)} collective-permute-done((bf16[16,4608]{1,0:T(8,128)(2,1)S(1)}, bf16[16,4608]{1,0:T(8,128)(2,1)S(1)}, u32[]{:S(2)}, u32[]{:S(2)}) %collective-permute-start.11) | collective-permute-done | bytes 147488 | tf_op jit(solution)/shard_map/ppermute | solution.py:519
  52.0 1.9 %collective-permute-start.12 = (bf16[16,4608]{1,0:T(8,128)(2,1)S(1)}, bf16[16,4608]{1,0:T(8,128)(2,1)S(1)}, u32[]{:S(2)}, u32[]{:S(2)}) collective-permute-start(bf16[16,4608]{1,0:T(8,128)(2,1)S(1)} %add_convert_fusion.2), channel_id=1, source_target_pairs={{0,4},{4,8},{8,12},{12,14},{14,10},{10,6},{6,2},{2,0},{1,5},{5,9},... | collective-permute-start | bytes 442376 | tf_op jit(solution)/shard_map/ppermute | solution.py:519
  53.9 0.0 collective-permute-done.15
  54.0 0.2 collective-permute-start.16
  54.2 3.0 %collective-permute-done.12.from_left = bf16[16,4608]{1,0:T(8,128)(2,1)S(1)} collective-permute-done((bf16[16,4608]{1,0:T(8,128)(2,1)S(1)}, bf16[16,4608]{1,0:T(8,128)(2,1)S(1)}, u32[]{:S(2)}, u32[]{:S(2)}) %collective-permute-start.12) | collective-permute-done | bytes 147488 | tf_op jit(solution)/shard_map/ppermute | solution.py:519
  57.2 2.0 %collective-permute-done.16.from_right = bf16[16,4608]{1,0:T(8,128)(2,1)S(1)} collective-permute-done((bf16[16,4608]{1,0:T(8,128)(2,1)S(1)}, bf16[16,4608]{1,0:T(8,128)(2,1)S(1)}, u32[]{:S(2)}, u32[]{:S(2)}) %collective-permute-start.16) | collective-permute-done | bytes 147488 | tf_op jit(solution)/shard_map/ppermute | solution.py:520
  59.2 0.1 shard_map.167
  59.2 0.1 collective-permute-start.17
  59.3 1.3 %collective-permute-done.17.theirs = bf16[8,4608]{1,0:T(8,128)(2,1)S(1)} collective-permute-done((bf16[8,4608]{1,0:T(8,128)(2,1)S(1)}, bf16[8,4608]{1,0:T(8,128)(2,1)S(1)}, u32[]{:S(2)}, u32[]{:S(2)}) %collective-permute-start.17) | collective-permute-done | bytes 73760 | tf_op jit(solution)/shard_map/ppermute | solution.py:529
  60.6 1.1 %shard_map.168 = bf16[32,3072]{1,0:T(8,128)(2,1)} custom-call(f32[32,3072]{1,0:T(8,128)S(1)} %copy-done.3, bf16[8,4608]{1,0:T(8,128)(2,1)S(1)} %get-tuple-element.47.mine, bf16[8,4608]{1,0:T(8,128)(2,1)S(1)} %collective-permute-done.17.theirs, s32[2,32]{1,0:T(2,128)S(1)} %bitcast.12, f32[2,32]{1,0:T(2,128)S(1)} %bitcast.13), custom_call_target="tpu_custom_call" | custom-call | flops 20000000 | bytes 800000 | tf_op jit(solution)/shard_map/pallas_call | solution.py:353
  (26 shorter events, 0.3 us)
Async XLA Ops:
  0.6 9.9 %copy-start = (bf16[1,6144,256]{2,1,0:T(8,128)(2,1)S(1)}, bf16[1,6144,256]{2,1,0:T(8,128)(2,1)}, u32[]{:S(2)}) copy-start(bf16[1,6144,256]{2,1,0:T(8,128)(2,1)} %param.25) | copy-start | bytes 9437188
  5.8 1.7 %collective-permute-start = (bf16[8,4736]{1,0:T(8,128)(2,1)}, bf16[8,4736]{1,0:T(8,128)(2,1)S(1)}, u32[]{:S(2)}, u32[]{:S(2)}) collective-permute-start(bf16[8,4736]{1,0:T(8,128)(2,1)} %get-tuple-element.27), channel_id=1, source_target_pairs={{0,1},{1,0},{2,3},{3,2},{4,5},{5,4},{6,7},{7,6},{8,9},{9,8},{10,11... | collective-permute-start | bytes 227336 | tf_op jit(solution)/shard_map/ppermute | solution.py:443
  6.3 0.9 %copy-start.4 = (bf16[16,6912]{1,0:T(8,128)(2,1)S(1)}, bf16[16,6912]{1,0:T(8,128)(2,1)}, u32[]{:S(2)}) copy-start(bf16[16,6912]{1,0:T(8,128)(2,1)} %get-tuple-element.28.source) | copy-start | bytes 663556
  7.6 8.6 %collective-permute-start.1 = (bf16[16,6784]{1,0:T(8,128)(2,1)S(1)}, bf16[16,6784]{1,0:T(8,128)(2,1)S(1)}, u32[]{:S(2)}, u32[]{:S(2)}) collective-permute-start(bf16[16,6784]{1,0:T(8,128)(2,1)S(1)} %shard_map.160.refs_0_), channel_id=1, source_target_pairs={{0,4},{4,8},{8,12},{12,14},{14,10},{10,6},{6,2},{2,0},{1,5},{5,9},... | collective-permute-start | bytes 651272 | tf_op jit(solution)/shard_map/ppermute | solution.py:464
  10.5 7.1 %collective-permute-start.5 = (bf16[16,6784]{1,0:T(8,128)(2,1)S(1)}, bf16[16,6784]{1,0:T(8,128)(2,1)S(1)}, u32[]{:S(2)}, u32[]{:S(2)}) collective-permute-start(bf16[16,6784]{1,0:T(8,128)(2,1)S(1)} %shard_map.160.refs_0_), channel_id=1, source_target_pairs={{4,0},{8,4},{12,8},{14,12},{10,14},{6,10},{2,6},{0,2},{5,1},{9,5},... | collective-permute-start | bytes 651272 | tf_op jit(solution)/shard_map/ppermute | solution.py:464
  10.6 9.1 %copy-start.1 = (bf16[1,6144,256]{2,1,0:T(8,128)(2,1)S(1)}, bf16[1,6144,256]{2,1,0:T(8,128)(2,1)}, u32[]{:S(2)}) copy-start(bf16[1,6144,256]{2,1,0:T(8,128)(2,1)} %param.26) | copy-start | bytes 9437188
  17.7 6.3 %collective-permute-start.6 = (bf16[16,6784]{1,0:T(8,128)(2,1)S(1)}, bf16[16,6784]{1,0:T(8,128)(2,1)S(1)}, u32[]{:S(2)}, u32[]{:S(2)}) collective-permute-start(bf16[16,6784]{1,0:T(8,128)(2,1)S(1)} %collective-permute-done.5.refs_4_), channel_id=1, source_target_pairs={{4,0},{8,4},{12,8},{14,12},{10,14},{6,10},{2,6},{0,2},{5,1},{9,5},... | collective-permute-start | bytes 651272 | tf_op jit(solution)/shard_map/ppermute | solution.py:464
  18.0 6.6 %collective-permute-start.2 = (bf16[16,6784]{1,0:T(8,128)(2,1)S(1)}, bf16[16,6784]{1,0:T(8,128)(2,1)S(1)}, u32[]{:S(2)}, u32[]{:S(2)}) collective-permute-start(bf16[16,6784]{1,0:T(8,128)(2,1)S(1)} %collective-permute-done.1.refs_1_), channel_id=1, source_target_pairs={{0,4},{4,8},{8,12},{12,14},{14,10},{10,6},{6,2},{2,0},{1,5},{5,9},... | collective-permute-start | bytes 651272 | tf_op jit(solution)/shard_map/ppermute | solution.py:464
  19.7 6.3 %copy-start.2 = (bf16[1,256,6144]{2,1,0:T(8,128)(2,1)S(1)}, bf16[1,256,6144]{2,1,0:T(8,128)(2,1)}, u32[]{:S(2)}) copy-start(bf16[1,256,6144]{2,1,0:T(8,128)(2,1)} %param.27) | copy-start | bytes 9437188
  23.9 6.2 %collective-permute-start.7 = (bf16[16,6784]{1,0:T(8,128)(2,1)S(1)}, bf16[16,6784]{1,0:T(8,128)(2,1)S(1)}, u32[]{:S(2)}, u32[]{:S(2)}) collective-permute-start(bf16[16,6784]{1,0:T(8,128)(2,1)S(1)} %collective-permute-done.6.refs_5_), channel_id=1, source_target_pairs={{4,0},{8,4},{12,8},{14,12},{10,14},{6,10},{2,6},{0,2},{5,1},{9,5},... | collective-permute-start | bytes 651272 | tf_op jit(solution)/shard_map/ppermute | solution.py:464
  24.5 6.0 %collective-permute-start.3 = (bf16[16,6784]{1,0:T(8,128)(2,1)S(1)}, bf16[16,6784]{1,0:T(8,128)(2,1)S(1)}, u32[]{:S(2)}, u32[]{:S(2)}) collective-permute-start(bf16[16,6784]{1,0:T(8,128)(2,1)S(1)} %collective-permute-done.2.refs_2_), channel_id=1, source_target_pairs={{0,4},{4,8},{8,12},{12,14},{14,10},{10,6},{6,2},{2,0},{1,5},{5,9},... | collective-permute-start | bytes 651272 | tf_op jit(solution)/shard_map/ppermute | solution.py:464
  30.2 5.2 %collective-permute-start.8 = (bf16[16,3328]{1,0:T(8,128)(2,1)S(1)}, bf16[16,3328]{1,0:T(8,128)(2,1)S(1)}, u32[]{:S(2)}, u32[]{:S(2)}) collective-permute-start(bf16[16,3328]{1,0:T(8,128)(2,1)S(1)} %slice.32), channel_id=1, source_target_pairs={{4,0},{8,4},{12,8},{14,12},{10,14},{6,10},{2,6},{0,2},{5,1},{9,5},... | collective-permute-start | bytes 319496 | tf_op jit(solution)/shard_map/ppermute | solution.py:464
  30.5 4.8 %collective-permute-start.4 = (bf16[16,3456]{1,0:T(8,128)(2,1)S(1)}, bf16[16,3456]{1,0:T(8,128)(2,1)S(1)}, u32[]{:S(2)}, u32[]{:S(2)}) collective-permute-start(bf16[16,3456]{1,0:T(8,128)(2,1)S(1)} %slice.24), channel_id=1, source_target_pairs={{0,4},{4,8},{8,12},{12,14},{14,10},{10,6},{6,2},{2,0},{1,5},{5,9},... | collective-permute-start | bytes 331784 | tf_op jit(solution)/shard_map/ppermute | solution.py:464
  37.0 23.6 %copy-start.3 = (f32[32,3072]{1,0:T(8,128)S(1)}, f32[32,3072]{1,0:T(8,128)}, u32[]{:S(2)}) copy-start(f32[32,3072]{1,0:T(8,128)} %get-tuple-element.26.hidden) | copy-start | bytes 1179652
  37.0 23.6 %copy-start.5 = (s32[32,2]{0,1:T(2,128)S(1)}, s32[32,2]{0,1:T(2,128)}, u32[]{:S(2)}) copy-start(s32[32,2]{0,1:T(2,128)} %param.23) | copy-start | bytes 772
  37.0 23.6 %copy-start.6 = (f32[32,2]{0,1:T(2,128)S(1)}, f32[32,2]{0,1:T(2,128)}, u32[]{:S(2)}) copy-start(f32[32,2]{0,1:T(2,128)} %param.24) | copy-start | bytes 772
  37.0 4.4 %collective-permute-start.9 = (bf16[16,2304]{1,0:T(8,128)(2,1)S(1)}, bf16[16,2304]{1,0:T(8,128)(2,1)S(1)}, u32[]{:S(2)}, u32[]{:S(2)}) collective-permute-start(bf16[16,2304]{1,0:T(8,128)(2,1)S(1)} %get-tuple-element.51), channel_id=1, source_target_pairs={{0,4},{4,8},{8,12},{12,14},{14,10},{10,6},{6,2},{2,0},{1,5},{5,9},... | collective-permute-start | bytes 221192 | tf_op jit(solution)/shard_map/ppermute | solution.py:497
  39.0 4.4 %collective-permute-start.13 = (bf16[16,2304]{1,0:T(8,128)(2,1)S(1)}, bf16[16,2304]{1,0:T(8,128)(2,1)S(1)}, u32[]{:S(2)}, u32[]{:S(2)}) collective-permute-start(bf16[16,2304]{1,0:T(8,128)(2,1)S(1)} %get-tuple-element.50), channel_id=1, source_target_pairs={{4,0},{8,4},{12,8},{14,12},{10,14},{6,10},{2,6},{0,2},{5,1},{9,5},... | collective-permute-start | bytes 221192 | tf_op jit(solution)/shard_map/ppermute | solution.py:498
  41.5 5.2 %collective-permute-start.10 = (bf16[16,4608]{1,0:T(8,128)(2,1)S(1)}, bf16[16,4608]{1,0:T(8,128)(2,1)S(1)}, u32[]{:S(2)}, u32[]{:S(2)}) collective-permute-start(bf16[16,4608]{1,0:T(8,128)(2,1)S(1)} %pad_maximum_fusion), channel_id=1, source_target_pairs={{0,4},{4,8},{8,12},{12,14},{14,10},{10,6},{6,2},{2,0},{1,5},{5,9},... | collective-permute-start | bytes 442376 | tf_op jit(solution)/shard_map/ppermute | solution.py:519
  43.5 5.2 %collective-permute-start.14 = (bf16[16,4608]{1,0:T(8,128)(2,1)S(1)}, bf16[16,4608]{1,0:T(8,128)(2,1)S(1)}, u32[]{:S(2)}, u32[]{:S(2)}) collective-permute-start(bf16[16,4608]{1,0:T(8,128)(2,1)S(1)} %pad_maximum_fusion.1), channel_id=1, source_target_pairs={{4,0},{8,4},{12,8},{14,12},{10,14},{6,10},{2,6},{0,2},{5,1},{9,5},... | collective-permute-start | bytes 442376 | tf_op jit(solution)/shard_map/ppermute | solution.py:520
  46.7 5.2 %collective-permute-start.11 = (bf16[16,4608]{1,0:T(8,128)(2,1)S(1)}, bf16[16,4608]{1,0:T(8,128)(2,1)S(1)}, u32[]{:S(2)}, u32[]{:S(2)}) collective-permute-start(bf16[16,4608]{1,0:T(8,128)(2,1)S(1)} %add_convert_fusion.3), channel_id=1, source_target_pairs={{0,4},{4,8},{8,12},{12,14},{14,10},{10,6},{6,2},{2,0},{1,5},{5,9},... | collective-permute-start | bytes 442376 | tf_op jit(solution)/shard_map/ppermute | solution.py:519
  48.7 5.2 %collective-permute-start.15 = (bf16[16,4608]{1,0:T(8,128)(2,1)S(1)}, bf16[16,4608]{1,0:T(8,128)(2,1)S(1)}, u32[]{:S(2)}, u32[]{:S(2)}) collective-permute-start(bf16[16,4608]{1,0:T(8,128)(2,1)S(1)} %add_convert_fusion.1), channel_id=1, source_target_pairs={{4,0},{8,4},{12,8},{14,12},{10,14},{6,10},{2,6},{0,2},{5,1},{9,5},... | collective-permute-start | bytes 442376 | tf_op jit(solution)/shard_map/ppermute | solution.py:520
  52.0 5.2 %collective-permute-start.12 = (bf16[16,4608]{1,0:T(8,128)(2,1)S(1)}, bf16[16,4608]{1,0:T(8,128)(2,1)S(1)}, u32[]{:S(2)}, u32[]{:S(2)}) collective-permute-start(bf16[16,4608]{1,0:T(8,128)(2,1)S(1)} %add_convert_fusion.2), channel_id=1, source_target_pairs={{0,4},{4,8},{8,12},{12,14},{14,10},{10,6},{6,2},{2,0},{1,5},{5,9},... | collective-permute-start | bytes 442376 | tf_op jit(solution)/shard_map/ppermute | solution.py:519
  54.0 5.2 %collective-permute-start.16 = (bf16[16,4608]{1,0:T(8,128)(2,1)S(1)}, bf16[16,4608]{1,0:T(8,128)(2,1)S(1)}, u32[]{:S(2)}, u32[]{:S(2)}) collective-permute-start(bf16[16,4608]{1,0:T(8,128)(2,1)S(1)} %add_convert_fusion), channel_id=1, source_target_pairs={{4,0},{8,4},{12,8},{14,12},{10,14},{6,10},{2,6},{0,2},{5,1},{9,5},... | collective-permute-start | bytes 442376 | tf_op jit(solution)/shard_map/ppermute | solution.py:520
  59.2 1.3 %collective-permute-start.17 = (bf16[8,4608]{1,0:T(8,128)(2,1)S(1)}, bf16[8,4608]{1,0:T(8,128)(2,1)S(1)}, u32[]{:S(2)}, u32[]{:S(2)}) collective-permute-start(bf16[8,4608]{1,0:T(8,128)(2,1)S(1)} %get-tuple-element.48), channel_id=1, source_target_pairs={{0,1},{1,0},{2,3},{3,2},{4,5},{5,4},{6,7},{7,6},{8,9},{9,8},{10,11... | collective-permute-start | bytes 221192 | tf_op jit(solution)/shard_map/ppermute | solution.py:529

commit v4 on v3

--- a/solution.py
+++ b/solution.py
@@ -68,28 +68,22 @@
     return high.astype(F32), middle.astype(F32), low.astype(F32)
 
 
-def attend_kernel(hosted, *refs):
-    sources, (hidden, kept, other), held_here, sems = refs[:11], refs[11:14], refs[14:25], refs[25]
-    counts, tails, order, routes, mig_pages, mig_dest, queries, new_kv, residual, gain, pool = held_here
-    rows = queries.shape[0]
-    tokens = pool.shape[0]
-    pages = tokens // PAGE
-    heads_here = pool.shape[1] // (2 * HD)
-    group = queries.shape[1] // (heads_here * HD)
-
-    copies = [
-        pltpu.make_async_copy(a, b, sems.at[k]) for k, (a, b) in enumerate(zip(sources[:-1], held_here[:-1]))
-    ]
-    for head in range(heads_here):
+def load(sources, held, sems, small):
+    copies = [pltpu.make_async_copy(a, b, sems.at[k]) for k, (a, b) in enumerate(zip(sources[:-1], held[:-1]))]
+    pool = held[-1]
+    for head in range(pool.shape[1] // (2 * HD)):
         columns = pl.ds(2 * head * HD, 2 * HD)
         copies.append(
             pltpu.make_async_copy(sources[-1].at[:, columns], pool.at[:, columns], sems.at[len(sources) - 1 + head])
         )
-    for copy in copies[:8] + copies[10:] + copies[8:10]:
+    for copy in copies:
         copy.start()
-    for copy in copies[:6]:
+    for copy in copies[:small]:
         copy.wait()
-
+    return copies[small:]
+
+
+def tokens_held(counts, tails, rows, pages):
     counts_row = counts[...].astype(F32)
     row_a, row_b = iota((rows, rows), 0), iota((rows, rows), 1)
     first = jnp.sum(jnp.where(row_b < row_a, counts_row, 0.0), axis=1, keepdims=True)
@@ -97,88 +91,126 @@
     tail = to_column(tails[...].astype(F32), rows)
     place = iota((rows, pages), 1).astype(F32)
     inside = (place >= first) & (place < first + count)
-    held = jnp.where(inside, jnp.where(place == first + count - 1.0, tail, float(PAGE)), 0.0)
+    return jnp.where(inside, jnp.where(place == first + count - 1.0, tail, float(PAGE)), 0.0)
+
+
+def hide_foreign(held, order, tokens):
+    rows, pages = held.shape
     page_at = to_column(order[...].astype(F32), pages)
     page_of = (iota((pages, tokens), 1) // PAGE).astype(F32)
     placed = jnp.where(page_at == page_of, 1.0, 0.0).astype(BF16)
     limit = dot(held.astype(BF16), placed)
     visible = (iota((rows, tokens), 1) % PAGE).astype(F32) < limit
-    copies[6].wait()
-    copies[7].wait()
-    squares = jnp.zeros((rows, HD), F32)
-    penalty = jnp.where(visible, 0.0, NEG)[None]
-    own_penalty = jnp.where(eye(rows), 0.0, NEG)[None]
-    def qk(head):
-        base = head * group * HD
-        query = jnp.concatenate(
-            [queries[:, base + g * HD : base + (g + 1) * HD] for g in range(group)], axis=0
-        )
+    return jnp.where(visible, 0.0, NEG)
+
+
+def attend(query_of, newest, pool, penalty, waits, finish):
+    rows, tokens = penalty.shape
+    heads_here = pool.shape[1] // (2 * HD)
+    own_penalty = jnp.where(eye(rows), 0.0, NEG)
+    products = []
+    for head in range(heads_here):
+        if head % 2 == 0:
+            for copy in waits[head : head + 2]:
+                copy.wait()
         keys = slice(2 * head * HD, (2 * head + 1) * HD)
-        scores = dot_t(query, pool[:, keys])
-        own = dot_t(query, new_kv[:, keys])
-        scores = (scores.reshape(group, rows, tokens) + penalty).reshape(group * rows, tokens)
-        own = (own.reshape(group, rows, rows) + own_penalty).reshape(group * rows, rows)
-        return scores, own
-    def soft(so):
-        scores, own = so
-        top = jnp.maximum(
-            jnp.max(scores, axis=1, keepdims=True), jnp.max(own, axis=1, keepdims=True)
-        )
+        query = query_of(head)
+        group = query.shape[0] // rows
+        scores = dot_t(query, pool[:, keys]).reshape(group, rows, tokens) + penalty[None]
+        own = dot_t(query, newest[:, keys]).reshape(group, rows, rows) + own_penalty[None]
+        products.append((scores.reshape(group * rows, tokens), own.reshape(group * rows, rows)))
+    for head, (scores, own) in enumerate(products):
+        values = slice((2 * head + 1) * HD, (2 * head + 2) * HD)
+        top = jnp.maximum(jnp.max(scores, axis=1, keepdims=True), jnp.max(own, axis=1, keepdims=True))
         weights = jnp.exp((scores - top) * SCORE_SCALE)
         own_weights = jnp.exp((own - top) * SCORE_SCALE)
         total = jnp.sum(weights, axis=1, keepdims=True) + jnp.sum(own_weights, axis=1, keepdims=True)
         inverse = 1.0 / total
-        return (weights * inverse).astype(BF16), (own_weights * inverse).astype(BF16)
-    def pv(head, w, squares):
+        mixed = dot((weights * inverse).astype(BF16), pool[:, values])
+        mixed = mixed + dot((own_weights * inverse).astype(BF16), newest[:, values])
+        for g in range(group):
+            at = (head * group + g) * HD
+            finish(slice(at, at + HD), mixed[g * rows : (g + 1) * rows])
+
+
+def hidden_kernel(*refs):
+    sources, hidden, held, sems = refs[:7], refs[7], refs[8:15], refs[15]
+    counts, tails, order, queries, new_kv, residual, pool = held
+    waits = load(sources, held, sems, 3)
+    rows, tokens = queries.shape[0], pool.shape[0]
+    penalty = hide_foreign(tokens_held(counts, tails, rows, tokens // PAGE), order, tokens)
+    for copy in waits[:3]:
+        copy.wait()
+    heads_here = pool.shape[1] // (2 * HD)
+    group = queries.shape[1] // (heads_here * HD)
+
+    def query_of(head):
         base = head * group * HD
-        values = slice((2 * head + 1) * HD, (2 * head + 2) * HD)
-        mixed = dot(w[0], pool[:, values])
-        mixed = mixed + dot(w[1], new_kv[:, values])
-        for g in range(group):
-            columns = slice(base + g * HD, base + (g + 1) * HD)
-            part = residual[:, columns].astype(F32) + mixed[g * rows : (g + 1) * rows]
-            hidden[:, columns] = part
-            squares = squares + part * part
-        return squares
-    s = []
-    for head in range(heads_here):
-        if head % 2 == 0:
-            copies[10 + head].wait()
-            copies[11 + head].wait()
-        s.append(qk(head))
-    copies[8].wait()
-    copies[9].wait()
-    for head in range(heads_here):
-        squares = pv(head, soft(s[head]), squares)
-    square_row = to_row(jnp.sum(squares, axis=1, keepdims=True), rows)
-
-    scaled = (hidden[...] * gain[...]).astype(BF16)
-    lows, mixes = [], []
+        return jnp.concatenate([queries[:, base + g * HD : base + (g + 1) * HD] for g in range(group)], axis=0)
+
+    def finish(columns, attended):
+        hidden[:, columns] = residual[:, columns].astype(F32) + attended
+
+    attend(query_of, new_kv, pool, penalty, waits[3:], finish)
+
+
+def slots_kernel(hosted, *refs):
+    sources, (kept, other), held, (hidden, sems) = refs[:11], refs[11:13], refs[13:24], refs[24:]
+    counts, tails, order, routes, mig_pages, mig_dest, queries, new_kv, residual, gain, pool = held
+    waits = load(sources, held, sems, 6)
+    rows, tokens = queries.shape[0], pool.shape[0]
+    heads_here = pool.shape[1] // (2 * HD)
+    group = queries.shape[1] // (heads_here * HD)
+
+    row_a, row_b = iota((rows, rows), 0), iota((rows, rows), 1)
+    maps, mixed = [], None
     for expert in range(hosted):
         member_row = members(routes[...], expert)
-        member = to_column(member_row, rows)
-        rank = jnp.sum(jnp.where(row_a <= row_b, member, 0.0), axis=0, keepdims=True) - 1.0
+        rank = jnp.sum(jnp.where(row_a <= row_b, to_column(member_row, rows), 0.0), axis=0, keepdims=True) - 1.0
         rank = jnp.where(member_row > 0.0, rank, -2.0)
-        lows.append(rank == iota((LO, rows), 0).astype(F32))
-        mixes.append([rank == mix_slots((LO, rows), 0, part) for part in range(2)])
-    picked = []
-    for part in range(2):
-        maps = [jnp.where(m, 1.0, 0.0) for m in lows] + [jnp.where(m[part], 1.0, 0.0) for m in mixes]
-        stacked = jnp.concatenate(maps, axis=0).astype(BF16)
-        picked.append(dot(stacked, scaled[:, part * QUARTER : (part + 1) * QUARTER]))
+        maps.append(jnp.where(rank == iota((LO, rows), 0).astype(F32), 1.0, 0.0))
+        part = jnp.where(rank == mix_slots((LO, rows), 0, expert), 1.0, 0.0)
+        mixed = part if mixed is None else mixed + part
+    chosen = jnp.concatenate(maps + [mixed], axis=0).astype(BF16)
+    slots = chosen.shape[0]
+    held_here = dot(chosen, tokens_held(counts, tails, rows, tokens // PAGE).astype(BF16))
+    penalty = hide_foreign(held_here, order, tokens)
+    for copy in waits[:4]:
+        copy.wait()
+    newest = dot(chosen, new_kv[...]).astype(BF16)
+    hidden[...] = dot(chosen, residual[...])
+    squares = [jnp.zeros((slots, HD), F32)]
+
+    def query_of(head):
+        picked = dot(chosen, queries[:, head * group * HD : (head + 1) * group * HD])
+        return jnp.concatenate([picked[:, g * HD : (g + 1) * HD] for g in range(group)], axis=0).astype(BF16)
+
+    def finish(columns, attended):
+        part = hidden[:, columns] + attended
+        hidden[:, columns] = part * gain[:, columns]
+        squares[0] = squares[0] + part * part
+
+    attend(query_of, newest, pool, penalty, waits[4:], finish)
+
+    sums = jnp.sum(squares[0], axis=1, keepdims=True) + jnp.zeros((slots, LANES), F32)
+    upper = iota((LO, 1), 0) < 4
+    tail_rows, tail_sums = hidden[hosted * LO :, :], sums[hosted * LO :]
     lane = iota((LO, LANES), 1)
     by_expert = []
     for expert in range(hosted):
-        low_at, mix_at = expert * LO, (hosted + expert) * LO
-        low_sum = jnp.sum(jnp.where(lows[expert], square_row, 0.0), axis=1, keepdims=True)
-        mix_map = mixes[expert][0] | mixes[expert][1]
-        mix_sum = jnp.sum(jnp.where(mix_map, square_row, 0.0), axis=1, keepdims=True)
+
+        def spread(first, second):
+            if expert == 0:
+                return jnp.where(upper, first, pltpu.roll(second, 4, 0))
+            return jnp.where(upper, pltpu.roll(first, 4, 0), second)
+
+        low = hidden[expert * LO : (expert + 1) * LO, :]
+        mix = spread(tail_rows[:, :QUARTER], tail_rows[:, QUARTER:])
         extra = jnp.zeros((LO, LANES), F32)
-        for at, piece in enumerate(split_three(low_sum) + split_three(mix_sum)):
+        pieces = split_three(sums[expert * LO : (expert + 1) * LO]) + split_three(spread(tail_sums, tail_sums))
+        for at, piece in enumerate(pieces):
             extra = jnp.where(lane == at, piece, extra)
-        low_rows = [picked[part][low_at : low_at + LO] for part in range(2)]
-        mixed_rows = picked[0][mix_at : mix_at + LO] + picked[1][mix_at : mix_at + LO]
-        by_expert.append(jnp.concatenate(low_rows + [mixed_rows, extra], axis=1))
+        by_expert.append(jnp.concatenate([low, mix, extra], axis=1))
     first_half = lax.axis_index("expert") == 0
     extra_at = SLOT_COLS + LANES
     mine = jnp.where(first_half, by_expert[0], by_expert[1])
@@ -314,6 +346,11 @@
             @pl.when((slot >= 0) & (slot < entries))
             def _():
                 arrived[slot] = block[:, at : at + page_width]
+
+
+def gather_kernel(core, own, arrived, jumped, out):
+    extra = jnp.where(lax.axis_index("expert") == core, jumped[...].astype(F32), 0.0)
+    out[...] = (own[...].astype(F32) + arrived[...].astype(F32) + extra).astype(BF16)
 
 
 def finish_kernel(own, from_left, from_right, mine, other):
@@ -406,38 +443,36 @@
     around = ring_order(n)
     right = [(around[i], around[(i + 1) % n]) for i in range(n)]
     left = [(b, a) for a, b in right]
+    reach = n // 2 - 1
+    jump = [(around[i] * hosted, around[(i + reach) % n] * hosted) for i in range(n)]
+    jump += [(around[i] * hosted + 1, around[(i - reach) % n] * hosted + 1) for i in range(n)]
     swap = [(0, 1), (1, 0)]
     shape = jax.ShapeDtypeStruct
 
     moved_cols = entries * page_width + LANES
-    sources = (
-        page_counts,
-        tail_tokens.reshape(1, -1),
-        page_order,
-        routes.T,
-        mig_pages,
-        mig_dest,
-        queries,
-        new_kv,
-        residual,
-        norm_gain.reshape(1, -1),
-        pool,
-    )
-    spaces = [pltpu.VMEM] * 4 + [pltpu.SMEM] * 2 + [pltpu.VMEM] * 5
-    hidden, kept, other = call(
-        functools.partial(attend_kernel, hosted),
-        [
-            shape((rows, width), F32),
-            shape((2 * LO, SLOT_COLS + LANES + moved_cols), BF16),
-            shape((LO, SLOT_COLS + LANES), BF16),
-        ],
-        [HBM] * len(sources),
-        sources,
-        scratch=[space(x.shape, x.dtype) for space, x in zip(spaces, sources)]
-        + [pltpu.SemaphoreType.DMA((len(sources) + page_width // (2 * HD),))],
-        flops=500_000_000,
-        bytes_accessed=3_500_000,
-        vmem=60 << 20,
+    lengths = (page_counts, tail_tokens.reshape(1, -1), page_order)
+    spaces = {mig_pages.shape: pltpu.SMEM}
+
+    def attention(kernel, outs, sources, scratch, flops):
+        held = [spaces.get(x.shape, pltpu.VMEM)(x.shape, x.dtype) for x in sources]
+        sems = pltpu.SemaphoreType.DMA((len(sources) + page_width // (2 * HD),))
+        return call(
+            kernel,
+            outs,
+            [HBM] * len(sources),
+            sources,
+            scratch=held + scratch + [sems],
+            flops=flops,
+            bytes_accessed=3_500_000,
+            vmem=60 << 20,
+        )
+
+    kept, other = attention(
+        functools.partial(slots_kernel, hosted),
+        [shape((2 * LO, SLOT_COLS + LANES + moved_cols), BF16), shape((LO, SLOT_COLS + LANES), BF16)],
+        (*lengths, routes.T, mig_pages, mig_dest, queries, new_kv, residual, norm_gain.reshape(1, -1), pool),
+        [pltpu.VMEM((2 * CAP, width), F32)],
+        400_000_000,
     )
     tie = lax.optimization_barrier
     theirs = lax.ppermute(other, "expert", swap)
@@ -462,9 +497,19 @@
         if step == far - 1:
             a, b = a[:, :cut], b[:, cut:]
         a, b = lax.ppermute(a, "attn", right), lax.ppermute(b, "attn", left)
-        if step < len(stored):
-            weights.append(fetch(stored[step]))
-            a, weights[-1] = tie((a, weights[-1]))
+        if step == 0:
+            hidden = attention(
+                hidden_kernel,
+                shape((rows, width), F32),
+                (*lengths, queries, new_kv, residual, pool),
+                [],
+                4_000_000_000,
+            )
+            b, hidden = tie((b, hidden))
+        else:
+            for weight in stored[2 * step - 2 : 2 * step]:
+                weights.append(fetch(weight))
+                a, weights[-1] = tie((a, weights[-1]))
         from_left.append(a)
         from_right.append(b)
     last_a, last_b = from_left.pop(), from_right.pop()
@@ -488,36 +533,47 @@
         )
 
     outs = list(feed_forward(blocks, n - 1, None))
-    last_a, outs[0] = tie((last_a, outs[0]))
-    outs = outs + list(feed_forward((last_a, last_b), 1, cut))
-
     to_left = {k: outs[k] for k in range(1, far)}
     to_right = {k: outs[far - 1 + k] for k in range(1, far)}
-    split = SLOT_COLS // 2
-    going_right = lax.ppermute(outs[n - 1][:, :split], "attn", right)
-    going_left = lax.ppermute(outs[n - 1][:, split:], "attn", left)
-    arrived = call(
-        functools.partial(arrive_kernel, n, cut, page_width),
-        shape((entries, PAGE, page_width), BF16),
-        [VMEM] * (n + 1),
-        (*blocks, last_a, last_b),
-        scratch=(
-            pltpu.VMEM((n, LANES), jnp.int32),
-            pltpu.SMEM((n, LANES), jnp.int32),
-            pltpu.SemaphoreType.DMA,
-        ),
-        flops=100_000,
-        bytes_accessed=2_000_000,
-    )
-    going_right, arrived = tie((going_right, arrived))
+    going_right = going_left = jumped = None
+
+    def gather(core, *terms):
+        return call(
+            functools.partial(gather_kernel, core),
+            shape((2 * LO, SLOT_COLS), BF16),
+            [VMEM] * 3,
+            terms,
+            flops=300_000,
+            bytes_accessed=600_000,
+        )
+
     for k in range(far - 1, 0, -1):
-        if k == far - 1:
-            send_right = jnp.concatenate([add(to_right[k][:, :split], going_right), to_right[k][:, split:]], axis=1)
-            send_left = jnp.concatenate([to_left[k][:, :split], add(to_left[k][:, split:], going_left)], axis=1)
-        else:
-            send_right, send_left = add(to_right[k], going_right), add(to_left[k], going_left)
+        send_right, send_left = to_right[k], to_left[k]
+        if k == 1:
+            send_right, send_left = gather(0, send_right, going_right, jumped), gather(1, send_left, going_left, jumped)
+        elif k < far - 1:
+            send_right, send_left = add(send_right, going_right), add(send_left, going_left)
         going_right = lax.ppermute(send_right, "attn", right)
         going_left = lax.ppermute(send_left, "attn", left)
+        if k == far - 1:
+            (opposite,) = feed_forward((last_a, last_b), 1, cut)
+            going_right, opposite = tie((going_right, opposite))
+            jumped = lax.ppermute(opposite, ("attn", "expert"), jump)
+        if k == far - 2:
+            arrived = call(
+                functools.partial(arrive_kernel, n, cut, page_width),
+                shape((entries, PAGE, page_width), BF16),
+                [VMEM] * (n + 1),
+                (*blocks, last_a, last_b),
+                scratch=(
+                    pltpu.VMEM((n, LANES), jnp.int32),
+                    pltpu.SMEM((n, LANES), jnp.int32),
+                    pltpu.SemaphoreType.DMA,
+                ),
+                flops=100_000,
+                bytes_accessed=2_000_000,
+            )
+            going_left, arrived = tie((going_left, arrived))
     kept, other_half = call(
         finish_kernel,
         [shape((LO, SLOT_COLS), BF16)] * 2,

time: 61.8 us -> 60.5 us (0.979)
  waiting for transfers between devices: 28.6 us -> 20.5 us
  Pallas kernels: 12.6 us -> 17 us
  local copies, waits for them, and re-layouts: 1.01 us -> 2.64 us
  starting transfers between devices: 18.4 us -> 19.3 us
    ppermute x8, waiting for transfers between devices: 15.5 us -> 8.81 us  [per_device(): a, b = (lax.ppermute(a, 'attn', right), lax.ppermute(b, 'attn', left))]
    pallas_call x11 -> x14, Pallas kernels: 12.6 us -> 17 us  [call(): pl.pallas_call(kernel, out_shape=outs, in_specs=in_specs, out_specs=[VMEM...]
    ppermute x3, starting transfers between devices: 0.62 us -> 3.94 us  [per_device(): going_left = lax.ppermute(send_left, 'attn', left)]
    ppermute x3, waiting for transfers between devices: 9.04 us -> 5.72 us  [per_device(): going_right = lax.ppermute(send_right, 'attn', right)]
    ppermute x2 -> x1, waiting for transfers between devices: 0.72 us -> 3.26 us  [per_device(): jumped = lax.ppermute(opposite, ('attn', 'expert'), jump)]
    ppermute x3, starting transfers between devices: 5.77 us -> 3.59 us  [per_device(): going_right = lax.ppermute(send_right, 'attn', right)]
    unnamed x14, local copies, waits for them, and re-layouts: 0.97 us -> 2.63 us
    ppermute x3, waiting for transfers between devices: 1.99 us -> 1.24 us  [per_device(): going_left = lax.ppermute(send_left, 'attn', left)]
  transfers between devices with their start and end apart: 18 -> 17, of which waited for: 12 -> 11; matrix products, arithmetic and copies ran while one was open for 0% -> 0% of each run, Pallas kernels for 7% -> 18%
where the time goes in v4:
time: 60.5 us; the launch traced here: 60.2 us
  waiting for transfers between devices  20.5 us (34%)
  starting transfers between devices  19.3 us (32%)
  Pallas kernels  17 us (28%)
  local copies, waits for them, and re-layouts  2.64 us (4%)
  between operations  0.79 us (1%)
    pallas_call x14, Pallas kernels, call(): pl.pallas_call(kernel, out_shape=outs, in_specs=in_specs, out_specs=[VMEM...  17 us
    ppermute x8, starting transfers between devices, per_device(): a, b = (lax.ppermute(a, 'attn', right), lax.ppermute(b, 'attn', left))  9.3 us
    ppermute x8, waiting for transfers between devices, per_device(): a, b = (lax.ppermute(a, 'attn', right), lax.ppermute(b, 'attn', left))  8.81 us
    ppermute x3, waiting for transfers between devices, per_device(): going_right = lax.ppermute(send_right, 'attn', right)  5.72 us
    ppermute x3, starting transfers between devices, per_device(): going_left = lax.ppermute(send_left, 'attn', left)  3.94 us
    ppermute x3, starting transfers between devices, per_device(): going_right = lax.ppermute(send_right, 'attn', right)  3.59 us
    ppermute x1, waiting for transfers between devices, per_device(): jumped = lax.ppermute(opposite, ('attn', 'expert'), jump)  3.26 us
    unnamed x14, local copies, waits for them, and re-layouts  2.63 us
  transfers between devices with their start and end apart: 17, of which 11 were waited for; matrix products, arithmetic and copies ran while one was open for 0% of the time, Pallas kernels for 18%

profile of v4, /device:TPU:0, one launch (start us, length us, event | category | flops | bytes accessed | tf_op | source)
XLA Modules:
  0.0 60.2 jit_solution(12888772987449346842)
XLA Ops:
  0.6 4.7 %shard_map.158 = (bf16[16,6912]{1,0:T(8,128)(2,1)}, bf16[8,4736]{1,0:T(8,128)(2,1)}) custom-call(s32[1,32]{1,0:T(1,128)} %refs_0_.3, s32[1,32]{1,0:T(1,128)} %bitcast.17, s32[1,72]{1,0:T(1,128)} %refs_2_.3, s32[2,32]{1,0:T(2,128)} %bitcast.11, s32[1,2]{1,0:T(1,128)} %refs_4_.2, s32[1,2]{1,0:T(1,128)} %refs_5_.2, bf16[32,3072]{1,0:T(8,128)(2,1)} %refs_3_.1, ...), custom_call_target="tpu_custom_call" | custom-call | flops 400000000 | bytes 3500000 | tf_op jit(solution)/shard_map/pallas_call | solution.py:390
  5.3 0.5 collective-permute-start
  5.8 0.9 %copy-done.4 = bf16[16,6912]{1,0:T(8,128)(2,1)S(1)} copy-done((bf16[16,6912]{1,0:T(8,128)(2,1)S(1)}, bf16[16,6912]{1,0:T(8,128)(2,1)}, u32[]{:S(2)}) %copy-start.4) | copy-done | bytes 221208
  6.8 0.2 collective-permute-done.theirs
  7.0 0.1 shard_map.160.refs_0_
  7.1 0.0 copy-start
  7.1 3.0 %collective-permute-start.2 = (bf16[16,6784]{1,0:T(8,128)(2,1)S(1)}, bf16[16,6784]{1,0:T(8,128)(2,1)S(1)}, u32[]{:S(2)}, u32[]{:S(2)}) collective-permute-start(bf16[16,6784]{1,0:T(8,128)(2,1)S(1)} %shard_map.160.refs_0_), channel_id=1, source_target_pairs={{0,4},{4,8},{8,12},{12,14},{14,10},{10,6},{6,2},{2,0},{1,5},{5,9},... | collective-permute-start | bytes 651272 | tf_op jit(solution)/shard_map/ppermute | solution.py:499
  10.1 0.0 collective-permute-start.1
  10.1 4.7 %shard_map.161.hidden = f32[32,3072]{1,0:T(8,128)} custom-call(s32[1,32]{1,0:T(1,128)} %refs_0_.3, s32[1,32]{1,0:T(1,128)} %bitcast.18, s32[1,72]{1,0:T(1,128)} %refs_2_.3, bf16[32,3072]{1,0:T(8,128)(2,1)} %refs_3_.1, bf16[32,1024]{1,0:T(8,128)(2,1)} %refs_4_.3, bf16[32,3072]{1,0:T(8,128)(2,1)} %refs_5_.3, bf16[1152,1024]{1,0:T(8,128)(2,1)} %bitcast.15), custom_call_target="tpu_custom_call" | custom-call | flops 4000000000 | bytes 3500000 | tf_op jit(solution)/shard_map/pallas_call | solution.py:390
  14.8 0.9 %collective-permute-done.2.refs_1_ = bf16[16,6784]{1,0:T(8,128)(2,1)S(1)} collective-permute-done((bf16[16,6784]{1,0:T(8,128)(2,1)S(1)}, bf16[16,6784]{1,0:T(8,128)(2,1)S(1)}, u32[]{:S(2)}, u32[]{:S(2)}) %collective-permute-start.2) | collective-permute-done | bytes 217120 | tf_op jit(solution)/shard_map/ppermute | solution.py:499
  15.7 1.8 %collective-permute-start.3 = (bf16[16,6784]{1,0:T(8,128)(2,1)S(1)}, bf16[16,6784]{1,0:T(8,128)(2,1)S(1)}, u32[]{:S(2)}, u32[]{:S(2)}) collective-permute-start(bf16[16,6784]{1,0:T(8,128)(2,1)S(1)} %collective-permute-done.2.refs_1_), channel_id=1, source_target_pairs={{0,4},{4,8},{8,12},{12,14},{14,10},{10,6},{6,2},{2,0},{1,5},{5,9},... | collective-permute-start | bytes 651272 | tf_op jit(solution)/shard_map/ppermute | solution.py:499
  17.5 0.0 collective-permute-done.1.refs_4_
  17.5 0.2 collective-permute-start.5
  17.7 0.2 shard_map.162.refs_7_.refs_2_
  17.9 1.7 %copy-done.1 = bf16[1,6144,256]{2,1,0:T(8,128)(2,1)S(1)} copy-done((bf16[1,6144,256]{2,1,0:T(8,128)(2,1)S(1)}, bf16[1,6144,256]{2,1,0:T(8,128)(2,1)}, u32[]{:S(2)}) %copy-start.1) | copy-done | bytes 3145752
  19.6 0.2 shard_map.163.refs_8_.refs_3_
  19.8 2.7 %collective-permute-done.3.refs_2_ = bf16[16,6784]{1,0:T(8,128)(2,1)S(1)} collective-permute-done((bf16[16,6784]{1,0:T(8,128)(2,1)S(1)}, bf16[16,6784]{1,0:T(8,128)(2,1)S(1)}, u32[]{:S(2)}, u32[]{:S(2)}) %collective-permute-start.3) | collective-permute-done | bytes 217120 | tf_op jit(solution)/shard_map/ppermute | solution.py:499
  22.6 1.2 %collective-permute-done.5.refs_5_ = bf16[16,6784]{1,0:T(8,128)(2,1)S(1)} collective-permute-done((bf16[16,6784]{1,0:T(8,128)(2,1)S(1)}, bf16[16,6784]{1,0:T(8,128)(2,1)S(1)}, u32[]{:S(2)}, u32[]{:S(2)}) %collective-permute-start.5) | collective-permute-done | bytes 217120 | tf_op jit(solution)/shard_map/ppermute | solution.py:499
  23.8 0.5 collective-permute-start.6
  24.3 1.5 %collective-permute-start.4 = (bf16[16,6784]{1,0:T(8,128)(2,1)S(1)}, bf16[16,6784]{1,0:T(8,128)(2,1)S(1)}, u32[]{:S(2)}, u32[]{:S(2)}) collective-permute-start(bf16[16,6784]{1,0:T(8,128)(2,1)S(1)} %collective-permute-done.3.refs_2_), channel_id=1, source_target_pairs={{0,4},{4,8},{8,12},{12,14},{14,10},{10,6},{6,2},{2,0},{1,5},{5,9},... | collective-permute-start | bytes 651272 | tf_op jit(solution)/shard_map/ppermute | solution.py:499
  25.8 0.2 shard_map.164.refs_9_.refs_4_
  26.0 3.9 %collective-permute-done.6.refs_6_ = bf16[16,6784]{1,0:T(8,128)(2,1)S(1)} collective-permute-done((bf16[16,6784]{1,0:T(8,128)(2,1)S(1)}, bf16[16,6784]{1,0:T(8,128)(2,1)S(1)}, u32[]{:S(2)}, u32[]{:S(2)}) %collective-permute-start.6) | collective-permute-done | bytes 217120 | tf_op jit(solution)/shard_map/ppermute | solution.py:499
  30.0 0.3 collective-permute-start.9
  30.3 0.0 collective-permute-done.4.refs_3_
  30.3 2.0 %collective-permute-start.8 = (bf16[16,3456]{1,0:T(8,128)(2,1)S(1)}, bf16[16,3456]{1,0:T(8,128)(2,1)S(1)}, u32[]{:S(2)}, u32[]{:S(2)}) collective-permute-start(bf16[16,3456]{1,0:T(8,128)(2,1)S(1)} %slice.6), channel_id=1, source_target_pairs={{0,4},{4,8},{8,12},{12,14},{14,10},{10,6},{6,2},{2,0},{1,5},{5,9},... | collective-permute-start | bytes 331784 | tf_op jit(solution)/shard_map/ppermute | solution.py:499
  32.3 2.3 %shard_map.165 = (bf16[16,4608]{1,0:T(8,128)(2,1)S(1)}, bf16[16,4608]{1,0:T(8,128)(2,1)S(1)}, bf16[16,4608]{1,0:T(8,128)(2,1)S(1)}, bf16[16,4608]{1,0:T(8,128)(2...) custom-call(bf16[16,6784]{1,0:T(8,128)(2,1)S(1)} %shard_map.160.refs_0_, ...), custom_call_target="tpu_custom_call" | custom-call | flops 2000000000 | bytes 8000000 | tf_op jit(solution)/shard_map/pallas_call | solution.py:390
  34.5 1.6 %collective-permute-start.7 = (bf16[16,4608]{1,0:T(8,128)(2,1)S(1)}, bf16[16,4608]{1,0:T(8,128)(2,1)S(1)}, u32[]{:S(2)}, u32[]{:S(2)}) collective-permute-start(bf16[16,4608]{1,0:T(8,128)(2,1)S(1)} %get-tuple-element.42), channel_id=1, source_target_pairs={{0,4},{4,8},{8,12},{12,14},{14,10},{10,6},{6,2},{2,0},{1,5},{5,9},... | collective-permute-start | bytes 442376 | tf_op jit(solution)/shard_map/ppermute | solution.py:556
  36.2 0.4 collective-permute-start.13
  36.6 1.7 %shard_map.166 = bf16[16,4608]{1,0:T(8,128)(2,1)S(1)} custom-call(bf16[16,3456]{1,0:T(8,128)(2,1)S(1)} %collective-permute-done.8.refs_0_.refs_7_, bf16[16,3328]{1,0:T(8,128)(2,1)S(1)} %collective-permute-done.9.refs_1_.refs_8_, bf16[6144,256]{1,0:T(8,128)(2,1)S(1)} %shard_map.162.refs_7_.refs_2_, bf16[6144,256]{1,0:T(8,128)(2,1)S(1)} %shard_map.163.refs_8_.refs_3_, ...), custom_call_target="tpu_custom_call" | custom-call | flops 2000000000 | bytes 8000000 | tf_op jit(solution)/shard_map/pallas_call | solution.py:390
  38.3 0.0 copy-start.6
  38.3 2.7 %collective-permute-done.7 = bf16[16,4608]{1,0:T(8,128)(2,1)S(1)} collective-permute-done((bf16[16,4608]{1,0:T(8,128)(2,1)S(1)}, bf16[16,4608]{1,0:T(8,128)(2,1)S(1)}, u32[]{:S(2)}, u32[]{:S(2)}) %collective-permute-start.7) | collective-permute-done | bytes 147488 | tf_op jit(solution)/shard_map/ppermute | solution.py:556
  41.1 1.9 %collective-permute-start.10 = (bf16[16,4608]{1,0:T(8,128)(2,1)S(1)}, bf16[16,4608]{1,0:T(8,128)(2,1)S(1)}, u32[]{:S(2)}, u32[]{:S(2)}) collective-permute-start(bf16[16,4608]{1,0:T(8,128)(2,1)S(1)} %add_convert_fusion.1), channel_id=1, source_target_pairs={{0,4},{4,8},{8,12},{12,14},{14,10},{10,6},{6,2},{2,0},{1,5},{5,9},... | collective-permute-start | bytes 442376 | tf_op jit(solution)/shard_map/ppermute | solution.py:556
  43.0 1.9 %collective-permute-start.11 = (bf16[16,4608]{1,0:T(8,128)(2,1)S(1)}, bf16[16,4608]{1,0:T(8,128)(2,1)S(1)}, u32[]{:S(2)}, u32[]{:S(2)}) collective-permute-start(bf16[16,4608]{1,0:T(8,128)(2,1)S(1)} %shard_map.166), channel_id=1, source_target_pairs={{0,12},{4,14},{8,10},{12,6},{14,2},{10,0},{6,4},{2,8},{1,11},{5,7}... | collective-permute-start | bytes 442376 | tf_op jit(solution)/shard_map/ppermute | solution.py:561
  44.9 0.7 %collective-permute-done.13 = bf16[16,4608]{1,0:T(8,128)(2,1)S(1)} collective-permute-done((bf16[16,4608]{1,0:T(8,128)(2,1)S(1)}, bf16[16,4608]{1,0:T(8,128)(2,1)S(1)}, u32[]{:S(2)}, u32[]{:S(2)}) %collective-permute-start.13) | collective-permute-done | bytes 147488 | tf_op jit(solution)/shard_map/ppermute | solution.py:557
  45.6 1.4 %collective-permute-start.14 = (bf16[16,4608]{1,0:T(8,128)(2,1)S(1)}, bf16[16,4608]{1,0:T(8,128)(2,1)S(1)}, u32[]{:S(2)}, u32[]{:S(2)}) collective-permute-start(bf16[16,4608]{1,0:T(8,128)(2,1)S(1)} %add_convert_fusion), channel_id=1, source_target_pairs={{4,0},{8,4},{12,8},{14,12},{10,14},{6,10},{2,6},{0,2},{5,1},{9,5},... | collective-permute-start | bytes 442376 | tf_op jit(solution)/shard_map/ppermute | solution.py:557
  47.1 1.6 %shard_map.168 = bf16[2,16,1024]{2,1,0:T(8,128)(2,1)} custom-call(bf16[16,6784]{1,0:T(8,128)(2,1)S(1)} %shard_map.160.refs_0_, bf16[16,6784]{1,0:T(8,128)(2,1)S(1)} %collective-permute-done.2.refs_1_, bf16[16,6784]{1,0:T(8,128)(2,1)S(1)} %collective-permute-done.3.refs_2_, bf16[16,6784]{1,0:T(8,128)(2,1)S(1)} %collective-permute-done.4.refs_3_, ...), custom_call_target="tpu_custom_call" | custom-call | flops 100000 | bytes 2000000 | tf_op jit(solution)/shard_map/pallas_call | solution.py:390
  48.6 0.0 collective-permute-done.10.arrived
  48.7 3.3 %collective-permute-done.11.jumped = bf16[16,4608]{1,0:T(8,128)(2,1)S(1)} collective-permute-done((bf16[16,4608]{1,0:T(8,128)(2,1)S(1)}, bf16[16,4608]{1,0:T(8,128)(2,1)S(1)}, u32[]{:S(2)}, u32[]{:S(2)}) %collective-permute-start.11) | collective-permute-done | bytes 147488 | tf_op jit(solution)/shard_map/ppermute | solution.py:561
  51.9 0.1 shard_map.167
  52.0 0.1 collective-permute-start.12
  52.1 0.1 shard_map.169
  52.1 2.1 %collective-permute-start.15 = (bf16[16,4608]{1,0:T(8,128)(2,1)S(1)}, bf16[16,4608]{1,0:T(8,128)(2,1)S(1)}, u32[]{:S(2)}, u32[]{:S(2)}) collective-permute-start(bf16[16,4608]{1,0:T(8,128)(2,1)S(1)} %shard_map.169), channel_id=1, source_target_pairs={{4,0},{8,4},{12,8},{14,12},{10,14},{6,10},{2,6},{0,2},{5,1},{9,5},... | collective-permute-start | bytes 442376 | tf_op jit(solution)/shard_map/ppermute | solution.py:557
  54.2 3.0 %collective-permute-done.12.from_left = bf16[16,4608]{1,0:T(8,128)(2,1)S(1)} collective-permute-done((bf16[16,4608]{1,0:T(8,128)(2,1)S(1)}, bf16[16,4608]{1,0:T(8,128)(2,1)S(1)}, u32[]{:S(2)}, u32[]{:S(2)}) %collective-permute-start.12) | collective-permute-done | bytes 147488 | tf_op jit(solution)/shard_map/ppermute | solution.py:556
  57.2 0.5 collective-permute-done.15.from_right
  57.7 0.1 shard_map.170
  57.8 0.1 collective-permute-start.16
  57.8 1.3 %collective-permute-done.16.theirs = bf16[8,4608]{1,0:T(8,128)(2,1)S(1)} collective-permute-done((bf16[8,4608]{1,0:T(8,128)(2,1)S(1)}, bf16[8,4608]{1,0:T(8,128)(2,1)S(1)}, u32[]{:S(2)}, u32[]{:S(2)}) %collective-permute-start.16) | collective-permute-done | bytes 73760 | tf_op jit(solution)/shard_map/ppermute | solution.py:585
  59.1 1.1 %shard_map.171 = bf16[32,3072]{1,0:T(8,128)(2,1)} custom-call(f32[32,3072]{1,0:T(8,128)S(1)} %copy-done.3, bf16[8,4608]{1,0:T(8,128)(2,1)S(1)} %get-tuple-element.49.mine, bf16[8,4608]{1,0:T(8,128)(2,1)S(1)} %collective-permute-done.16.theirs, s32[2,32]{1,0:T(2,128)S(1)} %bitcast.12, f32[2,32]{1,0:T(2,128)S(1)} %bitcast.13), custom_call_target="tpu_custom_call" | custom-call | flops 20000000 | bytes 800000 | tf_op jit(solution)/shard_map/pallas_call | solution.py:390
  (18 shorter events, 0.1 us)
Async XLA Ops:
  5.3 1.7 %collective-permute-start = (bf16[8,4736]{1,0:T(8,128)(2,1)}, bf16[8,4736]{1,0:T(8,128)(2,1)S(1)}, u32[]{:S(2)}, u32[]{:S(2)}) collective-permute-start(bf16[8,4736]{1,0:T(8,128)(2,1)} %get-tuple-element.27), channel_id=1, source_target_pairs={{0,1},{1,0},{2,3},{3,2},{4,5},{5,4},{6,7},{7,6},{8,9},{9,8},{10,11... | collective-permute-start | bytes 227336 | tf_op jit(solution)/shard_map/ppermute | solution.py:478
  5.8 0.9 %copy-start.4 = (bf16[16,6912]{1,0:T(8,128)(2,1)S(1)}, bf16[16,6912]{1,0:T(8,128)(2,1)}, u32[]{:S(2)}) copy-start(bf16[16,6912]{1,0:T(8,128)(2,1)} %get-tuple-element.28.source) | copy-start | bytes 663556
  7.1 10.6 %copy-start = (bf16[1,6144,256]{2,1,0:T(8,128)(2,1)S(1)}, bf16[1,6144,256]{2,1,0:T(8,128)(2,1)}, u32[]{:S(2)}) copy-start(bf16[1,6144,256]{2,1,0:T(8,128)(2,1)} %param.25) | copy-start | bytes 9437188
  7.1 8.6 %collective-permute-start.2 = (bf16[16,6784]{1,0:T(8,128)(2,1)S(1)}, bf16[16,6784]{1,0:T(8,128)(2,1)S(1)}, u32[]{:S(2)}, u32[]{:S(2)}) collective-permute-start(bf16[16,6784]{1,0:T(8,128)(2,1)S(1)} %shard_map.160.refs_0_), channel_id=1, source_target_pairs={{0,4},{4,8},{8,12},{12,14},{14,10},{10,6},{6,2},{2,0},{1,5},{5,9},... | collective-permute-start | bytes 651272 | tf_op jit(solution)/shard_map/ppermute | solution.py:499
  10.1 7.4 %collective-permute-start.1 = (bf16[16,6784]{1,0:T(8,128)(2,1)S(1)}, bf16[16,6784]{1,0:T(8,128)(2,1)S(1)}, u32[]{:S(2)}, u32[]{:S(2)}) collective-permute-start(bf16[16,6784]{1,0:T(8,128)(2,1)S(1)} %shard_map.160.refs_0_), channel_id=1, source_target_pairs={{4,0},{8,4},{12,8},{14,12},{10,14},{6,10},{2,6},{0,2},{5,1},{9,5},... | collective-permute-start | bytes 651272 | tf_op jit(solution)/shard_map/ppermute | solution.py:499
  15.7 6.9 %collective-permute-start.3 = (bf16[16,6784]{1,0:T(8,128)(2,1)S(1)}, bf16[16,6784]{1,0:T(8,128)(2,1)S(1)}, u32[]{:S(2)}, u32[]{:S(2)}) collective-permute-start(bf16[16,6784]{1,0:T(8,128)(2,1)S(1)} %collective-permute-done.2.refs_1_), channel_id=1, source_target_pairs={{0,4},{4,8},{8,12},{12,14},{14,10},{10,6},{6,2},{2,0},{1,5},{5,9},... | collective-permute-start | bytes 651272 | tf_op jit(solution)/shard_map/ppermute | solution.py:499
  17.5 6.3 %collective-permute-start.5 = (bf16[16,6784]{1,0:T(8,128)(2,1)S(1)}, bf16[16,6784]{1,0:T(8,128)(2,1)S(1)}, u32[]{:S(2)}, u32[]{:S(2)}) collective-permute-start(bf16[16,6784]{1,0:T(8,128)(2,1)S(1)} %collective-permute-done.1.refs_4_), channel_id=1, source_target_pairs={{4,0},{8,4},{12,8},{14,12},{10,14},{6,10},{2,6},{0,2},{5,1},{9,5},... | collective-permute-start | bytes 651272 | tf_op jit(solution)/shard_map/ppermute | solution.py:499
  17.7 1.9 %copy-start.1 = (bf16[1,6144,256]{2,1,0:T(8,128)(2,1)S(1)}, bf16[1,6144,256]{2,1,0:T(8,128)(2,1)}, u32[]{:S(2)}) copy-start(bf16[1,6144,256]{2,1,0:T(8,128)(2,1)} %param.26) | copy-start | bytes 9437188
  19.6 6.2 %copy-start.2 = (bf16[1,256,6144]{2,1,0:T(8,128)(2,1)S(1)}, bf16[1,256,6144]{2,1,0:T(8,128)(2,1)}, u32[]{:S(2)}) copy-start(bf16[1,256,6144]{2,1,0:T(8,128)(2,1)} %param.27) | copy-start | bytes 9437188
  23.8 6.2 %collective-permute-start.6 = (bf16[16,6784]{1,0:T(8,128)(2,1)S(1)}, bf16[16,6784]{1,0:T(8,128)(2,1)S(1)}, u32[]{:S(2)}, u32[]{:S(2)}) collective-permute-start(bf16[16,6784]{1,0:T(8,128)(2,1)S(1)} %collective-permute-done.5.refs_5_), channel_id=1, source_target_pairs={{4,0},{8,4},{12,8},{14,12},{10,14},{6,10},{2,6},{0,2},{5,1},{9,5},... | collective-permute-start | bytes 651272 | tf_op jit(solution)/shard_map/ppermute | solution.py:499
  24.3 6.0 %collective-permute-start.4 = (bf16[16,6784]{1,0:T(8,128)(2,1)S(1)}, bf16[16,6784]{1,0:T(8,128)(2,1)S(1)}, u32[]{:S(2)}, u32[]{:S(2)}) collective-permute-start(bf16[16,6784]{1,0:T(8,128)(2,1)S(1)} %collective-permute-done.3.refs_2_), channel_id=1, source_target_pairs={{0,4},{4,8},{8,12},{12,14},{14,10},{10,6},{6,2},{2,0},{1,5},{5,9},... | collective-permute-start | bytes 651272 | tf_op jit(solution)/shard_map/ppermute | solution.py:499
  30.0 6.6 %collective-permute-start.9 = (bf16[16,3328]{1,0:T(8,128)(2,1)S(1)}, bf16[16,3328]{1,0:T(8,128)(2,1)S(1)}, u32[]{:S(2)}, u32[]{:S(2)}) collective-permute-start(bf16[16,3328]{1,0:T(8,128)(2,1)S(1)} %slice.8), channel_id=1, source_target_pairs={{4,0},{8,4},{12,8},{14,12},{10,14},{6,10},{2,6},{0,2},{5,1},{9,5},... | collective-permute-start | bytes 319496 | tf_op jit(solution)/shard_map/ppermute | solution.py:499
  30.3 6.3 %collective-permute-start.8 = (bf16[16,3456]{1,0:T(8,128)(2,1)S(1)}, bf16[16,3456]{1,0:T(8,128)(2,1)S(1)}, u32[]{:S(2)}, u32[]{:S(2)}) collective-permute-start(bf16[16,3456]{1,0:T(8,128)(2,1)S(1)} %slice.6), channel_id=1, source_target_pairs={{0,4},{4,8},{8,12},{12,14},{14,10},{10,6},{6,2},{2,0},{1,5},{5,9},... | collective-permute-start | bytes 331784 | tf_op jit(solution)/shard_map/ppermute | solution.py:499
  34.5 6.5 %collective-permute-start.7 = (bf16[16,4608]{1,0:T(8,128)(2,1)S(1)}, bf16[16,4608]{1,0:T(8,128)(2,1)S(1)}, u32[]{:S(2)}, u32[]{:S(2)}) collective-permute-start(bf16[16,4608]{1,0:T(8,128)(2,1)S(1)} %get-tuple-element.42), channel_id=1, source_target_pairs={{0,4},{4,8},{8,12},{12,14},{14,10},{10,6},{6,2},{2,0},{1,5},{5,9},... | collective-permute-start | bytes 442376 | tf_op jit(solution)/shard_map/ppermute | solution.py:556
  36.2 9.4 %collective-permute-start.13 = (bf16[16,4608]{1,0:T(8,128)(2,1)S(1)}, bf16[16,4608]{1,0:T(8,128)(2,1)S(1)}, u32[]{:S(2)}, u32[]{:S(2)}) collective-permute-start(bf16[16,4608]{1,0:T(8,128)(2,1)S(1)} %get-tuple-element.47), channel_id=1, source_target_pairs={{4,0},{8,4},{12,8},{14,12},{10,14},{6,10},{2,6},{0,2},{5,1},{9,5},... | collective-permute-start | bytes 442376 | tf_op jit(solution)/shard_map/ppermute | solution.py:557
  38.3 20.8 %copy-start.3 = (f32[32,3072]{1,0:T(8,128)S(1)}, f32[32,3072]{1,0:T(8,128)}, u32[]{:S(2)}) copy-start(f32[32,3072]{1,0:T(8,128)} %shard_map.161.hidden) | copy-start | bytes 1179652
  38.3 20.8 %copy-start.5 = (s32[32,2]{0,1:T(2,128)S(1)}, s32[32,2]{0,1:T(2,128)}, u32[]{:S(2)}) copy-start(s32[32,2]{0,1:T(2,128)} %param.23) | copy-start | bytes 772
  38.3 20.8 %copy-start.6 = (f32[32,2]{0,1:T(2,128)S(1)}, f32[32,2]{0,1:T(2,128)}, u32[]{:S(2)}) copy-start(f32[32,2]{0,1:T(2,128)} %param.24) | copy-start | bytes 772
  41.1 7.5 %collective-permute-start.10 = (bf16[16,4608]{1,0:T(8,128)(2,1)S(1)}, bf16[16,4608]{1,0:T(8,128)(2,1)S(1)}, u32[]{:S(2)}, u32[]{:S(2)}) collective-permute-start(bf16[16,4608]{1,0:T(8,128)(2,1)S(1)} %add_convert_fusion.1), channel_id=1, source_target_pairs={{0,4},{4,8},{8,12},{12,14},{14,10},{10,6},{6,2},{2,0},{1,5},{5,9},... | collective-permute-start | bytes 442376 | tf_op jit(solution)/shard_map/ppermute | solution.py:556
  43.0 8.9 %collective-permute-start.11 = (bf16[16,4608]{1,0:T(8,128)(2,1)S(1)}, bf16[16,4608]{1,0:T(8,128)(2,1)S(1)}, u32[]{:S(2)}, u32[]{:S(2)}) collective-permute-start(bf16[16,4608]{1,0:T(8,128)(2,1)S(1)} %shard_map.166), channel_id=1, source_target_pairs={{0,12},{4,14},{8,10},{12,6},{14,2},{10,0},{6,4},{2,8},{1,11},{5,7}... | collective-permute-start | bytes 442376 | tf_op jit(solution)/shard_map/ppermute | solution.py:561
  45.6 6.4 %collective-permute-start.14 = (bf16[16,4608]{1,0:T(8,128)(2,1)S(1)}, bf16[16,4608]{1,0:T(8,128)(2,1)S(1)}, u32[]{:S(2)}, u32[]{:S(2)}) collective-permute-start(bf16[16,4608]{1,0:T(8,128)(2,1)S(1)} %add_convert_fusion), channel_id=1, source_target_pairs={{4,0},{8,4},{12,8},{14,12},{10,14},{6,10},{2,6},{0,2},{5,1},{9,5},... | collective-permute-start | bytes 442376 | tf_op jit(solution)/shard_map/ppermute | solution.py:557
  52.0 5.2 %collective-permute-start.12 = (bf16[16,4608]{1,0:T(8,128)(2,1)S(1)}, bf16[16,4608]{1,0:T(8,128)(2,1)S(1)}, u32[]{:S(2)}, u32[]{:S(2)}) collective-permute-start(bf16[16,4608]{1,0:T(8,128)(2,1)S(1)} %shard_map.167), channel_id=1, source_target_pairs={{0,4},{4,8},{8,12},{12,14},{14,10},{10,6},{6,2},{2,0},{1,5},{5,9},... | collective-permute-start | bytes 442376 | tf_op jit(solution)/shard_map/ppermute | solution.py:556
  52.1 5.6 %collective-permute-start.15 = (bf16[16,4608]{1,0:T(8,128)(2,1)S(1)}, bf16[16,4608]{1,0:T(8,128)(2,1)S(1)}, u32[]{:S(2)}, u32[]{:S(2)}) collective-permute-start(bf16[16,4608]{1,0:T(8,128)(2,1)S(1)} %shard_map.169), channel_id=1, source_target_pairs={{4,0},{8,4},{12,8},{14,12},{10,14},{6,10},{2,6},{0,2},{5,1},{9,5},... | collective-permute-start | bytes 442376 | tf_op jit(solution)/shard_map/ppermute | solution.py:557
  57.8 1.3 %collective-permute-start.16 = (bf16[8,4608]{1,0:T(8,128)(2,1)S(1)}, bf16[8,4608]{1,0:T(8,128)(2,1)S(1)}, u32[]{:S(2)}, u32[]{:S(2)}) collective-permute-start(bf16[8,4608]{1,0:T(8,128)(2,1)S(1)} %get-tuple-element.50), channel_id=1, source_target_pairs={{0,1},{1,0},{2,3},{3,2},{4,5},{5,4},{6,7},{7,6},{8,9},{9,8},{10,11... | collective-permute-start | bytes 221192 | tf_op jit(solution)/shard_map/ppermute | solution.py:585

commit v5 on v4

--- a/solution.py
+++ b/solution.py
@@ -444,8 +444,8 @@
     right = [(around[i], around[(i + 1) % n]) for i in range(n)]
     left = [(b, a) for a, b in right]
     reach = n // 2 - 1
-    jump = [(around[i] * hosted, around[(i + reach) % n] * hosted) for i in range(n)]
-    jump += [(around[i] * hosted + 1, around[(i - reach) % n] * hosted + 1) for i in range(n)]
+    jump = [(around[i] * hosted, around[(i + reach) % n] * hosted + 1) for i in range(n)]
+    jump += [(around[i] * hosted + 1, around[(i - reach) % n] * hosted) for i in range(n)]
     swap = [(0, 1), (1, 0)]
     shape = jax.ShapeDtypeStruct
 
@@ -509,7 +509,10 @@
         else:
             for weight in stored[2 * step - 2 : 2 * step]:
                 weights.append(fetch(weight))
-                a, weights[-1] = tie((a, weights[-1]))
+                if step == 2:
+                    a, weights[-1] = tie((a, weights[-1]))
+                else:
+                    b, weights[-1] = tie((b, weights[-1]))
         from_left.append(a)
         from_right.append(b)
     last_a, last_b = from_left.pop(), from_right.pop()
@@ -558,7 +561,7 @@
         if k == far - 1:
             (opposite,) = feed_forward((last_a, last_b), 1, cut)
             going_right, opposite = tie((going_right, opposite))
-            jumped = lax.ppermute(opposite, ("attn", "expert"), jump)
+            jumped = lax.ppermute(lax.ppermute(opposite, ("attn", "expert"), jump), "expert", swap)
         if k == far - 2:
             arrived = call(
                 functools.partial(arrive_kernel, n, cut, page_width),

time: 60.5 us -> 59.9 us (0.990)
  starting transfers between devices: 19.3 us -> 17.1 us
  waiting for transfers between devices: 20.5 us -> 22.1 us
    ppermute x3, starting transfers between devices: 3.94 us -> 1.54 us  [per_device(): going_left = lax.ppermute(send_left, 'attn', left)]
    ppermute x3, waiting for transfers between devices: 1.24 us -> 3.01 us  [per_device(): going_left = lax.ppermute(send_left, 'attn', left)]
    ppermute x3, starting transfers between devices: 3.59 us -> 4.8 us  [per_device(): going_right = lax.ppermute(send_right, 'attn', right)]
    ppermute x1 -> x2, starting transfers between devices: 1.86 us -> 0.88 us  [the longest x1 0.88 us: per_device(): lax.ppermute(lax.ppermute(opposite, ('attn', 'expert'), jump), 'expert',...]
    ppermute x1 -> x2, waiting for transfers between devices: 3.26 us -> 4.1 us  [the longest x1 4.1 us: per_device(): lax.ppermute(opposite, ('attn', 'expert'), jump)]
    ppermute x3, waiting for transfers between devices: 5.72 us -> 5.01 us  [per_device(): going_right = lax.ppermute(send_right, 'attn', right)]
  transfers between devices with their start and end apart: 17 -> 18, of which waited for: 11 -> 10; matrix products, arithmetic and copies ran while one was open for 0% -> 0% of each run, Pallas kernels for 18% -> 18%
where the time goes in v5:
time: 59.9 us; the launch traced here: 59.7 us
  waiting for transfers between devices  22.1 us (37%)
  starting transfers between devices  17.1 us (29%)
  Pallas kernels  16.9 us (28%)
  local copies, waits for them, and re-layouts  2.64 us (4%)
  between operations  0.79 us (1%)
    pallas_call x14, Pallas kernels, call(): pl.pallas_call(kernel, out_shape=outs, in_specs=in_specs, out_specs=[VMEM...  16.9 us
    ppermute x8, starting transfers between devices, per_device(): a, b = (lax.ppermute(a, 'attn', right), lax.ppermute(b, 'attn', left))  9.31 us
    ppermute x8, waiting for transfers between devices, per_device(): a, b = (lax.ppermute(a, 'attn', right), lax.ppermute(b, 'attn', left))  8.53 us
    ppermute x3, waiting for transfers between devices, per_device(): going_right = lax.ppermute(send_right, 'attn', right)  5.01 us
    ppermute x3, starting transfers between devices, per_device(): going_right = lax.ppermute(send_right, 'attn', right)  4.8 us
    ppermute x1, waiting for transfers between devices, per_device(): lax.ppermute(opposite, ('attn', 'expert'), jump)  4.1 us
    ppermute x3, waiting for transfers between devices, per_device(): going_left = lax.ppermute(send_left, 'attn', left)  3.01 us
    unnamed x14, local copies, waits for them, and re-layouts  2.63 us
  transfers between devices with their start and end apart: 18, of which 10 were waited for; matrix products, arithmetic and copies ran while one was open for 0% of the time, Pallas kernels for 18%

profile of v5, /device:TPU:0, one launch (start us, length us, event | category | flops | bytes accessed | tf_op | source)
XLA Modules:
  0.0 59.7 jit_solution(13274654992273979728)
XLA Ops:
  0.6 4.7 %shard_map.158 = (bf16[16,6912]{1,0:T(8,128)(2,1)}, bf16[8,4736]{1,0:T(8,128)(2,1)}) custom-call(s32[1,32]{1,0:T(1,128)} %refs_0_.3, s32[1,32]{1,0:T(1,128)} %bitcast.17, s32[1,72]{1,0:T(1,128)} %refs_2_.3, s32[2,32]{1,0:T(2,128)} %bitcast.11, s32[1,2]{1,0:T(1,128)} %refs_4_.2, s32[1,2]{1,0:T(1,128)} %refs_5_.2, bf16[32,3072]{1,0:T(8,128)(2,1)} %refs_3_.1, ...), custom_call_target="tpu_custom_call" | custom-call | flops 400000000 | bytes 3500000 | tf_op jit(solution)/shard_map/pallas_call | solution.py:390
  5.3 0.5 collective-permute-start
  5.8 0.9 %copy-done.4 = bf16[16,6912]{1,0:T(8,128)(2,1)S(1)} copy-done((bf16[16,6912]{1,0:T(8,128)(2,1)S(1)}, bf16[16,6912]{1,0:T(8,128)(2,1)}, u32[]{:S(2)}) %copy-start.4) | copy-done | bytes 221208
  6.8 0.2 collective-permute-done.theirs
  7.0 0.1 shard_map.160.refs_0_
  7.1 0.0 copy-start
  7.1 3.0 %collective-permute-start.2 = (bf16[16,6784]{1,0:T(8,128)(2,1)S(1)}, bf16[16,6784]{1,0:T(8,128)(2,1)S(1)}, u32[]{:S(2)}, u32[]{:S(2)}) collective-permute-start(bf16[16,6784]{1,0:T(8,128)(2,1)S(1)} %shard_map.160.refs_0_), channel_id=1, source_target_pairs={{0,4},{4,8},{8,12},{12,14},{14,10},{10,6},{6,2},{2,0},{1,5},{5,9},... | collective-permute-start | bytes 651272 | tf_op jit(solution)/shard_map/ppermute | solution.py:499
  10.1 0.0 collective-permute-start.1
  10.1 4.7 %shard_map.161.hidden = f32[32,3072]{1,0:T(8,128)} custom-call(s32[1,32]{1,0:T(1,128)} %refs_0_.3, s32[1,32]{1,0:T(1,128)} %bitcast.18, s32[1,72]{1,0:T(1,128)} %refs_2_.3, bf16[32,3072]{1,0:T(8,128)(2,1)} %refs_3_.1, bf16[32,1024]{1,0:T(8,128)(2,1)} %refs_4_.3, bf16[32,3072]{1,0:T(8,128)(2,1)} %refs_5_.3, bf16[1152,1024]{1,0:T(8,128)(2,1)} %bitcast.15), custom_call_target="tpu_custom_call" | custom-call | flops 4000000000 | bytes 3500000 | tf_op jit(solution)/shard_map/pallas_call | solution.py:390
  14.8 2.4 %collective-permute-done.1.refs_4_ = bf16[16,6784]{1,0:T(8,128)(2,1)S(1)} collective-permute-done((bf16[16,6784]{1,0:T(8,128)(2,1)S(1)}, bf16[16,6784]{1,0:T(8,128)(2,1)S(1)}, u32[]{:S(2)}, u32[]{:S(2)}) %collective-permute-start.1) | collective-permute-done | bytes 217120 | tf_op jit(solution)/shard_map/ppermute | solution.py:499
  17.2 0.3 collective-permute-start.5
  17.5 0.0 collective-permute-done.2.refs_1_
  17.5 1.7 %collective-permute-start.3 = (bf16[16,6784]{1,0:T(8,128)(2,1)S(1)}, bf16[16,6784]{1,0:T(8,128)(2,1)S(1)}, u32[]{:S(2)}, u32[]{:S(2)}) collective-permute-start(bf16[16,6784]{1,0:T(8,128)(2,1)S(1)} %collective-permute-done.2.refs_1_), channel_id=1, source_target_pairs={{0,4},{4,8},{8,12},{12,14},{14,10},{10,6},{6,2},{2,0},{1,5},{5,9},... | collective-permute-start | bytes 651272 | tf_op jit(solution)/shard_map/ppermute | solution.py:499
  19.2 0.2 shard_map.163.refs_7_.refs_2_
  19.5 1.7 %copy-done.1 = bf16[1,6144,256]{2,1,0:T(8,128)(2,1)S(1)} copy-done((bf16[1,6144,256]{2,1,0:T(8,128)(2,1)S(1)}, bf16[1,6144,256]{2,1,0:T(8,128)(2,1)}, u32[]{:S(2)}) %copy-start.1) | copy-done | bytes 3145752
  21.1 0.2 shard_map.164.refs_8_.refs_3_
  21.4 2.1 %collective-permute-done.5.refs_5_ = bf16[16,6784]{1,0:T(8,128)(2,1)S(1)} collective-permute-done((bf16[16,6784]{1,0:T(8,128)(2,1)S(1)}, bf16[16,6784]{1,0:T(8,128)(2,1)S(1)}, u32[]{:S(2)}, u32[]{:S(2)}) %collective-permute-start.5) | collective-permute-done | bytes 217120 | tf_op jit(solution)/shard_map/ppermute | solution.py:499
  23.5 0.6 %collective-permute-start.6 = (bf16[16,6784]{1,0:T(8,128)(2,1)S(1)}, bf16[16,6784]{1,0:T(8,128)(2,1)S(1)}, u32[]{:S(2)}, u32[]{:S(2)}) collective-permute-start(bf16[16,6784]{1,0:T(8,128)(2,1)S(1)} %collective-permute-done.5.refs_5_), channel_id=1, source_target_pairs={{4,0},{8,4},{12,8},{14,12},{10,14},{6,10},{2,6},{0,2},{5,1},{9,5},... | collective-permute-start | bytes 651272 | tf_op jit(solution)/shard_map/ppermute | solution.py:499
  24.1 0.0 collective-permute-done.3.refs_2_
  24.1 1.4 %collective-permute-start.4 = (bf16[16,6784]{1,0:T(8,128)(2,1)S(1)}, bf16[16,6784]{1,0:T(8,128)(2,1)S(1)}, u32[]{:S(2)}, u32[]{:S(2)}) collective-permute-start(bf16[16,6784]{1,0:T(8,128)(2,1)S(1)} %collective-permute-done.3.refs_2_), channel_id=1, source_target_pairs={{0,4},{4,8},{8,12},{12,14},{14,10},{10,6},{6,2},{2,0},{1,5},{5,9},... | collective-permute-start | bytes 651272 | tf_op jit(solution)/shard_map/ppermute | solution.py:499
  25.5 0.2 shard_map.162.refs_9_.refs_4_
  25.7 4.0 %collective-permute-done.6.refs_6_ = bf16[16,6784]{1,0:T(8,128)(2,1)S(1)} collective-permute-done((bf16[16,6784]{1,0:T(8,128)(2,1)S(1)}, bf16[16,6784]{1,0:T(8,128)(2,1)S(1)}, u32[]{:S(2)}, u32[]{:S(2)}) %collective-permute-start.6) | collective-permute-done | bytes 217120 | tf_op jit(solution)/shard_map/ppermute | solution.py:499
  29.7 0.3 collective-permute-start.9
  30.1 1.9 %collective-permute-start.8 = (bf16[16,3456]{1,0:T(8,128)(2,1)S(1)}, bf16[16,3456]{1,0:T(8,128)(2,1)S(1)}, u32[]{:S(2)}, u32[]{:S(2)}) collective-permute-start(bf16[16,3456]{1,0:T(8,128)(2,1)S(1)} %slice.6), channel_id=1, source_target_pairs={{0,4},{4,8},{8,12},{12,14},{14,10},{10,6},{6,2},{2,0},{1,5},{5,9},... | collective-permute-start | bytes 331784 | tf_op jit(solution)/shard_map/ppermute | solution.py:499
  32.0 2.3 %shard_map.165 = (bf16[16,4608]{1,0:T(8,128)(2,1)S(1)}, bf16[16,4608]{1,0:T(8,128)(2,1)S(1)}, bf16[16,4608]{1,0:T(8,128)(2,1)S(1)}, bf16[16,4608]{1,0:T(8,128)(2...) custom-call(bf16[16,6784]{1,0:T(8,128)(2,1)S(1)} %shard_map.160.refs_0_, ...), custom_call_target="tpu_custom_call" | custom-call | flops 2000000000 | bytes 8000000 | tf_op jit(solution)/shard_map/pallas_call | solution.py:390
  34.3 1.6 %collective-permute-start.7 = (bf16[16,4608]{1,0:T(8,128)(2,1)S(1)}, bf16[16,4608]{1,0:T(8,128)(2,1)S(1)}, u32[]{:S(2)}, u32[]{:S(2)}) collective-permute-start(bf16[16,4608]{1,0:T(8,128)(2,1)S(1)} %get-tuple-element.42), channel_id=1, source_target_pairs={{0,4},{4,8},{8,12},{12,14},{14,10},{10,6},{6,2},{2,0},{1,5},{5,9},... | collective-permute-start | bytes 442376 | tf_op jit(solution)/shard_map/ppermute | solution.py:559
  35.9 0.4 collective-permute-start.14
  36.3 1.7 %shard_map.166 = bf16[16,4608]{1,0:T(8,128)(2,1)S(1)} custom-call(bf16[16,3456]{1,0:T(8,128)(2,1)S(1)} %collective-permute-done.8.refs_0_.refs_7_, bf16[16,3328]{1,0:T(8,128)(2,1)S(1)} %collective-permute-done.9.refs_1_.refs_8_, bf16[6144,256]{1,0:T(8,128)(2,1)S(1)} %shard_map.163.refs_7_.refs_2_, bf16[6144,256]{1,0:T(8,128)(2,1)S(1)} %shard_map.164.refs_8_.refs_3_, ...), custom_call_target="tpu_custom_call" | custom-call | flops 2000000000 | bytes 8000000 | tf_op jit(solution)/shard_map/pallas_call | solution.py:390
  38.0 0.0 copy-start.6
  38.1 1.4 %collective-permute-done.7 = bf16[16,4608]{1,0:T(8,128)(2,1)S(1)} collective-permute-done((bf16[16,4608]{1,0:T(8,128)(2,1)S(1)}, bf16[16,4608]{1,0:T(8,128)(2,1)S(1)}, u32[]{:S(2)}, u32[]{:S(2)}) %collective-permute-start.7) | collective-permute-done | bytes 147488 | tf_op jit(solution)/shard_map/ppermute | solution.py:559
  39.5 1.6 %collective-permute-done.14 = bf16[16,4608]{1,0:T(8,128)(2,1)S(1)} collective-permute-done((bf16[16,4608]{1,0:T(8,128)(2,1)S(1)}, bf16[16,4608]{1,0:T(8,128)(2,1)S(1)}, u32[]{:S(2)}, u32[]{:S(2)}) %collective-permute-start.14) | collective-permute-done | bytes 147488 | tf_op jit(solution)/shard_map/ppermute | solution.py:560
  41.1 0.5 collective-permute-start.15
  41.6 1.6 %collective-permute-start.10 = (bf16[16,4608]{1,0:T(8,128)(2,1)S(1)}, bf16[16,4608]{1,0:T(8,128)(2,1)S(1)}, u32[]{:S(2)}, u32[]{:S(2)}) collective-permute-start(bf16[16,4608]{1,0:T(8,128)(2,1)S(1)} %add_convert_fusion.1), channel_id=1, source_target_pairs={{0,4},{4,8},{8,12},{12,14},{14,10},{10,6},{6,2},{2,0},{1,5},{5,9},... | collective-permute-start | bytes 442376 | tf_op jit(solution)/shard_map/ppermute | solution.py:559
  43.3 4.1 %collective-permute-done.11 = bf16[16,4608]{1,0:T(8,128)(2,1)S(1)} collective-permute-done((bf16[16,4608]{1,0:T(8,128)(2,1)S(1)}, bf16[16,4608]{1,0:T(8,128)(2,1)S(1)}, u32[]{:S(2)}, u32[]{:S(2)}) %collective-permute-start.11) | collective-permute-done | bytes 147488 | tf_op jit(solution)/shard_map/ppermute | solution.py:564
  47.3 0.9 %collective-permute-start.12 = (bf16[16,4608]{1,0:T(8,128)(2,1)S(1)}, bf16[16,4608]{1,0:T(8,128)(2,1)S(1)}, u32[]{:S(2)}, u32[]{:S(2)}) collective-permute-start(bf16[16,4608]{1,0:T(8,128)(2,1)S(1)} %collective-permute-done.11), channel_id=1, source_target_pairs={{0,1},{1,0},{2,3},{3,2},{4,5},{5,4},{6,7},{7,6},{8,9},{9,8},{10,11... | collective-permute-start | bytes 442376 | tf_op jit(solution)/shard_map/ppermute | solution.py:564
  48.2 1.6 %shard_map.168 = bf16[2,16,1024]{2,1,0:T(8,128)(2,1)} custom-call(bf16[16,6784]{1,0:T(8,128)(2,1)S(1)} %shard_map.160.refs_0_, bf16[16,6784]{1,0:T(8,128)(2,1)S(1)} %collective-permute-done.2.refs_1_, bf16[16,6784]{1,0:T(8,128)(2,1)S(1)} %collective-permute-done.3.refs_2_, bf16[16,6784]{1,0:T(8,128)(2,1)S(1)} %collective-permute-done.4.refs_3_, ...), custom_call_target="tpu_custom_call" | custom-call | flops 100000 | bytes 2000000 | tf_op jit(solution)/shard_map/pallas_call | solution.py:390
  49.8 0.0 collective-permute-done.10.arrived
  49.8 0.0 collective-permute-done.12.jumped
  49.8 0.1 shard_map.167
  49.9 1.5 %collective-permute-start.13 = (bf16[16,4608]{1,0:T(8,128)(2,1)S(1)}, bf16[16,4608]{1,0:T(8,128)(2,1)S(1)}, u32[]{:S(2)}, u32[]{:S(2)}) collective-permute-start(bf16[16,4608]{1,0:T(8,128)(2,1)S(1)} %shard_map.167), channel_id=1, source_target_pairs={{0,4},{4,8},{8,12},{12,14},{14,10},{10,6},{6,2},{2,0},{1,5},{5,9},... | collective-permute-start | bytes 442376 | tf_op jit(solution)/shard_map/ppermute | solution.py:559
  51.4 0.1 shard_map.169
  51.5 0.6 %collective-permute-start.16 = (bf16[16,4608]{1,0:T(8,128)(2,1)S(1)}, bf16[16,4608]{1,0:T(8,128)(2,1)S(1)}, u32[]{:S(2)}, u32[]{:S(2)}) collective-permute-start(bf16[16,4608]{1,0:T(8,128)(2,1)S(1)} %shard_map.169), channel_id=1, source_target_pairs={{4,0},{8,4},{12,8},{14,12},{10,14},{6,10},{2,6},{0,2},{5,1},{9,5},... | collective-permute-start | bytes 442376 | tf_op jit(solution)/shard_map/ppermute | solution.py:560
  52.1 3.6 %collective-permute-done.13.from_left = bf16[16,4608]{1,0:T(8,128)(2,1)S(1)} collective-permute-done((bf16[16,4608]{1,0:T(8,128)(2,1)S(1)}, bf16[16,4608]{1,0:T(8,128)(2,1)S(1)}, u32[]{:S(2)}, u32[]{:S(2)}) %collective-permute-start.13) | collective-permute-done | bytes 147488 | tf_op jit(solution)/shard_map/ppermute | solution.py:559
  55.7 1.4 %collective-permute-done.16.from_right = bf16[16,4608]{1,0:T(8,128)(2,1)S(1)} collective-permute-done((bf16[16,4608]{1,0:T(8,128)(2,1)S(1)}, bf16[16,4608]{1,0:T(8,128)(2,1)S(1)}, u32[]{:S(2)}, u32[]{:S(2)}) %collective-permute-start.16) | collective-permute-done | bytes 147488 | tf_op jit(solution)/shard_map/ppermute | solution.py:560
  57.1 0.1 shard_map.170
  57.2 0.1 collective-permute-start.17
  57.3 1.3 %collective-permute-done.17.theirs = bf16[8,4608]{1,0:T(8,128)(2,1)S(1)} collective-permute-done((bf16[8,4608]{1,0:T(8,128)(2,1)S(1)}, bf16[8,4608]{1,0:T(8,128)(2,1)S(1)}, u32[]{:S(2)}, u32[]{:S(2)}) %collective-permute-start.17) | collective-permute-done | bytes 73760 | tf_op jit(solution)/shard_map/ppermute | solution.py:588
  58.5 1.1 %shard_map.171 = bf16[32,3072]{1,0:T(8,128)(2,1)} custom-call(f32[32,3072]{1,0:T(8,128)S(1)} %copy-done.3, bf16[8,4608]{1,0:T(8,128)(2,1)S(1)} %get-tuple-element.49.mine, bf16[8,4608]{1,0:T(8,128)(2,1)S(1)} %collective-permute-done.17.theirs, s32[2,32]{1,0:T(2,128)S(1)} %bitcast.12, f32[2,32]{1,0:T(2,128)S(1)} %bitcast.13), custom_call_target="tpu_custom_call" | custom-call | flops 20000000 | bytes 800000 | tf_op jit(solution)/shard_map/pallas_call | solution.py:390
  (20 shorter events, 0.1 us)
Async XLA Ops:
  5.3 1.7 %collective-permute-start = (bf16[8,4736]{1,0:T(8,128)(2,1)}, bf16[8,4736]{1,0:T(8,128)(2,1)S(1)}, u32[]{:S(2)}, u32[]{:S(2)}) collective-permute-start(bf16[8,4736]{1,0:T(8,128)(2,1)} %get-tuple-element.27), channel_id=1, source_target_pairs={{0,1},{1,0},{2,3},{3,2},{4,5},{5,4},{6,7},{7,6},{8,9},{9,8},{10,11... | collective-permute-start | bytes 227336 | tf_op jit(solution)/shard_map/ppermute | solution.py:478
  5.8 0.9 %copy-start.4 = (bf16[16,6912]{1,0:T(8,128)(2,1)S(1)}, bf16[16,6912]{1,0:T(8,128)(2,1)}, u32[]{:S(2)}) copy-start(bf16[16,6912]{1,0:T(8,128)(2,1)} %get-tuple-element.28.source) | copy-start | bytes 663556
  7.1 12.1 %copy-start = (bf16[1,6144,256]{2,1,0:T(8,128)(2,1)S(1)}, bf16[1,6144,256]{2,1,0:T(8,128)(2,1)}, u32[]{:S(2)}) copy-start(bf16[1,6144,256]{2,1,0:T(8,128)(2,1)} %param.25) | copy-start | bytes 9437188
  7.1 10.4 %collective-permute-start.2 = (bf16[16,6784]{1,0:T(8,128)(2,1)S(1)}, bf16[16,6784]{1,0:T(8,128)(2,1)S(1)}, u32[]{:S(2)}, u32[]{:S(2)}) collective-permute-start(bf16[16,6784]{1,0:T(8,128)(2,1)S(1)} %shard_map.160.refs_0_), channel_id=1, source_target_pairs={{0,4},{4,8},{8,12},{12,14},{14,10},{10,6},{6,2},{2,0},{1,5},{5,9},... | collective-permute-start | bytes 651272 | tf_op jit(solution)/shard_map/ppermute | solution.py:499
  10.1 7.1 %collective-permute-start.1 = (bf16[16,6784]{1,0:T(8,128)(2,1)S(1)}, bf16[16,6784]{1,0:T(8,128)(2,1)S(1)}, u32[]{:S(2)}, u32[]{:S(2)}) collective-permute-start(bf16[16,6784]{1,0:T(8,128)(2,1)S(1)} %shard_map.160.refs_0_), channel_id=1, source_target_pairs={{4,0},{8,4},{12,8},{14,12},{10,14},{6,10},{2,6},{0,2},{5,1},{9,5},... | collective-permute-start | bytes 651272 | tf_op jit(solution)/shard_map/ppermute | solution.py:499
  17.2 6.3 %collective-permute-start.5 = (bf16[16,6784]{1,0:T(8,128)(2,1)S(1)}, bf16[16,6784]{1,0:T(8,128)(2,1)S(1)}, u32[]{:S(2)}, u32[]{:S(2)}) collective-permute-start(bf16[16,6784]{1,0:T(8,128)(2,1)S(1)} %collective-permute-done.1.refs_4_), channel_id=1, source_target_pairs={{4,0},{8,4},{12,8},{14,12},{10,14},{6,10},{2,6},{0,2},{5,1},{9,5},... | collective-permute-start | bytes 651272 | tf_op jit(solution)/shard_map/ppermute | solution.py:499
  17.5 6.6 %collective-permute-start.3 = (bf16[16,6784]{1,0:T(8,128)(2,1)S(1)}, bf16[16,6784]{1,0:T(8,128)(2,1)S(1)}, u32[]{:S(2)}, u32[]{:S(2)}) collective-permute-start(bf16[16,6784]{1,0:T(8,128)(2,1)S(1)} %collective-permute-done.2.refs_1_), channel_id=1, source_target_pairs={{0,4},{4,8},{8,12},{12,14},{14,10},{10,6},{6,2},{2,0},{1,5},{5,9},... | collective-permute-start | bytes 651272 | tf_op jit(solution)/shard_map/ppermute | solution.py:499
  19.2 1.9 %copy-start.1 = (bf16[1,6144,256]{2,1,0:T(8,128)(2,1)S(1)}, bf16[1,6144,256]{2,1,0:T(8,128)(2,1)}, u32[]{:S(2)}) copy-start(bf16[1,6144,256]{2,1,0:T(8,128)(2,1)} %param.26) | copy-start | bytes 9437188
  21.1 4.4 %copy-start.2 = (bf16[1,256,6144]{2,1,0:T(8,128)(2,1)S(1)}, bf16[1,256,6144]{2,1,0:T(8,128)(2,1)}, u32[]{:S(2)}) copy-start(bf16[1,256,6144]{2,1,0:T(8,128)(2,1)} %param.27) | copy-start | bytes 9437188
  23.5 6.2 %collective-permute-start.6 = (bf16[16,6784]{1,0:T(8,128)(2,1)S(1)}, bf16[16,6784]{1,0:T(8,128)(2,1)S(1)}, u32[]{:S(2)}, u32[]{:S(2)}) collective-permute-start(bf16[16,6784]{1,0:T(8,128)(2,1)S(1)} %collective-permute-done.5.refs_5_), channel_id=1, source_target_pairs={{4,0},{8,4},{12,8},{14,12},{10,14},{6,10},{2,6},{0,2},{5,1},{9,5},... | collective-permute-start | bytes 651272 | tf_op jit(solution)/shard_map/ppermute | solution.py:499
  24.1 6.0 %collective-permute-start.4 = (bf16[16,6784]{1,0:T(8,128)(2,1)S(1)}, bf16[16,6784]{1,0:T(8,128)(2,1)S(1)}, u32[]{:S(2)}, u32[]{:S(2)}) collective-permute-start(bf16[16,6784]{1,0:T(8,128)(2,1)S(1)} %collective-permute-done.3.refs_2_), channel_id=1, source_target_pairs={{0,4},{4,8},{8,12},{12,14},{14,10},{10,6},{6,2},{2,0},{1,5},{5,9},... | collective-permute-start | bytes 651272 | tf_op jit(solution)/shard_map/ppermute | solution.py:499
  29.7 6.6 %collective-permute-start.9 = (bf16[16,3328]{1,0:T(8,128)(2,1)S(1)}, bf16[16,3328]{1,0:T(8,128)(2,1)S(1)}, u32[]{:S(2)}, u32[]{:S(2)}) collective-permute-start(bf16[16,3328]{1,0:T(8,128)(2,1)S(1)} %slice.8), channel_id=1, source_target_pairs={{4,0},{8,4},{12,8},{14,12},{10,14},{6,10},{2,6},{0,2},{5,1},{9,5},... | collective-permute-start | bytes 319496 | tf_op jit(solution)/shard_map/ppermute | solution.py:499
  30.1 6.3 %collective-permute-start.8 = (bf16[16,3456]{1,0:T(8,128)(2,1)S(1)}, bf16[16,3456]{1,0:T(8,128)(2,1)S(1)}, u32[]{:S(2)}, u32[]{:S(2)}) collective-permute-start(bf16[16,3456]{1,0:T(8,128)(2,1)S(1)} %slice.6), channel_id=1, source_target_pairs={{0,4},{4,8},{8,12},{12,14},{14,10},{10,6},{6,2},{2,0},{1,5},{5,9},... | collective-permute-start | bytes 331784 | tf_op jit(solution)/shard_map/ppermute | solution.py:499
  34.3 5.2 %collective-permute-start.7 = (bf16[16,4608]{1,0:T(8,128)(2,1)S(1)}, bf16[16,4608]{1,0:T(8,128)(2,1)S(1)}, u32[]{:S(2)}, u32[]{:S(2)}) collective-permute-start(bf16[16,4608]{1,0:T(8,128)(2,1)S(1)} %get-tuple-element.42), channel_id=1, source_target_pairs={{0,4},{4,8},{8,12},{12,14},{14,10},{10,6},{6,2},{2,0},{1,5},{5,9},... | collective-permute-start | bytes 442376 | tf_op jit(solution)/shard_map/ppermute | solution.py:559
  35.9 5.1 %collective-permute-start.14 = (bf16[16,4608]{1,0:T(8,128)(2,1)S(1)}, bf16[16,4608]{1,0:T(8,128)(2,1)S(1)}, u32[]{:S(2)}, u32[]{:S(2)}) collective-permute-start(bf16[16,4608]{1,0:T(8,128)(2,1)S(1)} %get-tuple-element.47), channel_id=1, source_target_pairs={{4,0},{8,4},{12,8},{14,12},{10,14},{6,10},{2,6},{0,2},{5,1},{9,5},... | collective-permute-start | bytes 442376 | tf_op jit(solution)/shard_map/ppermute | solution.py:560
  38.0 20.5 %copy-start.3 = (f32[32,3072]{1,0:T(8,128)S(1)}, f32[32,3072]{1,0:T(8,128)}, u32[]{:S(2)}) copy-start(f32[32,3072]{1,0:T(8,128)} %shard_map.161.hidden) | copy-start | bytes 1179652
  38.0 20.5 %copy-start.5 = (s32[32,2]{0,1:T(2,128)S(1)}, s32[32,2]{0,1:T(2,128)}, u32[]{:S(2)}) copy-start(s32[32,2]{0,1:T(2,128)} %param.23) | copy-start | bytes 772
  38.0 20.5 %copy-start.6 = (f32[32,2]{0,1:T(2,128)S(1)}, f32[32,2]{0,1:T(2,128)}, u32[]{:S(2)}) copy-start(f32[32,2]{0,1:T(2,128)} %param.24) | copy-start | bytes 772
  39.5 7.9 %collective-permute-start.11 = (bf16[16,4608]{1,0:T(8,128)(2,1)S(1)}, bf16[16,4608]{1,0:T(8,128)(2,1)S(1)}, u32[]{:S(2)}, u32[]{:S(2)}) collective-permute-start(bf16[16,4608]{1,0:T(8,128)(2,1)S(1)} %shard_map.166), channel_id=1, source_target_pairs={{0,13},{4,15},{8,11},{12,7},{14,3},{10,1},{6,5},{2,9},{1,10},{5,6}... | collective-permute-start | bytes 442376 | tf_op jit(solution)/shard_map/ppermute | solution.py:564
  41.1 8.7 %collective-permute-start.15 = (bf16[16,4608]{1,0:T(8,128)(2,1)S(1)}, bf16[16,4608]{1,0:T(8,128)(2,1)S(1)}, u32[]{:S(2)}, u32[]{:S(2)}) collective-permute-start(bf16[16,4608]{1,0:T(8,128)(2,1)S(1)} %add_convert_fusion), channel_id=1, source_target_pairs={{4,0},{8,4},{12,8},{14,12},{10,14},{6,10},{2,6},{0,2},{5,1},{9,5},... | collective-permute-start | bytes 442376 | tf_op jit(solution)/shard_map/ppermute | solution.py:560
  41.6 8.2 %collective-permute-start.10 = (bf16[16,4608]{1,0:T(8,128)(2,1)S(1)}, bf16[16,4608]{1,0:T(8,128)(2,1)S(1)}, u32[]{:S(2)}, u32[]{:S(2)}) collective-permute-start(bf16[16,4608]{1,0:T(8,128)(2,1)S(1)} %add_convert_fusion.1), channel_id=1, source_target_pairs={{0,4},{4,8},{8,12},{12,14},{14,10},{10,6},{6,2},{2,0},{1,5},{5,9},... | collective-permute-start | bytes 442376 | tf_op jit(solution)/shard_map/ppermute | solution.py:559
  47.3 2.5 %collective-permute-start.12 = (bf16[16,4608]{1,0:T(8,128)(2,1)S(1)}, bf16[16,4608]{1,0:T(8,128)(2,1)S(1)}, u32[]{:S(2)}, u32[]{:S(2)}) collective-permute-start(bf16[16,4608]{1,0:T(8,128)(2,1)S(1)} %collective-permute-done.11), channel_id=1, source_target_pairs={{0,1},{1,0},{2,3},{3,2},{4,5},{5,4},{6,7},{7,6},{8,9},{9,8},{10,11... | collective-permute-start | bytes 442376 | tf_op jit(solution)/shard_map/ppermute | solution.py:564
  49.9 5.8 %collective-permute-start.13 = (bf16[16,4608]{1,0:T(8,128)(2,1)S(1)}, bf16[16,4608]{1,0:T(8,128)(2,1)S(1)}, u32[]{:S(2)}, u32[]{:S(2)}) collective-permute-start(bf16[16,4608]{1,0:T(8,128)(2,1)S(1)} %shard_map.167), channel_id=1, source_target_pairs={{0,4},{4,8},{8,12},{12,14},{14,10},{10,6},{6,2},{2,0},{1,5},{5,9},... | collective-permute-start | bytes 442376 | tf_op jit(solution)/shard_map/ppermute | solution.py:559
  51.5 5.6 %collective-permute-start.16 = (bf16[16,4608]{1,0:T(8,128)(2,1)S(1)}, bf16[16,4608]{1,0:T(8,128)(2,1)S(1)}, u32[]{:S(2)}, u32[]{:S(2)}) collective-permute-start(bf16[16,4608]{1,0:T(8,128)(2,1)S(1)} %shard_map.169), channel_id=1, source_target_pairs={{4,0},{8,4},{12,8},{14,12},{10,14},{6,10},{2,6},{0,2},{5,1},{9,5},... | collective-permute-start | bytes 442376 | tf_op jit(solution)/shard_map/ppermute | solution.py:560
  57.2 1.3 %collective-permute-start.17 = (bf16[8,4608]{1,0:T(8,128)(2,1)S(1)}, bf16[8,4608]{1,0:T(8,128)(2,1)S(1)}, u32[]{:S(2)}, u32[]{:S(2)}) collective-permute-start(bf16[8,4608]{1,0:T(8,128)(2,1)S(1)} %get-tuple-element.50), channel_id=1, source_target_pairs={{0,1},{1,0},{2,3},{3,2},{4,5},{5,4},{6,7},{7,6},{8,9},{9,8},{10,11... | collective-permute-start | bytes 221192 | tf_op jit(solution)/shard_map/ppermute | solution.py:588

commit v6 on v5

--- a/solution.py
+++ b/solution.py
@@ -332,7 +332,20 @@
     source = jnp.sum(jnp.where(lane == entries, notes, 0.0), axis=1, keepdims=True)
     earlier = to_row(source, n) < source
     rank = jnp.sum(jnp.where(earlier, to_row(named, n), 0.0), axis=1, keepdims=True)
-    board[...] = jnp.where(match, rank, -1.0).astype(jnp.int32)
+    table = jnp.where(match, rank, -1.0)
+    if n * entries <= 32:
+        pages = [jnp.zeros((PAGE, page_width), F32)] * entries
+        for j in range(n):
+            block, shift = (blocks[j], 0) if j < n - 1 else (blocks[n], cut)
+            for entry in range(entries):
+                at = SLOT_COLS + entry * page_width - shift
+                page = block[:, at : at + page_width].astype(F32)
+                place = jnp.broadcast_to(table[j : j + 1, entry : entry + 1], page.shape)
+                pages = [jnp.where(place == float(slot), page, old) for slot, old in enumerate(pages)]
+        for slot in range(entries):
+            arrived[slot] = pages[slot].astype(BF16)
+        return
+    board[...] = table.astype(jnp.int32)
     copy = pltpu.make_async_copy(board, board_smem, sem)
     copy.start()
     arrived[...] = jnp.zeros_like(arrived)
@@ -507,10 +520,10 @@
             )
             b, hidden = tie((b, hidden))
         else:
-            for weight in stored[2 * step - 2 : 2 * step]:
+            for weight in {1: stored[:1], 2: stored[1:]}.get(step, []):
                 weights.append(fetch(weight))
                 if step == 2:
-                    a, weights[-1] = tie((a, weights[-1]))
+                    b, weights[-1] = tie((b, weights[-1]))
                 else:
                     b, weights[-1] = tie((b, weights[-1]))
         from_left.append(a)

time: 59.9 us -> 59.8 us (level)
    ppermute x8, waiting for transfers between devices: 8.53 us -> 9.39 us  [per_device(): a, b = (lax.ppermute(a, 'attn', right), lax.ppermute(b, 'attn', left))]
  transfers between devices with their start and end apart: 18 -> 18, of which waited for: 10 -> 11; matrix products, arithmetic and copies ran while one was open for 0% -> 0% of each run, Pallas kernels for 18% -> 17%
where the time goes in v6:
time: 59.8 us; the launch traced here: 59.5 us
  waiting for transfers between devices  22.1 us (37%)
  starting transfers between devices  17.4 us (29%)
  Pallas kernels  16.4 us (27%)
  local copies, waits for them, and re-layouts  2.64 us (4%)
  between operations  0.79 us (1%)
    pallas_call x14, Pallas kernels, call(): pl.pallas_call(kernel, out_shape=outs, in_specs=in_specs, out_specs=[VMEM...  16.4 us
    ppermute x8, waiting for transfers between devices, per_device(): a, b = (lax.ppermute(a, 'attn', right), lax.ppermute(b, 'attn', left))  9.39 us
    ppermute x8, starting transfers between devices, per_device(): a, b = (lax.ppermute(a, 'attn', right), lax.ppermute(b, 'attn', left))  9.16 us
    ppermute x3, starting transfers between devices, per_device(): going_right = lax.ppermute(send_right, 'attn', right)  4.99 us
    ppermute x3, waiting for transfers between devices, per_device(): going_right = lax.ppermute(send_right, 'attn', right)  4.44 us
    ppermute x1, waiting for transfers between devices, per_device(): lax.ppermute(opposite, ('attn', 'expert'), jump)  3.96 us
    ppermute x3, waiting for transfers between devices, per_device(): going_left = lax.ppermute(send_left, 'attn', left)  2.93 us
    unnamed x14, local copies, waits for them, and re-layouts  2.63 us
  transfers between devices with their start and end apart: 18, of which 11 were waited for; matrix products, arithmetic and copies ran while one was open for 0% of the time, Pallas kernels for 17%

profile of v6, /device:TPU:0, one launch (start us, length us, event | category | flops | bytes accessed | tf_op | source)
XLA Modules:
  0.0 59.5 jit_solution(13002966581233816378)
XLA Ops:
  0.6 4.7 %shard_map.158 = (bf16[16,6912]{1,0:T(8,128)(2,1)}, bf16[8,4736]{1,0:T(8,128)(2,1)}) custom-call(s32[1,32]{1,0:T(1,128)} %refs_0_.3, s32[1,32]{1,0:T(1,128)} %bitcast.17, s32[1,72]{1,0:T(1,128)} %refs_2_.3, s32[2,32]{1,0:T(2,128)} %bitcast.11, s32[1,2]{1,0:T(1,128)} %refs_4_.2, s32[1,2]{1,0:T(1,128)} %refs_5_.2, bf16[32,3072]{1,0:T(8,128)(2,1)} %refs_3_.1, ...), custom_call_target="tpu_custom_call" | custom-call | flops 400000000 | bytes 3500000 | tf_op jit(solution)/shard_map/pallas_call | solution.py:403
  5.3 0.5 collective-permute-start
  5.8 0.9 %copy-done.4 = bf16[16,6912]{1,0:T(8,128)(2,1)S(1)} copy-done((bf16[16,6912]{1,0:T(8,128)(2,1)S(1)}, bf16[16,6912]{1,0:T(8,128)(2,1)}, u32[]{:S(2)}) %copy-start.4) | copy-done | bytes 221208
  6.8 0.2 collective-permute-done.theirs
  7.0 0.1 shard_map.160.refs_0_
  7.1 0.0 copy-start
  7.1 3.0 %collective-permute-start.2 = (bf16[16,6784]{1,0:T(8,128)(2,1)S(1)}, bf16[16,6784]{1,0:T(8,128)(2,1)S(1)}, u32[]{:S(2)}, u32[]{:S(2)}) collective-permute-start(bf16[16,6784]{1,0:T(8,128)(2,1)S(1)} %shard_map.160.refs_0_), channel_id=1, source_target_pairs={{0,4},{4,8},{8,12},{12,14},{14,10},{10,6},{6,2},{2,0},{1,5},{5,9},... | collective-permute-start | bytes 651272 | tf_op jit(solution)/shard_map/ppermute | solution.py:512
  10.1 0.0 collective-permute-start.1
  10.1 4.7 %shard_map.161.hidden = f32[32,3072]{1,0:T(8,128)} custom-call(s32[1,32]{1,0:T(1,128)} %refs_0_.3, s32[1,32]{1,0:T(1,128)} %bitcast.18, s32[1,72]{1,0:T(1,128)} %refs_2_.3, bf16[32,3072]{1,0:T(8,128)(2,1)} %refs_3_.1, bf16[32,1024]{1,0:T(8,128)(2,1)} %refs_4_.3, bf16[32,3072]{1,0:T(8,128)(2,1)} %refs_5_.3, bf16[1152,1024]{1,0:T(8,128)(2,1)} %bitcast.15), custom_call_target="tpu_custom_call" | custom-call | flops 4000000000 | bytes 3500000 | tf_op jit(solution)/shard_map/pallas_call | solution.py:403
  14.8 2.4 %collective-permute-done.1.refs_4_ = bf16[16,6784]{1,0:T(8,128)(2,1)S(1)} collective-permute-done((bf16[16,6784]{1,0:T(8,128)(2,1)S(1)}, bf16[16,6784]{1,0:T(8,128)(2,1)S(1)}, u32[]{:S(2)}, u32[]{:S(2)}) %collective-permute-start.1) | collective-permute-done | bytes 217120 | tf_op jit(solution)/shard_map/ppermute | solution.py:512
  17.2 0.0 collective-permute-done.2.refs_1_
  17.2 1.6 %collective-permute-start.3 = (bf16[16,6784]{1,0:T(8,128)(2,1)S(1)}, bf16[16,6784]{1,0:T(8,128)(2,1)S(1)}, u32[]{:S(2)}, u32[]{:S(2)}) collective-permute-start(bf16[16,6784]{1,0:T(8,128)(2,1)S(1)} %collective-permute-done.2.refs_1_), channel_id=1, source_target_pairs={{0,4},{4,8},{8,12},{12,14},{14,10},{10,6},{6,2},{2,0},{1,5},{5,9},... | collective-permute-start | bytes 651272 | tf_op jit(solution)/shard_map/ppermute | solution.py:512
  18.8 0.4 collective-permute-start.5
  19.2 0.2 shard_map.162.refs_7_.refs_2_
  19.5 4.0 %collective-permute-done.3.refs_2_ = bf16[16,6784]{1,0:T(8,128)(2,1)S(1)} collective-permute-done((bf16[16,6784]{1,0:T(8,128)(2,1)S(1)}, bf16[16,6784]{1,0:T(8,128)(2,1)S(1)}, u32[]{:S(2)}, u32[]{:S(2)}) %collective-permute-start.3) | collective-permute-done | bytes 217120 | tf_op jit(solution)/shard_map/ppermute | solution.py:512
  23.5 1.6 %collective-permute-start.4 = (bf16[16,6784]{1,0:T(8,128)(2,1)S(1)}, bf16[16,6784]{1,0:T(8,128)(2,1)S(1)}, u32[]{:S(2)}, u32[]{:S(2)}) collective-permute-start(bf16[16,6784]{1,0:T(8,128)(2,1)S(1)} %collective-permute-done.3.refs_2_), channel_id=1, source_target_pairs={{0,4},{4,8},{8,12},{12,14},{14,10},{10,6},{6,2},{2,0},{1,5},{5,9},... | collective-permute-start | bytes 651272 | tf_op jit(solution)/shard_map/ppermute | solution.py:512
  25.0 0.4 collective-permute-start.6
  25.5 0.2 shard_map.163.refs_8_.refs_3_
  25.7 1.7 %copy-done.2 = bf16[1,256,6144]{2,1,0:T(8,128)(2,1)S(1)} copy-done((bf16[1,256,6144]{2,1,0:T(8,128)(2,1)S(1)}, bf16[1,256,6144]{2,1,0:T(8,128)(2,1)}, u32[]{:S(2)}) %copy-start.2) | copy-done | bytes 3145752
  27.4 0.2 shard_map.164.refs_9_.refs_4_
  27.6 2.1 %collective-permute-done.4.refs_3_ = bf16[16,6784]{1,0:T(8,128)(2,1)S(1)} collective-permute-done((bf16[16,6784]{1,0:T(8,128)(2,1)S(1)}, bf16[16,6784]{1,0:T(8,128)(2,1)S(1)}, u32[]{:S(2)}, u32[]{:S(2)}) %collective-permute-start.4) | collective-permute-done | bytes 217120 | tf_op jit(solution)/shard_map/ppermute | solution.py:512
  29.7 1.6 %collective-permute-start.8 = (bf16[16,3456]{1,0:T(8,128)(2,1)S(1)}, bf16[16,3456]{1,0:T(8,128)(2,1)S(1)}, u32[]{:S(2)}, u32[]{:S(2)}) collective-permute-start(bf16[16,3456]{1,0:T(8,128)(2,1)S(1)} %slice.8), channel_id=1, source_target_pairs={{0,4},{4,8},{8,12},{12,14},{14,10},{10,6},{6,2},{2,0},{1,5},{5,9},... | collective-permute-start | bytes 331784 | tf_op jit(solution)/shard_map/ppermute | solution.py:512
  31.3 0.0 collective-permute-done.6.refs_6_
  31.3 0.5 collective-permute-start.9
  31.8 2.3 %shard_map.165 = (bf16[16,4608]{1,0:T(8,128)(2,1)S(1)}, bf16[16,4608]{1,0:T(8,128)(2,1)S(1)}, bf16[16,4608]{1,0:T(8,128)(2,1)S(1)}, bf16[16,4608]{1,0:T(8,128)(2...) custom-call(bf16[16,6784]{1,0:T(8,128)(2,1)S(1)} %shard_map.160.refs_0_, ...), custom_call_target="tpu_custom_call" | custom-call | flops 2000000000 | bytes 8000000 | tf_op jit(solution)/shard_map/pallas_call | solution.py:403
  34.1 1.6 %collective-permute-start.7 = (bf16[16,4608]{1,0:T(8,128)(2,1)S(1)}, bf16[16,4608]{1,0:T(8,128)(2,1)S(1)}, u32[]{:S(2)}, u32[]{:S(2)}) collective-permute-start(bf16[16,4608]{1,0:T(8,128)(2,1)S(1)} %get-tuple-element.42), channel_id=1, source_target_pairs={{0,4},{4,8},{8,12},{12,14},{14,10},{10,6},{6,2},{2,0},{1,5},{5,9},... | collective-permute-start | bytes 442376 | tf_op jit(solution)/shard_map/ppermute | solution.py:572
  35.7 0.4 collective-permute-start.14
  36.2 0.9 %collective-permute-done.9.refs_1_.refs_8_ = bf16[16,3328]{1,0:T(8,128)(2,1)S(1)} collective-permute-done((bf16[16,3328]{1,0:T(8,128)(2,1)S(1)}, bf16[16,3328]{1,0:T(8,128)(2,1)S(1)}, u32[]{:S(2)}, u32[]{:S(2)}) %collective-permute-start.9) | collective-permute-done | bytes 106528 | tf_op jit(solution)/shard_map/ppermute | solution.py:512
  37.0 1.7 %shard_map.166 = bf16[16,4608]{1,0:T(8,128)(2,1)S(1)} custom-call(bf16[16,3456]{1,0:T(8,128)(2,1)S(1)} %collective-permute-done.8.refs_0_.refs_7_, bf16[16,3328]{1,0:T(8,128)(2,1)S(1)} %collective-permute-done.9.refs_1_.refs_8_, bf16[6144,256]{1,0:T(8,128)(2,1)S(1)} %shard_map.162.refs_7_.refs_2_, bf16[6144,256]{1,0:T(8,128)(2,1)S(1)} %shard_map.163.refs_8_.refs_3_, ...), custom_call_target="tpu_custom_call" | custom-call | flops 2000000000 | bytes 8000000 | tf_op jit(solution)/shard_map/pallas_call | solution.py:403
  38.7 0.0 copy-start.6
  38.8 0.6 collective-permute-done.7
  39.3 1.6 %collective-permute-done.14 = bf16[16,4608]{1,0:T(8,128)(2,1)S(1)} collective-permute-done((bf16[16,4608]{1,0:T(8,128)(2,1)S(1)}, bf16[16,4608]{1,0:T(8,128)(2,1)S(1)}, u32[]{:S(2)}, u32[]{:S(2)}) %collective-permute-start.14) | collective-permute-done | bytes 147488 | tf_op jit(solution)/shard_map/ppermute | solution.py:573
  40.9 0.5 collective-permute-start.15
  41.5 1.6 %collective-permute-start.10 = (bf16[16,4608]{1,0:T(8,128)(2,1)S(1)}, bf16[16,4608]{1,0:T(8,128)(2,1)S(1)}, u32[]{:S(2)}, u32[]{:S(2)}) collective-permute-start(bf16[16,4608]{1,0:T(8,128)(2,1)S(1)} %add_convert_fusion.1), channel_id=1, source_target_pairs={{0,4},{4,8},{8,12},{12,14},{14,10},{10,6},{6,2},{2,0},{1,5},{5,9},... | collective-permute-start | bytes 442376 | tf_op jit(solution)/shard_map/ppermute | solution.py:572
  43.1 4.0 %collective-permute-done.11 = bf16[16,4608]{1,0:T(8,128)(2,1)S(1)} collective-permute-done((bf16[16,4608]{1,0:T(8,128)(2,1)S(1)}, bf16[16,4608]{1,0:T(8,128)(2,1)S(1)}, u32[]{:S(2)}, u32[]{:S(2)}) %collective-permute-start.11) | collective-permute-done | bytes 147488 | tf_op jit(solution)/shard_map/ppermute | solution.py:577
  47.1 1.3 %collective-permute-start.12 = (bf16[16,4608]{1,0:T(8,128)(2,1)S(1)}, bf16[16,4608]{1,0:T(8,128)(2,1)S(1)}, u32[]{:S(2)}, u32[]{:S(2)}) collective-permute-start(bf16[16,4608]{1,0:T(8,128)(2,1)S(1)} %collective-permute-done.11), channel_id=1, source_target_pairs={{0,1},{1,0},{2,3},{3,2},{4,5},{5,4},{6,7},{7,6},{8,9},{9,8},{10,11... | collective-permute-start | bytes 442376 | tf_op jit(solution)/shard_map/ppermute | solution.py:577
  48.4 1.0 %shard_map.168 = bf16[2,16,1024]{2,1,0:T(8,128)(2,1)} custom-call(bf16[16,6784]{1,0:T(8,128)(2,1)S(1)} %shard_map.160.refs_0_, bf16[16,6784]{1,0:T(8,128)(2,1)S(1)} %collective-permute-done.2.refs_1_, bf16[16,6784]{1,0:T(8,128)(2,1)S(1)} %collective-permute-done.3.refs_2_, bf16[16,6784]{1,0:T(8,128)(2,1)S(1)} %collective-permute-done.4.refs_3_, ...), custom_call_target="tpu_custom_call" | custom-call | flops 100000 | bytes 2000000 | tf_op jit(solution)/shard_map/pallas_call | solution.py:403
  49.5 0.0 collective-permute-done.12.jumped
  49.5 0.1 shard_map.167
  49.5 1.7 %collective-permute-start.13 = (bf16[16,4608]{1,0:T(8,128)(2,1)S(1)}, bf16[16,4608]{1,0:T(8,128)(2,1)S(1)}, u32[]{:S(2)}, u32[]{:S(2)}) collective-permute-start(bf16[16,4608]{1,0:T(8,128)(2,1)S(1)} %shard_map.167), channel_id=1, source_target_pairs={{0,4},{4,8},{8,12},{12,14},{14,10},{10,6},{6,2},{2,0},{1,5},{5,9},... | collective-permute-start | bytes 442376 | tf_op jit(solution)/shard_map/ppermute | solution.py:572
  51.3 0.1 shard_map.169
  51.3 0.4 collective-permute-start.16
  51.7 3.9 %collective-permute-done.13.from_left = bf16[16,4608]{1,0:T(8,128)(2,1)S(1)} collective-permute-done((bf16[16,4608]{1,0:T(8,128)(2,1)S(1)}, bf16[16,4608]{1,0:T(8,128)(2,1)S(1)}, u32[]{:S(2)}, u32[]{:S(2)}) %collective-permute-start.13) | collective-permute-done | bytes 147488 | tf_op jit(solution)/shard_map/ppermute | solution.py:572
  55.6 1.4 %collective-permute-done.16.from_right = bf16[16,4608]{1,0:T(8,128)(2,1)S(1)} collective-permute-done((bf16[16,4608]{1,0:T(8,128)(2,1)S(1)}, bf16[16,4608]{1,0:T(8,128)(2,1)S(1)}, u32[]{:S(2)}, u32[]{:S(2)}) %collective-permute-start.16) | collective-permute-done | bytes 147488 | tf_op jit(solution)/shard_map/ppermute | solution.py:573
  57.0 0.1 shard_map.170
  57.1 0.1 collective-permute-start.17
  57.1 1.3 %collective-permute-done.17.theirs = bf16[8,4608]{1,0:T(8,128)(2,1)S(1)} collective-permute-done((bf16[8,4608]{1,0:T(8,128)(2,1)S(1)}, bf16[8,4608]{1,0:T(8,128)(2,1)S(1)}, u32[]{:S(2)}, u32[]{:S(2)}) %collective-permute-start.17) | collective-permute-done | bytes 73760 | tf_op jit(solution)/shard_map/ppermute | solution.py:601
  58.4 1.1 %shard_map.171 = bf16[32,3072]{1,0:T(8,128)(2,1)} custom-call(f32[32,3072]{1,0:T(8,128)S(1)} %copy-done.3, bf16[8,4608]{1,0:T(8,128)(2,1)S(1)} %get-tuple-element.49.mine, bf16[8,4608]{1,0:T(8,128)(2,1)S(1)} %collective-permute-done.17.theirs, s32[2,32]{1,0:T(2,128)S(1)} %bitcast.12, f32[2,32]{1,0:T(2,128)S(1)} %bitcast.13), custom_call_target="tpu_custom_call" | custom-call | flops 20000000 | bytes 800000 | tf_op jit(solution)/shard_map/pallas_call | solution.py:403
  (20 shorter events, 0.1 us)
Async XLA Ops:
  5.3 1.7 %collective-permute-start = (bf16[8,4736]{1,0:T(8,128)(2,1)}, bf16[8,4736]{1,0:T(8,128)(2,1)S(1)}, u32[]{:S(2)}, u32[]{:S(2)}) collective-permute-start(bf16[8,4736]{1,0:T(8,128)(2,1)} %get-tuple-element.27), channel_id=1, source_target_pairs={{0,1},{1,0},{2,3},{3,2},{4,5},{5,4},{6,7},{7,6},{8,9},{9,8},{10,11... | collective-permute-start | bytes 227336 | tf_op jit(solution)/shard_map/ppermute | solution.py:491
  5.8 0.9 %copy-start.4 = (bf16[16,6912]{1,0:T(8,128)(2,1)S(1)}, bf16[16,6912]{1,0:T(8,128)(2,1)}, u32[]{:S(2)}) copy-start(bf16[16,6912]{1,0:T(8,128)(2,1)} %get-tuple-element.28.source) | copy-start | bytes 663556
  7.1 12.1 %copy-start = (bf16[1,6144,256]{2,1,0:T(8,128)(2,1)S(1)}, bf16[1,6144,256]{2,1,0:T(8,128)(2,1)}, u32[]{:S(2)}) copy-start(bf16[1,6144,256]{2,1,0:T(8,128)(2,1)} %param.25) | copy-start | bytes 9437188
  7.1 10.1 %collective-permute-start.2 = (bf16[16,6784]{1,0:T(8,128)(2,1)S(1)}, bf16[16,6784]{1,0:T(8,128)(2,1)S(1)}, u32[]{:S(2)}, u32[]{:S(2)}) collective-permute-start(bf16[16,6784]{1,0:T(8,128)(2,1)S(1)} %shard_map.160.refs_0_), channel_id=1, source_target_pairs={{0,4},{4,8},{8,12},{12,14},{14,10},{10,6},{6,2},{2,0},{1,5},{5,9},... | collective-permute-start | bytes 651272 | tf_op jit(solution)/shard_map/ppermute | solution.py:512
  10.1 7.1 %collective-permute-start.1 = (bf16[16,6784]{1,0:T(8,128)(2,1)S(1)}, bf16[16,6784]{1,0:T(8,128)(2,1)S(1)}, u32[]{:S(2)}, u32[]{:S(2)}) collective-permute-start(bf16[16,6784]{1,0:T(8,128)(2,1)S(1)} %shard_map.160.refs_0_), channel_id=1, source_target_pairs={{4,0},{8,4},{12,8},{14,12},{10,14},{6,10},{2,6},{0,2},{5,1},{9,5},... | collective-permute-start | bytes 651272 | tf_op jit(solution)/shard_map/ppermute | solution.py:512
  17.2 6.3 %collective-permute-start.3 = (bf16[16,6784]{1,0:T(8,128)(2,1)S(1)}, bf16[16,6784]{1,0:T(8,128)(2,1)S(1)}, u32[]{:S(2)}, u32[]{:S(2)}) collective-permute-start(bf16[16,6784]{1,0:T(8,128)(2,1)S(1)} %collective-permute-done.2.refs_1_), channel_id=1, source_target_pairs={{0,4},{4,8},{8,12},{12,14},{14,10},{10,6},{6,2},{2,0},{1,5},{5,9},... | collective-permute-start | bytes 651272 | tf_op jit(solution)/shard_map/ppermute | solution.py:512
  18.8 6.3 %collective-permute-start.5 = (bf16[16,6784]{1,0:T(8,128)(2,1)S(1)}, bf16[16,6784]{1,0:T(8,128)(2,1)S(1)}, u32[]{:S(2)}, u32[]{:S(2)}) collective-permute-start(bf16[16,6784]{1,0:T(8,128)(2,1)S(1)} %collective-permute-done.1.refs_4_), channel_id=1, source_target_pairs={{4,0},{8,4},{12,8},{14,12},{10,14},{6,10},{2,6},{0,2},{5,1},{9,5},... | collective-permute-start | bytes 651272 | tf_op jit(solution)/shard_map/ppermute | solution.py:512
  19.2 6.3 %copy-start.1 = (bf16[1,6144,256]{2,1,0:T(8,128)(2,1)S(1)}, bf16[1,6144,256]{2,1,0:T(8,128)(2,1)}, u32[]{:S(2)}) copy-start(bf16[1,6144,256]{2,1,0:T(8,128)(2,1)} %param.26) | copy-start | bytes 9437188
  23.5 6.2 %collective-permute-start.4 = (bf16[16,6784]{1,0:T(8,128)(2,1)S(1)}, bf16[16,6784]{1,0:T(8,128)(2,1)S(1)}, u32[]{:S(2)}, u32[]{:S(2)}) collective-permute-start(bf16[16,6784]{1,0:T(8,128)(2,1)S(1)} %collective-permute-done.3.refs_2_), channel_id=1, source_target_pairs={{0,4},{4,8},{8,12},{12,14},{14,10},{10,6},{6,2},{2,0},{1,5},{5,9},... | collective-permute-start | bytes 651272 | tf_op jit(solution)/shard_map/ppermute | solution.py:512
  25.0 6.3 %collective-permute-start.6 = (bf16[16,6784]{1,0:T(8,128)(2,1)S(1)}, bf16[16,6784]{1,0:T(8,128)(2,1)S(1)}, u32[]{:S(2)}, u32[]{:S(2)}) collective-permute-start(bf16[16,6784]{1,0:T(8,128)(2,1)S(1)} %collective-permute-done.5.refs_5_), channel_id=1, source_target_pairs={{4,0},{8,4},{12,8},{14,12},{10,14},{6,10},{2,6},{0,2},{5,1},{9,5},... | collective-permute-start | bytes 651272 | tf_op jit(solution)/shard_map/ppermute | solution.py:512
  25.5 1.9 %copy-start.2 = (bf16[1,256,6144]{2,1,0:T(8,128)(2,1)S(1)}, bf16[1,256,6144]{2,1,0:T(8,128)(2,1)}, u32[]{:S(2)}) copy-start(bf16[1,256,6144]{2,1,0:T(8,128)(2,1)} %param.27) | copy-start | bytes 9437188
  29.7 7.4 %collective-permute-start.8 = (bf16[16,3456]{1,0:T(8,128)(2,1)S(1)}, bf16[16,3456]{1,0:T(8,128)(2,1)S(1)}, u32[]{:S(2)}, u32[]{:S(2)}) collective-permute-start(bf16[16,3456]{1,0:T(8,128)(2,1)S(1)} %slice.8), channel_id=1, source_target_pairs={{0,4},{4,8},{8,12},{12,14},{14,10},{10,6},{6,2},{2,0},{1,5},{5,9},... | collective-permute-start | bytes 331784 | tf_op jit(solution)/shard_map/ppermute | solution.py:512
  31.3 5.7 %collective-permute-start.9 = (bf16[16,3328]{1,0:T(8,128)(2,1)S(1)}, bf16[16,3328]{1,0:T(8,128)(2,1)S(1)}, u32[]{:S(2)}, u32[]{:S(2)}) collective-permute-start(bf16[16,3328]{1,0:T(8,128)(2,1)S(1)} %slice.7), channel_id=1, source_target_pairs={{4,0},{8,4},{12,8},{14,12},{10,14},{6,10},{2,6},{0,2},{5,1},{9,5},... | collective-permute-start | bytes 319496 | tf_op jit(solution)/shard_map/ppermute | solution.py:512
  34.1 5.2 %collective-permute-start.7 = (bf16[16,4608]{1,0:T(8,128)(2,1)S(1)}, bf16[16,4608]{1,0:T(8,128)(2,1)S(1)}, u32[]{:S(2)}, u32[]{:S(2)}) collective-permute-start(bf16[16,4608]{1,0:T(8,128)(2,1)S(1)} %get-tuple-element.42), channel_id=1, source_target_pairs={{0,4},{4,8},{8,12},{12,14},{14,10},{10,6},{6,2},{2,0},{1,5},{5,9},... | collective-permute-start | bytes 442376 | tf_op jit(solution)/shard_map/ppermute | solution.py:572
  35.7 5.1 %collective-permute-start.14 = (bf16[16,4608]{1,0:T(8,128)(2,1)S(1)}, bf16[16,4608]{1,0:T(8,128)(2,1)S(1)}, u32[]{:S(2)}, u32[]{:S(2)}) collective-permute-start(bf16[16,4608]{1,0:T(8,128)(2,1)S(1)} %get-tuple-element.47), channel_id=1, source_target_pairs={{4,0},{8,4},{12,8},{14,12},{10,14},{6,10},{2,6},{0,2},{5,1},{9,5},... | collective-permute-start | bytes 442376 | tf_op jit(solution)/shard_map/ppermute | solution.py:573
  38.7 19.7 %copy-start.3 = (f32[32,3072]{1,0:T(8,128)S(1)}, f32[32,3072]{1,0:T(8,128)}, u32[]{:S(2)}) copy-start(f32[32,3072]{1,0:T(8,128)} %shard_map.161.hidden) | copy-start | bytes 1179652
  38.7 19.7 %copy-start.5 = (s32[32,2]{0,1:T(2,128)S(1)}, s32[32,2]{0,1:T(2,128)}, u32[]{:S(2)}) copy-start(s32[32,2]{0,1:T(2,128)} %param.23) | copy-start | bytes 772
  38.7 19.7 %copy-start.6 = (f32[32,2]{0,1:T(2,128)S(1)}, f32[32,2]{0,1:T(2,128)}, u32[]{:S(2)}) copy-start(f32[32,2]{0,1:T(2,128)} %param.24) | copy-start | bytes 772
  39.3 7.7 %collective-permute-start.11 = (bf16[16,4608]{1,0:T(8,128)(2,1)S(1)}, bf16[16,4608]{1,0:T(8,128)(2,1)S(1)}, u32[]{:S(2)}, u32[]{:S(2)}) collective-permute-start(bf16[16,4608]{1,0:T(8,128)(2,1)S(1)} %shard_map.166), channel_id=1, source_target_pairs={{0,13},{4,15},{8,11},{12,7},{14,3},{10,1},{6,5},{2,9},{1,10},{5,6}... | collective-permute-start | bytes 442376 | tf_op jit(solution)/shard_map/ppermute | solution.py:577
  40.9 8.5 %collective-permute-start.15 = (bf16[16,4608]{1,0:T(8,128)(2,1)S(1)}, bf16[16,4608]{1,0:T(8,128)(2,1)S(1)}, u32[]{:S(2)}, u32[]{:S(2)}) collective-permute-start(bf16[16,4608]{1,0:T(8,128)(2,1)S(1)} %add_convert_fusion), channel_id=1, source_target_pairs={{4,0},{8,4},{12,8},{14,12},{10,14},{6,10},{2,6},{0,2},{5,1},{9,5},... | collective-permute-start | bytes 442376 | tf_op jit(solution)/shard_map/ppermute | solution.py:573
  41.5 8.0 %collective-permute-start.10 = (bf16[16,4608]{1,0:T(8,128)(2,1)S(1)}, bf16[16,4608]{1,0:T(8,128)(2,1)S(1)}, u32[]{:S(2)}, u32[]{:S(2)}) collective-permute-start(bf16[16,4608]{1,0:T(8,128)(2,1)S(1)} %add_convert_fusion.1), channel_id=1, source_target_pairs={{0,4},{4,8},{8,12},{12,14},{14,10},{10,6},{6,2},{2,0},{1,5},{5,9},... | collective-permute-start | bytes 442376 | tf_op jit(solution)/shard_map/ppermute | solution.py:572
  47.1 2.4 %collective-permute-start.12 = (bf16[16,4608]{1,0:T(8,128)(2,1)S(1)}, bf16[16,4608]{1,0:T(8,128)(2,1)S(1)}, u32[]{:S(2)}, u32[]{:S(2)}) collective-permute-start(bf16[16,4608]{1,0:T(8,128)(2,1)S(1)} %collective-permute-done.11), channel_id=1, source_target_pairs={{0,1},{1,0},{2,3},{3,2},{4,5},{5,4},{6,7},{7,6},{8,9},{9,8},{10,11... | collective-permute-start | bytes 442376 | tf_op jit(solution)/shard_map/ppermute | solution.py:577
  49.5 6.1 %collective-permute-start.13 = (bf16[16,4608]{1,0:T(8,128)(2,1)S(1)}, bf16[16,4608]{1,0:T(8,128)(2,1)S(1)}, u32[]{:S(2)}, u32[]{:S(2)}) collective-permute-start(bf16[16,4608]{1,0:T(8,128)(2,1)S(1)} %shard_map.167), channel_id=1, source_target_pairs={{0,4},{4,8},{8,12},{12,14},{14,10},{10,6},{6,2},{2,0},{1,5},{5,9},... | collective-permute-start | bytes 442376 | tf_op jit(solution)/shard_map/ppermute | solution.py:572
  51.3 5.6 %collective-permute-start.16 = (bf16[16,4608]{1,0:T(8,128)(2,1)S(1)}, bf16[16,4608]{1,0:T(8,128)(2,1)S(1)}, u32[]{:S(2)}, u32[]{:S(2)}) collective-permute-start(bf16[16,4608]{1,0:T(8,128)(2,1)S(1)} %shard_map.169), channel_id=1, source_target_pairs={{4,0},{8,4},{12,8},{14,12},{10,14},{6,10},{2,6},{0,2},{5,1},{9,5},... | collective-permute-start | bytes 442376 | tf_op jit(solution)/shard_map/ppermute | solution.py:573
  57.1 1.3 %collective-permute-start.17 = (bf16[8,4608]{1,0:T(8,128)(2,1)S(1)}, bf16[8,4608]{1,0:T(8,128)(2,1)S(1)}, u32[]{:S(2)}, u32[]{:S(2)}) collective-permute-start(bf16[8,4608]{1,0:T(8,128)(2,1)S(1)} %get-tuple-element.50), channel_id=1, source_target_pairs={{0,1},{1,0},{2,3},{3,2},{4,5},{5,4},{6,7},{7,6},{8,9},{9,8},{10,11... | collective-permute-start | bytes 221192 | tf_op jit(solution)/shard_map/ppermute | solution.py:601
